TPU v7x, 32 devices: a whole 2x2x4 slice. The times are simulated.
32 devices in a mesh: tm: 8 (over y, x, core), group: 4 (over z).
Axes of the slice: x: 2, y: 2, z: 4, core: 2. Of those that a mesh axis runs over, the one named last changes fastest.
Arguments:
- clips: bfloat16 [4, 64, 128, 512], P('group', 'tm'), may hold values from -6 to 6
- lengths: int32 [4, 8], P('group'), may hold values from 1 to 16, 64 in all within a row
- w_time: bfloat16 [3, 512, 512], P(None, 'tm'), may hold values from -0.15625 to 0.15625
- w_down: bfloat16 [3, 512, 512], P(None, 'tm'), may hold values from -0.15625 to 0.15625
- cotangent: bfloat16 [4, 32, 128, 512], P('group', 'tm'), may hold values from -6 to 6
Outputs:
- reduced: bfloat16 [4, 32, 128, 512], P('group', 'tm')
- grad_clips: bfloat16 [4, 64, 128, 512], P('group', 'tm')
- grad_time: float32 [3, 512, 512], P(None, 'tm')
- grad_down: float32 [3, 512, 512], P(None, 'tm')
All inputs are finite; a program needn't handle non-finite values.
Results may differ from a plain program's by a relative error of at most 0.0052.
Values may be sent and summed in bfloat16 or wider, within the bound.
No kernel may reach another device: no remote copies, remote signals or barrier semaphores. Data moves between devices by JAX's collectives and lax.ppermute only.
A program may use at most 64 MiB of HBM per device.

v0:
```python
import jax
import jax.numpy as jnp
from jax import lax
from jax.sharding import PartitionSpec as P


def shifted(block, axis, distance):
    devices = range(lax.axis_size(axis))
    route = [(i - distance, i) for i in devices if i - distance in devices]
    return lax.ppermute(block, axis, route)


def clip_start(lengths_row, frames):
    ends = jnp.cumsum(lengths_row)
    return jnp.sum(jnp.where(ends[None, :] <= frames[:, None], lengths_row[None, :], 0), axis=1)


def features(x_wide):
    scale = lax.rsqrt(jnp.mean(x_wide * x_wide, axis=-1, keepdims=True) + 1e-06)
    return jax.nn.silu(x_wide * scale)


def project(block, weight):
    shape = block.shape
    flat = jnp.dot(block.reshape(-1, shape[-1]), weight, preferred_element_type=jnp.float32)
    return flat.reshape(shape[:-1] + (weight.shape[1],))


def outer(left, right):
    width = left.shape[-1]
    return jnp.dot(
        left.reshape(-1, width).T,
        right.reshape(-1, right.shape[-1]),
        preferred_element_type=jnp.float32,
    )


def shards(clips, lengths, w_time, w_down, cotangent):
    x_bf = clips[0]
    lengths_row = lengths[0]
    cot_local = cotangent[0]
    frame_count = x_bf.shape[0]
    half_count = frame_count // 2
    position = lax.axis_index("tm")
    frames = position * frame_count + jnp.arange(frame_count, dtype=jnp.int32)
    starts = clip_start(lengths_row, frames)
    time_full = lax.all_gather(w_time, "tm", axis=1, tiled=True)
    x_wide = x_bf.astype(jnp.float32)
    h_in = features(x_wide).astype(jnp.bfloat16)
    before = shifted(h_in[frame_count - 2 :], "tm", 1)
    h_ext = jnp.concatenate([before, h_in], axis=0)
    mixed = x_wide
    time_taps = []
    for offset in range(3):
        valid = frames - offset >= starts
        tapped = jnp.where(
            valid[:, None, None],
            h_ext[2 - offset : 2 - offset + frame_count],
            jnp.zeros((), jnp.bfloat16),
        )
        time_taps.append(tapped)
        mixed = mixed + project(tapped, time_full[offset])
    hidden = mixed.astype(jnp.bfloat16)
    down_full = lax.all_gather(w_down, "tm", axis=1, tiled=True)
    out_frames = position * frame_count + 2 * jnp.arange(half_count, dtype=jnp.int32)
    out_starts = clip_start(lengths_row, out_frames)
    hidden_before = shifted(hidden[frame_count - 2 :], "tm", 1)
    hidden_ext = jnp.concatenate([hidden_before, hidden], axis=0)
    reduced = jnp.zeros((half_count,) + hidden.shape[1:], jnp.float32)
    down_taps = []
    for offset in range(3):
        valid = out_frames - offset >= out_starts
        tapped = jnp.where(
            valid[:, None, None],
            hidden_ext[2 - offset : 2 - offset + frame_count][::2],
            jnp.zeros((), jnp.bfloat16),
        )
        down_taps.append(tapped)
        reduced = reduced + project(tapped, down_full[offset])
    grad_down = jnp.stack([outer(down_taps[offset], cot_local) for offset in range(3)])
    cot_next = shifted(cot_local[:1], "tm", -1)
    cot_ext = jnp.concatenate([cot_local, cot_next], axis=0)
    ext_frames = position * frame_count + 2 * jnp.arange(half_count + 1, dtype=jnp.int32)
    ext_starts = clip_start(lengths_row, ext_frames)
    grad_hidden = jnp.zeros(x_wide.shape, jnp.float32)
    for offset in range(3):
        valid = ext_frames - offset >= ext_starts
        spread = jnp.where(
            valid[:, None, None], project(cot_ext, down_full[offset].T), jnp.zeros((), jnp.float32)
        )
        placed = jnp.stack([spread, jnp.zeros_like(spread)], axis=1).reshape(
            (frame_count + 2,) + spread.shape[1:]
        )
        grad_hidden = grad_hidden + placed[offset : offset + frame_count]
    grad_mixed = grad_hidden.astype(jnp.bfloat16)
    grad_time = jnp.stack([outer(time_taps[offset], grad_mixed) for offset in range(3)])
    grad_next = shifted(grad_mixed[:2], "tm", -1)
    grad_ext = jnp.concatenate([grad_mixed, grad_next], axis=0)
    grad_hin = jnp.zeros(x_wide.shape, jnp.float32)
    for offset in range(3):
        valid = frames >= clip_start(lengths_row, frames + offset)
        tapped = jnp.where(
            valid[:, None, None],
            grad_ext[offset : offset + frame_count],
            jnp.zeros((), jnp.bfloat16),
        )
        grad_hin = grad_hin + project(tapped, time_full[offset].T)
    _, pullback = jax.vjp(features, x_wide)
    grad_feat = pullback(grad_hin)[0]
    grad_clips = (grad_hidden + grad_feat).astype(jnp.bfloat16)
    share_time, share_down = (
        lax.psum_scatter(grad_time, "tm", scatter_dimension=1, tiled=True),
        lax.psum_scatter(grad_down, "tm", scatter_dimension=1, tiled=True),
    )
    final_time, final_down = lax.psum((share_time, share_down), "group")
    return (reduced.astype(jnp.bfloat16)[None], grad_clips[None], final_time, final_down)


def solution(mesh):
    in_specs = (
        P("group", "tm", None, None),
        P("group", None),
        P(None, "tm", None),
        P(None, "tm", None),
        P("group", "tm", None, None),
    )
    out_specs = (
        P("group", "tm", None, None),
        P("group", "tm", None, None),
        P(None, "tm", None),
        P(None, "tm", None),
    )
    return jax.shard_map(shards, mesh=mesh, in_specs=in_specs, out_specs=out_specs, check_vma=False)
```

profile of v0, /device:TPU:0, one launch (start us, length us, event | category | flops | bytes accessed | tf_op | source)
XLA Modules:
  0.0 242.9 jit_solution(9616779287174765106)
XLA Ops:
  7.9 0.9 slice_bitcast_fusion.18
  8.9 1.3 collective-permute-start.2
  10.3 0.8 reduce-window.8
  11.1 0.9 select_reduce_fusion
  12.0 0.8 select_reduce_fusion.2
  12.8 1.5 fusion.20
  14.4 23.9 %all-gather.5.cloned.1.call-done = bf16[3,512,512]{2,1,0:T(8,128)(2,1)} async-done(((bf16[3,64,512]{2,1,0:T(8,128)(2,1)}), bf16[3,512,512]{2,1,0:T(8,128)(2,1)}) %all-gather.5.cloned.1.call-update) | async-done | bytes 1572880 | tf_op jit(solution)/shard_map/all_gather | solution.py:64
  38.3 1.7 fusion.30
  40.5 0.8 copy-done.5
  44.2 0.8 fusion.85
  45.5 1.3 collective-permute-start.3
  46.8 22.0 %all-gather.3.cloned.1.call-done = bf16[3,512,512]{2,1,0:T(8,128)(2,1)} async-done(((bf16[3,64,512]{2,1,0:T(8,128)(2,1)}), bf16[3,512,512]{2,1,0:T(8,128)(2,1)}) %all-gather.3.cloned.1.call-update) | async-done | bytes 1572880 | tf_op jit(solution)/shard_map/all_gather | solution.py:47
  68.8 1.9 fusion.50
  70.7 2.1 fusion.35
  72.8 2.8 %fusion.24 = (f32[8,128]{1,0:T(8,128)S(1)}, f32[8,128,512]{2,1,0:T(8,128)S(1)}) fusion(bf16[1,8,128,512]{3,2,1,0:T(8,128)(2,1)S(1)} %copy-done.4, f32[8,128]{1,0:T(8,128)S(1)} %fusion.66, bf16[3,512,512]{2,1,0:T(8,128)(2,1)S(1)} %copy-done.13, bf16[2,128,512]{2,1,0:T(8,128)(2,1)} %collective-permute-done.3, bf16[8,128,512]{2,1,0:T(8,128)(2,1)S(1)} %copy-done.10, ...), kind=kOutput, calls=%fused_computation.32 | convolution fusion | flops 545782784 | bytes 9183744 | tf_op jit(solution)/shard_map/dot_general | solution.py:25
  75.7 2.3 fusion.40
  78.1 2.2 collective-permute-start
  80.2 0.8 convolution_bitcast_fusion.5
  81.4 0.8 convolution_bitcast_fusion.4
  82.2 0.8 convolution_bitcast_fusion.3
  83.0 1.9 pad_maximum_fusion
  86.4 1.0 fusion.43
  87.6 0.8 fusion.64
  88.4 0.9 fusion.23
  89.3 5.6 %collective-permute-start.1 = (bf16[2,128,512]{2,1,0:T(8,128)(2,1)S(1)}, bf16[2,128,512]{2,1,0:T(8,128)(2,1)S(1)}, u32[]{:S(2)}, u32[]{:S(2)}) collective-permute-start(bf16[2,128,512]{2,1,0:T(8,128)(2,1)S(1)} %slice.113), channel_id=1, source_target_pairs={{0,4},{4,8},{8,12},{12,16},{16,20},{20,24},{24,28},{1,5},{5,9},{9,... | collective-permute-start | bytes 786440 | tf_op jit(solution)/shard_map/ppermute | solution.py:10
  97.1 2.0 pad_maximum_fusion.1
  99.2 37.5 %reduce-scatter.3.cloned.1.call-done = f32[3,64,512]{2,1,0:T(8,128)} async-done(((f32[3,512,512]{2,1,0:T(8,128)}), f32[3,64,512]{2,1,0:T(8,128)}) %reduce-scatter.3.cloned.1.call-update) | async-done | bytes 393232 | tf_op jit(solution)/shard_map/reduce_scatter | solution.py:112
  136.6 49.9 %reduce-scatter.5.cloned.1.call-done = f32[3,64,512]{2,1,0:T(8,128)} async-done(((f32[3,512,512]{2,1,0:T(8,128)}), f32[3,64,512]{2,1,0:T(8,128)}) %reduce-scatter.5.cloned.1.call-update) | async-done | bytes 393232 | tf_op jit(solution)/shard_map/reduce_scatter | solution.py:113
  187.4 1.2 fusion.32
  188.6 44.2 %all-reduce.6.cloned.1.call-done = (f32[3,64,512]{2,1,0:T(8,128)}, f32[3,64,512]{2,1,0:T(8,128)}) async-done(((f32[3,64,512]{2,1,0:T(8,128)}, f32[3,64,512]{2,1,0:T(8,128)}), (f32[3,64,512]{2,1,0:T(8,128)}, f32[3,64,512]{2,1,0:T(8,128)})) %all-reduce.6.cloned.1.call-update) | async-done | bytes 786448 | tf_op jit(solution)/shard_map/psum | solution.py:115
  232.8 1.8 copy.27
  234.6 1.8 copy.28
  (76 shorter events, 9.7 us)
Async XLA Ops:
  7.2 31.2 %all-gather.5.cloned.1.call-start = ((), (), s32[]{:S(2)}) async-start(), calls=%async_computation.3 | async-start | bytes 1769472 | tf_op jit(solution)/shard_map/all_gather | solution.py:64
  7.9 60.9 %all-gather.3.cloned.1.call-start = ((), (), s32[]{:S(2)}) async-start(), calls=%async_computation.2 | async-start | bytes 1769472 | tf_op jit(solution)/shard_map/all_gather | solution.py:47
  8.9 5.5 %collective-permute-start.2 = (bf16[1,128,512]{2,1,0:T(8,128)(2,1)S(1)}, bf16[1,128,512]{2,1,0:T(8,128)(2,1)S(1)}, u32[]{:S(2)}, u32[]{:S(2)}) collective-permute-start(bf16[1,128,512]{2,1,0:T(8,128)(2,1)S(1)} %slice_bitcast_fusion.18), channel_id=1, source_target_pairs={{4,0},{8,4},{12,8},{16,12},{20,16},{24,20},{28,24},{5,1},{9,5},{13... | collective-permute-start | bytes 393224 | tf_op jit(solution)/shard_map/ppermute | solution.py:10
  10.2 126.4 %reduce-scatter.3.cloned.1.call-start = ((), (), s32[]{:S(2)}) async-start(), calls=%async_computation.4 | async-start | bytes 3538944 | tf_op jit(solution)/shard_map/reduce_scatter | solution.py:112
  40.3 1.0 copy-start.5
  40.3 1.6 copy-start.11
  42.9 1.3 copy-start
  43.8 1.7 copy-start.2
  45.5 23.3 %copy-start.9 = (bf16[8,128,512]{2,1,0:T(8,128)(2,1)}, bf16[8,128,512]{2,1,0:T(8,128)(2,1)S(1)}, u32[]{:S(2)}) copy-start(bf16[8,128,512]{2,1,0:T(8,128)(2,1)S(1)} %fusion.85) | copy-start | bytes 3145732
  45.5 25.2 %collective-permute-start.3 = (bf16[2,128,512]{2,1,0:T(8,128)(2,1)S(1)}, bf16[2,128,512]{2,1,0:T(8,128)(2,1)}, u32[]{:S(2)}, u32[]{:S(2)}) collective-permute-start(bf16[2,128,512]{2,1,0:T(8,128)(2,1)S(1)} %slice.119), channel_id=1, source_target_pairs={{4,0},{8,4},{12,8},{16,12},{20,16},{24,20},{28,24},{5,1},{9,5},{13... | collective-permute-start | bytes 786440 | tf_op jit(solution)/shard_map/ppermute | solution.py:10
  68.8 2.0 copy-start.13
  70.7 2.1 copy-start.4
  70.7 2.1 copy-start.10
  72.8 2.9 %copy-start.1 = (f32[4,2,128,512]{3,2,1,0:T(8,128)S(1)}, f32[4,2,128,512]{3,2,1,0:T(8,128)}, u32[]{:S(2)}) copy-start(f32[4,2,128,512]{3,2,1,0:T(8,128)} %copy-done) | copy-start | bytes 6291460
  72.8 2.9 %copy-start.3 = (f32[5,2,128,512]{3,2,1,0:T(8,128)S(1)}, f32[5,2,128,512]{3,2,1,0:T(8,128)}, u32[]{:S(2)}) copy-start(f32[5,2,128,512]{3,2,1,0:T(8,128)} %copy-done.2) | copy-start | bytes 7864324
  78.0 4.1 %copy-start.7 = (bf16[8,128,512]{2,1,0:T(8,128)(2,1)}, bf16[8,128,512]{2,1,0:T(8,128)(2,1)S(1)}, u32[]{:S(2)}) copy-start(bf16[8,128,512]{2,1,0:T(8,128)(2,1)S(1)} %get-tuple-element.12) | copy-start | bytes 3145732
  78.1 3.3 %collective-permute-start = (bf16[2,128,512]{2,1,0:T(8,128)(2,1)S(1)}, bf16[2,128,512]{2,1,0:T(8,128)(2,1)S(1)}, u32[]{:S(2)}, u32[]{:S(2)}) collective-permute-start(bf16[2,128,512]{2,1,0:T(8,128)(2,1)S(1)} %slice.107), channel_id=1, source_target_pairs={{0,4},{4,8},{8,12},{12,16},{16,20},{20,24},{24,28},{1,5},{5,9},{9,... | collective-permute-start | bytes 786440 | tf_op jit(solution)/shard_map/ppermute | solution.py:10
  84.9 0.7 copy-start.15
  84.9 1.4 copy-start.14
  85.0 101.5 %reduce-scatter.5.cloned.1.call-start = ((), (), s32[]{:S(2)}) async-start(), calls=%async_computation.5 | async-start | bytes 3538944 | tf_op jit(solution)/shard_map/reduce_scatter | solution.py:113
  86.4 1.2 copy-start.8
  88.3 6.6 %copy-start.6 = (bf16[1,4,128,512]{3,2,1,0:T(8,128)(2,1)S(1)}, bf16[1,4,128,512]{3,2,1,0:T(8,128)(2,1)}, u32[]{:S(2)}) copy-start(bf16[1,4,128,512]{3,2,1,0:T(8,128)(2,1)} %param.9) | copy-start | bytes 1572868
  89.3 6.5 %collective-permute-start.1 = (bf16[2,128,512]{2,1,0:T(8,128)(2,1)S(1)}, bf16[2,128,512]{2,1,0:T(8,128)(2,1)S(1)}, u32[]{:S(2)}, u32[]{:S(2)}) collective-permute-start(bf16[2,128,512]{2,1,0:T(8,128)(2,1)S(1)} %slice.113), channel_id=1, source_target_pairs={{0,4},{4,8},{8,12},{12,16},{16,20},{20,24},{24,28},{1,5},{5,9},{9,... | collective-permute-start | bytes 786440 | tf_op jit(solution)/shard_map/ppermute | solution.py:10
  99.1 87.4 %copy-start.12 = (bf16[3,512,512]{2,1,0:T(8,128)(2,1)S(1)}, bf16[3,512,512]{2,1,0:T(8,128)(2,1)}, u32[]{:S(2)}) copy-start(bf16[3,512,512]{2,1,0:T(8,128)(2,1)} %all-gather.5.cloned.1.call-done) | copy-start | bytes 4718596
  99.1 133.7 %all-reduce.6.cloned.1.call-start = ((), (), s32[]{:S(2)}) async-start(), calls=%async_computation.6 | async-start | bytes 1572864 | tf_op jit(solution)/shard_map/psum | solution.py:115
Sparse Core Ops, SparseCore 0:
  9.9 28.3 all-gather.4
  40.2 28.4 all-gather.2
  85.1 51.4 reduce-scatter.2
  140.2 46.2 reduce-scatter.4
  188.7 44.0 all-reduce.5
where the time goes:
time: 243 us
  waiting for transfers between devices  179 us (74%)
  matrix products  18.2 us (7%)
  between operations  14.2 us (6%)
  other arithmetic  11.9 us (5%)
  starting transfers between devices  10.5 us (4%)
  local copies, waits for them, and re-layouts  9.29 us (4%)
    reduce_scatter x1, waiting for transfers between devices, shards(): lax.psum_scatter(grad_down, 'tm', scatter_dimension=1, tiled=True)  49.9 us
    psum x1, waiting for transfers between devices, shards(): final_time, final_down = lax.psum((share_time, share_down), 'group')  44.2 us
    reduce_scatter x1, waiting for transfers between devices, shards(): lax.psum_scatter(grad_time, 'tm', scatter_dimension=1, tiled=True)  37.5 us
    all_gather x1, waiting for transfers between devices, shards(): down_full = lax.all_gather(w_down, 'tm', axis=1, tiled=True)  23.9 us
    all_gather x1, waiting for transfers between devices, shards(): time_full = lax.all_gather(w_time, 'tm', axis=1, tiled=True)  22 us
    dot_general x12, matrix products, project(): jnp.dot(block.reshape(-1, shape[-1]), weight, preferred_element_type=jnp....  14.3 us
    ppermute x4, starting transfers between devices, shifted(): return lax.ppermute(block, axis, route)  10.3 us
    unnamed x34, local copies, waits for them, and re-layouts  7.15 us
  transfers between devices with their start and end apart: 9, of which 7 were waited for; matrix products, arithmetic and copies ran while one was open for 9% of the time, Pallas kernels for 0%

commit v1 on v0

v1 whole, which is shorter than its diff:
```python
import functools

import jax
import jax.numpy as jnp
from jax import lax
from jax.experimental import pallas as pl
from jax.experimental.pallas import tpu as pltpu
from jax.sharding import PartitionSpec as P

EPS = 1e-06
VMEM = pl.BlockSpec(memory_space=pltpu.VMEM)
SMEM = pl.BlockSpec(memory_space=pltpu.SMEM)
F32 = jnp.float32
BF16 = jnp.bfloat16


def xor_step(value, axis, distance):
    count = lax.axis_size(axis)
    return lax.ppermute(value, axis, [(i, i ^ distance) for i in range(count)])


def shifted(block, axis, distance):
    devices = range(lax.axis_size(axis))
    route = [(i - distance, i) for i in devices if i - distance in devices]
    return lax.ppermute(block, axis, route)


def dot(left, right):
    return jnp.dot(left, right, preferred_element_type=F32)


def dot_t(left, right):
    return lax.dot_general(left, right, (((1,), (1,)), ((), ())), preferred_element_type=F32)


def kept(flag, block):
    return jnp.where(flag > 0, block, jnp.zeros((), block.dtype))


def live(meta, tap, frame, frames):
    return meta[1 + (tap - 1) * (frames + 3) + frame]


def block_index(meta, apart, other):
    me = meta[0]
    chip, core = me // 2, me % 2
    side = (1 - core) if other else core
    return (chip ^ apart) * 2 + side


def assemble(meta, own, other, full):
    chips, taps, rows, _ = own.shape
    for apart in range(chips):
        for side, source in ((False, own), (True, other)):
            at = pl.multiple_of(block_index(meta, apart, side) * rows, rows)
            for tap in range(taps):
                full[tap, pl.ds(at, rows), :] = source[apart, tap]


def place_rows(meta, chips, rows, values, target, columns):
    for apart in range(chips):
        for side in (False, True):
            at = pl.multiple_of(block_index(meta, apart, side) * rows, rows)
            to = (apart + (chips if side else 0)) * rows
            target[to:to + rows, columns] = values[pl.ds(at, rows), :]


def features_kernel(meta, clips, h_out, ht_out, flip, *, chips, rows):
    x = clips[0].astype(F32)
    scale = lax.rsqrt(jnp.mean(x * x, axis=-1, keepdims=True) + EPS)
    v = x * scale
    h = (v * jax.nn.sigmoid(v)).astype(BF16)
    h_out[0] = h
    flip[...] = h.T
    place_rows(meta, chips, rows, flip, ht_out, slice(None))


def split_rows(value, keep, send, tap):
    chips, _, rows, _ = keep.shape
    for apart in range(chips):
        keep[apart, tap] = value[apart * rows:(apart + 1) * rows]
        to = (chips + apart) * rows
        send[apart, tap] = value[to:to + rows].astype(BF16)


def backward_kernel(meta, cot, cot_next, own, other, ht, gh, gm, keep, send, w, c0, c1, c2, m1, m2):
    half, cells, _ = cot.shape
    frames = 2 * half
    assemble(meta, own, other, w)

    def cot_at(j):
        return cot[j] if j < half else cot_next[j - half]

    for m in range(half + 1):
        here = slice(m * cells, (m + 1) * cells)
        c0[here] = cot_at(m)
        ahead = cot_at(m + 1)
        c1[here] = kept(live(meta, 1, 2 * m + 2, frames), ahead)
        c2[here] = kept(live(meta, 2, 2 * m + 2, frames), ahead)
    odd = dot_t(c1[...], w[1])
    for m in range(half + 1):
        here = odd[m * cells:(m + 1) * cells]
        gm[2 * m + 1] = here.astype(BF16)
        if m < half:
            gh[2 * m + 1] = here
    even = dot_t(c0[...], w[0]) + dot_t(c2[...], w[2])
    for m in range(half + 1):
        here = even[m * cells:(m + 1) * cells]
        gm[2 * m] = here.astype(BF16)
        if m < half:
            gh[2 * m] = here
    for g in range(frames):
        here = slice(g * cells, (g + 1) * cells)
        m1[here] = kept(live(meta, 1, g + 1, frames), gm[g + 1])
        m2[here] = kept(live(meta, 2, g + 2, frames), gm[g + 2])
    flat = gm[0:frames].reshape(frames * cells, gm.shape[-1])
    split_rows(dot(ht[...], flat), keep, send, 0)
    split_rows(dot(ht[...], m1[...]), keep, send, 1)
    split_rows(dot(ht[...], m2[...]), keep, send, 2)


def forward_kernel(meta, clips, h_before, h, cot, cot_next, own, other, hidden, keep, send, w, t1, t2, flip, even_t, odd_t, c1, c2):
    frames, cells, width = clips.shape
    half = frames // 2
    chips, _, rows, _ = own.shape
    assemble(meta, own, other, w)

    def h_at(f):
        return h[f] if f >= 0 else h_before[f + 2]

    def cot_at(j):
        return cot[j] if j < half else cot_next[j - half]

    for f in range(frames):
        here = slice(f * cells, (f + 1) * cells)
        t1[here] = kept(live(meta, 1, f, frames), h_at(f - 1))
        t2[here] = kept(live(meta, 2, f, frames), h_at(f - 2))
    for j in range(half):
        here = slice(j * cells, (j + 1) * cells)
        c1[here] = kept(live(meta, 1, 2 * j + 2, frames), cot_at(j + 1))
        c2[here] = kept(live(meta, 2, 2 * j + 2, frames), cot_at(j + 1))
    flat = h[...].reshape(frames * cells, width)
    mixed = dot(flat, w[0]) + dot(t1[...], w[1]) + dot(t2[...], w[2])
    for f in range(frames):
        value = (clips[f].astype(F32) + mixed[f * cells:(f + 1) * cells]).astype(BF16)
        hidden[f] = value
        flip[...] = value.T
        columns = slice(f // 2 * cells, (f // 2 + 1) * cells)
        place_rows(meta, chips, rows, flip, odd_t if f % 2 else even_t, columns)
    flat_cot = cot[...].reshape(half * cells, width)
    split_rows(dot(even_t[...], flat_cot), keep, send, 0)
    split_rows(dot(odd_t[...], c1[...]), keep, send, 1)
    split_rows(dot(even_t[...], c2[...]), keep, send, 2)


def reduced_kernel(meta, before, hidden, own, other, reduced, w, t0, t1, t2):
    frames, cells, width = hidden.shape
    half = frames // 2
    assemble(meta, own, other, w)
    for j in range(half):
        here = slice(j * cells, (j + 1) * cells)
        t0[here] = hidden[2 * j]
        t1[here] = kept(live(meta, 1, 2 * j, frames), hidden[2 * j - 1] if j else before[1])
        t2[here] = kept(live(meta, 2, 2 * j, frames), hidden[2 * j - 2] if j else before[0])
    out = dot(t0[...], w[0]) + dot(t1[...], w[1]) + dot(t2[...], w[2])
    for j in range(half):
        reduced[j] = out[j * cells:(j + 1) * cells].astype(BF16)


def clips_kernel(meta, clips, gh, gm, own, other, out, w, m1, m2):
    frames, cells, width = clips.shape
    assemble(meta, own, other, w)
    for g in range(frames):
        here = slice(g * cells, (g + 1) * cells)
        m1[here] = kept(live(meta, 1, g + 1, frames), gm[g + 1])
        m2[here] = kept(live(meta, 2, g + 2, frames), gm[g + 2])
    flat = gm[0:frames].reshape(frames * cells, width)
    grad = dot_t(flat, w[0]) + dot_t(m1[...], w[1]) + dot_t(m2[...], w[2])
    for f in range(frames):
        g = grad[f * cells:(f + 1) * cells]
        x = clips[f].astype(F32)
        scale = lax.rsqrt(jnp.mean(x * x, axis=-1, keepdims=True) + EPS)
        v = x * scale
        gate = jax.nn.sigmoid(v)
        gv = g * (gate + v * gate * (1.0 - gate))
        along = jnp.mean(gv * x, axis=-1, keepdims=True)
        out[f] = (gh[f] + scale * gv - (scale * scale * scale) * along * x).astype(BF16)


def shards(clips, lengths, w_time, w_down, cotangent):
    x = clips[0]
    cot = cotangent[0]
    frames, cells, width = x.shape
    half = frames // 2
    devices = lax.axis_size("tm")
    chips = devices // 2
    taps, rows, _ = w_time.shape
    me = lax.axis_index("tm")
    params = pltpu.CompilerParams(vmem_limit_bytes=48 * 1024 * 1024)

    def sds(shape, dtype):
        return jax.ShapeDtypeStruct(shape, dtype)

    def scratch(shape, dtype=BF16):
        return pltpu.VMEM(shape, dtype)

    ends = jnp.cumsum(lengths[0])
    local = me * frames + jnp.arange(-2, frames + 3, dtype=jnp.int32)
    clip = jnp.sum((ends[None, :] <= local[:, None]).astype(jnp.int32), axis=1)
    clip = jnp.where(local < 0, -1, clip)
    live_1 = (clip[2:] == clip[1:-1]).astype(jnp.int32)
    live_2 = (clip[2:] == clip[:-2]).astype(jnp.int32)
    meta = jnp.concatenate([me[None].astype(jnp.int32), live_1, live_2])

    def gathered(weight):
        own = jnp.stack([weight] + [xor_step(weight, "tm", 2 * d) for d in range(1, chips)])
        return own, xor_step(own, "tm", 1)

    cot_next = shifted(cot[:2], "tm", -1)
    down_own, down_other = gathered(w_down)

    h, ht = pl.pallas_call(
        functools.partial(features_kernel, chips=chips, rows=rows),
        grid=(frames,),
        in_specs=[SMEM, pl.BlockSpec((1, cells, width), lambda f: (f, 0, 0))],
        out_specs=(
            pl.BlockSpec((1, cells, width), lambda f: (f, 0, 0)),
            pl.BlockSpec((width, cells), lambda f: (0, f)),
        ),
        out_shape=(sds((frames, cells, width), BF16), sds((width, frames * cells), BF16)),
        scratch_shapes=[scratch((width, cells))],
        name="features",
    )(meta, x)
    h_before = shifted(h[frames - 2:], "tm", 1)

    weight_scratch = scratch((taps, width, width))
    wide = sds((chips, taps, rows, width), F32)
    narrow = sds((chips, taps, rows, width), BF16)
    lot = frames * cells
    gh, gm, time_keep, time_send = pl.pallas_call(
        backward_kernel,
        in_specs=[SMEM] + [VMEM] * 5,
        out_specs=(VMEM,) * 4,
        out_shape=(sds((frames, cells, width), F32), sds((frames + 2, cells, width), BF16), wide, narrow),
        scratch_shapes=[weight_scratch] + [scratch(((half + 1) * cells, width))] * 3 + [scratch((lot, width))] * 2,
        compiler_params=params,
        name="backward",
    )(meta, cot, cot_next, down_own, down_other, ht)

    time_own, time_other = gathered(w_time)
    hidden, down_keep, down_send = pl.pallas_call(
        forward_kernel,
        in_specs=[SMEM] + [VMEM] * 7,
        out_specs=(VMEM,) * 3,
        out_shape=(sds((frames, cells, width), BF16), wide, narrow),
        scratch_shapes=[weight_scratch] + [scratch((lot, width))] * 2
        + [scratch((width, cells))] + [scratch((width, half * cells))] * 2 + [scratch((half * cells, width))] * 2,
        compiler_params=params,
        name="forward",
    )(meta, x, h_before, h, cot, cot_next, time_own, time_other)

    def summed(keep, send):
        part = keep + xor_step(send, "tm", 1).astype(F32)
        total = part[0]
        for d in range(1, chips):
            total = total + xor_step(part[d].astype(BF16), "tm", 2 * d).astype(F32)
        step = 1
        while step < lax.axis_size("group"):
            mine = total.astype(BF16)
            total = mine.astype(F32) + xor_step(mine, "group", step).astype(F32)
            step *= 2
        return total

    grad_time = summed(time_keep, time_send)
    grad_down = summed(down_keep, down_send)

    grad_clips = pl.pallas_call(
        clips_kernel,
        in_specs=[SMEM] + [VMEM] * 5,
        out_specs=VMEM,
        out_shape=sds((frames, cells, width), BF16),
        scratch_shapes=[weight_scratch] + [scratch((lot, width))] * 2,
        compiler_params=params,
        name="clips",
    )(meta, x, gh, gm, time_own, time_other)

    before = shifted(hidden[frames - 2:], "tm", 1)
    reduced = pl.pallas_call(
        reduced_kernel,
        in_specs=[SMEM] + [VMEM] * 4,
        out_specs=VMEM,
        out_shape=sds((half, cells, width), BF16),
        scratch_shapes=[weight_scratch] + [scratch((half * cells, width))] * 3,
        compiler_params=params,
        name="reduced",
    )(meta, before, hidden, down_own, down_other)
    return reduced[None], grad_clips[None], grad_time, grad_down


def solution(mesh):
    in_specs = (
        P("group", "tm", None, None),
        P("group", None),
        P(None, "tm", None),
        P(None, "tm", None),
        P("group", "tm", None, None),
    )
    out_specs = (
        P("group", "tm", None, None),
        P("group", "tm", None, None),
        P(None, "tm", None),
        P(None, "tm", None),
    )
    return jax.shard_map(shards, mesh=mesh, in_specs=in_specs, out_specs=out_specs, check_vma=False)
```

time: 243 us -> 100 us (0.41)
  waiting for transfers between devices: 179 us -> 30.4 us
  starting transfers between devices: 10.5 us -> 34.6 us
  Pallas kernels: 0 us -> 23.3 us
  matrix products: 18.2 us -> 0 us
  between operations: 14.2 us -> 0.82 us
  other arithmetic: 11.9 us -> 6.49 us
  local copies, waits for them, and re-layouts: 9.29 us -> 4.35 us
    reduce_scatter x2 -> x0, waiting for transfers between devices: 87.3 us -> none  [the longest x1 49.9 us: shards(): lax.psum_scatter(grad_down, 'tm', scatter_dimension=1, tiled=True)]
    all_gather x2 -> x0, waiting for transfers between devices: 45.9 us -> none  [the longest x1 23.9 us: shards(): down_full = lax.all_gather(w_down, 'tm', axis=1, tiled=True)]
    psum x1 -> x0, waiting for transfers between devices: 44.2 us -> none  [shards(): final_time, final_down = lax.psum((share_time, share_down), 'group')]
    ppermute x0 -> x20, waiting for transfers between devices: none -> 30.4 us  [xor_step(): return lax.ppermute(value, axis, [(i, i ^ distance) for i in range(count)])]
    ppermute x0 -> x20, starting transfers between devices: none -> 29.5 us  [xor_step(): return lax.ppermute(value, axis, [(i, i ^ distance) for i in range(count)])]
    pallas_call x0 -> x5, Pallas kernels: none -> 23.3 us  [the longest x1 6.08 us: shards(): pl.pallas_call(functools.partial(features_kernel, chips=chips, rows=rows)...]
    dot_general x18 -> x0, matrix products: 18.2 us -> none  [the longest x12 14.3 us: project(): jnp.dot(block.reshape(-1, shape[-1]), weight, preferred_element_type=jnp....]
    unnamed x34 -> x14, local copies, waits for them, and re-layouts: 7.15 us -> 1.61 us
  transfers between devices with their start and end apart: 9 -> 23, of which waited for: 7 -> 11; matrix products, arithmetic and copies ran while one was open for 9% -> 8% of each run, Pallas kernels for 0% -> 23%
where the time goes in v1:
time: 100 us
  starting transfers between devices  34.6 us (35%)
  waiting for transfers between devices  30.4 us (30%)
  Pallas kernels  23.3 us (23%)
  other arithmetic  6.49 us (6%)
  local copies, waits for them, and re-layouts  4.35 us (4%)
    ppermute x20, waiting for transfers between devices, xor_step(): return lax.ppermute(value, axis, [(i, i ^ distance) for i in range(count)])  30.4 us
    ppermute x20, starting transfers between devices, xor_step(): return lax.ppermute(value, axis, [(i, i ^ distance) for i in range(count)])  29.5 us
    pallas_call x1, Pallas kernels, shards(): pl.pallas_call(functools.partial(features_kernel, chips=chips, rows=rows)...  6.08 us
    pallas_call x1, Pallas kernels, shards(): pl.pallas_call(forward_kernel, in_specs=[SMEM] + [VMEM] * 7, out_specs=(V...  5.39 us
    ppermute x3, starting transfers between devices, shifted(): return lax.ppermute(block, axis, route)  5.14 us
    pallas_call x1, Pallas kernels, shards(): pl.pallas_call(backward_kernel, in_specs=[SMEM] + [VMEM] * 5, out_specs=(...  5.12 us
    pallas_call x1, Pallas kernels, shards(): pl.pallas_call(clips_kernel, in_specs=[SMEM] + [VMEM] * 5, out_specs=VMEM...  4.31 us
    pallas_call x1, Pallas kernels, shards(): pl.pallas_call(reduced_kernel, in_specs=[SMEM] + [VMEM] * 4, out_specs=VM...  2.43 us
  transfers between devices with their start and end apart: 23, of which 11 were waited for; matrix products, arithmetic and copies ran while one was open for 8% of the time, Pallas kernels for 23%

profile of v1, /device:TPU:0, one launch (start us, length us, event | category | flops | bytes accessed | tf_op | source)
XLA Modules:
  0.0 100.0 jit_solution(9389103118366327389)
XLA Ops:
  0.6 3.0 %collective-permute-start.2 = (bf16[3,64,512]{2,1,0:T(8,128)(2,1)}, bf16[3,64,512]{2,1,0:T(8,128)(2,1)S(1)}, u32[]{:S(2)}, u32[]{:S(2)}) collective-permute-start(bf16[3,64,512]{2,1,0:T(8,128)(2,1)} %param.7), channel_id=1, source_target_pairs={{0,8},{4,12},{8,0},{12,4},{16,24},{20,28},{24,16},{28,20},{1,9},{5... | collective-permute-start | bytes 589832 | tf_op jit(solution)/shard_map/ppermute | solution.py:19
  3.6 1.5 %collective-permute-start.4 = (bf16[3,64,512]{2,1,0:T(8,128)(2,1)}, bf16[3,64,512]{2,1,0:T(8,128)(2,1)S(1)}, u32[]{:S(2)}, u32[]{:S(2)}) collective-permute-start(bf16[3,64,512]{2,1,0:T(8,128)(2,1)} %param.7), channel_id=1, source_target_pairs={{0,24},{4,28},{8,16},{12,20},{16,8},{20,12},{24,0},{28,4},{1,25},{... | collective-permute-start | bytes 589832 | tf_op jit(solution)/shard_map/ppermute | solution.py:19
  5.2 1.9 %collective-permute-start.7 = (bf16[3,64,512]{2,1,0:T(8,128)(2,1)}, bf16[3,64,512]{2,1,0:T(8,128)(2,1)}, u32[]{:S(2)}, u32[]{:S(2)}) collective-permute-start(bf16[3,64,512]{2,1,0:T(8,128)(2,1)} %param.8), channel_id=1, source_target_pairs={{0,8},{4,12},{8,0},{12,4},{16,24},{20,28},{24,16},{28,20},{1,9},{5... | collective-permute-start | bytes 589832 | tf_op jit(solution)/shard_map/ppermute | solution.py:19
  7.1 1.5 %collective-permute-start.9 = (bf16[3,64,512]{2,1,0:T(8,128)(2,1)}, bf16[3,64,512]{2,1,0:T(8,128)(2,1)}, u32[]{:S(2)}, u32[]{:S(2)}) collective-permute-start(bf16[3,64,512]{2,1,0:T(8,128)(2,1)} %param.8), channel_id=1, source_target_pairs={{0,24},{4,28},{8,16},{12,20},{16,8},{20,12},{24,0},{28,4},{1,25},{... | collective-permute-start | bytes 589832 | tf_op jit(solution)/shard_map/ppermute | solution.py:19
  9.5 1.7 %slice_bitcast_fusion.2 = bf16[2,128,512]{2,1,0:T(8,128)(2,1)} fusion(bf16[1,4,128,512]{3,2,1,0:T(8,128)(2,1)} %param.9), kind=kLoop, calls=%fused_computation.18 | loop fusion | bytes 524288 | tf_op jit(solution)/shard_map/slice | solution.py:219
  11.7 3.7 %collective-permute-done.4 = bf16[3,64,512]{2,1,0:T(8,128)(2,1)S(1)} collective-permute-done((bf16[3,64,512]{2,1,0:T(8,128)(2,1)}, bf16[3,64,512]{2,1,0:T(8,128)(2,1)S(1)}, u32[]{:S(2)}, u32[]{:S(2)}) %collective-permute-start.4) | collective-permute-done | bytes 196640 | tf_op jit(solution)/shard_map/ppermute | solution.py:19
  15.4 1.3 %collective-permute-start.1 = (bf16[2,128,512]{2,1,0:T(8,128)(2,1)}, bf16[2,128,512]{2,1,0:T(8,128)(2,1)S(1)}, u32[]{:S(2)}, u32[]{:S(2)}) collective-permute-start(bf16[2,128,512]{2,1,0:T(8,128)(2,1)} %slice_bitcast_fusion.2), channel_id=1, source_target_pairs={{4,0},{8,4},{12,8},{16,12},{20,16},{24,20},{28,24},{5,1},{9,5},{13... | collective-permute-start | bytes 786440 | tf_op jit(solution)/shard_map/ppermute | solution.py:25
  19.6 6.1 %features.1 = (bf16[8,128,512]{2,1,0:T(8,128)(2,1)}, bf16[512,1024]{1,0:T(8,128)(2,1)}) custom-call(s32[23]{0:T(128)} %pad_add_fusion.meta, bf16[8,128,512]{2,1,0:T(8,128)(2,1)} %bitcast.49), custom_call_target="tpu_custom_call" | custom-call | tf_op jit(solution)/shard_map/features/pallas_call | solution.py:222
  26.6 1.9 %collective-permute-start = (bf16[2,128,512]{2,1,0:T(8,128)(2,1)S(1)}, bf16[2,128,512]{2,1,0:T(8,128)(2,1)S(1)}, u32[]{:S(2)}, u32[]{:S(2)}) collective-permute-start(bf16[2,128,512]{2,1,0:T(8,128)(2,1)S(1)} %slice.55), channel_id=1, source_target_pairs={{0,4},{4,8},{8,12},{12,16},{16,20},{20,24},{24,28},{1,5},{5,9},{9,... | collective-permute-start | bytes 786440 | tf_op jit(solution)/shard_map/ppermute | solution.py:25
  28.6 1.3 %pad_maximum_fusion.1.own = bf16[4,3,64,512]{3,2,1,0:T(8,128)(2,1)S(1)} fusion(bf16[1,3,64,512]{3,2,1,0:T(8,128)(2,1)} %bitcast.13, bf16[1,3,64,512]{3,2,1,0:T(8,128)(2,1)} %bitcast.12, bf16[1,3,64,512]{3,2,1,0:T(8,128)(2,1)} %bitcast.11, bf16[1,3,64,512]{3,2,1,0:T(8,128)(2,1)} %bitcast.57), kind=kLoop, calls=%fused_computation.3 | loop fusion | flops 1179648 | bytes 1572864 | tf_op jit(solution)/shard_map/stack | solution.py:216
  29.9 1.6 %collective-permute-start.10 = (bf16[4,3,64,512]{3,2,1,0:T(8,128)(2,1)S(1)}, bf16[4,3,64,512]{3,2,1,0:T(8,128)(2,1)S(1)}, u32[]{:S(2)}, u32[]{:S(2)}) collective-permute-start(bf16[4,3,64,512]{3,2,1,0:T(8,128)(2,1)S(1)} %pad_maximum_fusion.1.own), channel_id=1, source_target_pairs={{0,4},{4,0},{8,12},{12,8},{16,20},{20,16},{24,28},{28,24},{1,5},{5... | collective-permute-start | bytes 2359304 | tf_op jit(solution)/shard_map/ppermute | solution.py:19
  31.6 5.4 %forward.1 = (bf16[8,128,512]{2,1,0:T(8,128)(2,1)S(1)}, f32[4,3,64,512]{3,2,1,0:T(8,128)}, bf16[4,3,64,512]{3,2,1,0:T(8,128)(2,1)S(1)}) custom-call(s32[23]{0:T(128)S(1)} %copy-done.4, bf16[8,128,512]{2,1,0:T(8,128)(2,1)S(1)} %bitcast.50, bf16[2,128,512]{2,1,0:T(8,128)(2,1)S(1)} %collective-permute-done.h_before, bf16[8,128,512]{2,1,0:T(8,128)(2,1)} %get-tuple-element.13.h, ...), custom_call_target="tpu_custom_call" | custom-call | tf_op jit(solution)/shard_map/forward/pallas_call | solution.py:251
  37.0 1.8 %collective-permute-start.17 = (bf16[4,3,64,512]{3,2,1,0:T(8,128)(2,1)S(1)}, bf16[4,3,64,512]{3,2,1,0:T(8,128)(2,1)S(1)}, u32[]{:S(2)}, u32[]{:S(2)}) collective-permute-start(bf16[4,3,64,512]{3,2,1,0:T(8,128)(2,1)S(1)} %get-tuple-element.21), channel_id=1, source_target_pairs={{0,4},{4,0},{8,12},{12,8},{16,20},{20,16},{24,28},{28,24},{1,5},{5... | collective-permute-start | bytes 2359304 | tf_op jit(solution)/shard_map/ppermute | solution.py:19
  38.9 1.9 %collective-permute-start.6 = (bf16[2,128,512]{2,1,0:T(8,128)(2,1)S(1)}, bf16[2,128,512]{2,1,0:T(8,128)(2,1)S(1)}, u32[]{:S(2)}, u32[]{:S(2)}) collective-permute-start(bf16[2,128,512]{2,1,0:T(8,128)(2,1)S(1)} %slice.58), channel_id=1, source_target_pairs={{0,4},{4,8},{8,12},{12,16},{16,20},{20,24},{24,28},{1,5},{5,9},{9,... | collective-permute-start | bytes 786440 | tf_op jit(solution)/shard_map/ppermute | solution.py:25
  40.8 5.1 %backward.1 = (f32[8,128,512]{2,1,0:T(8,128)}, bf16[10,128,512]{2,1,0:T(8,128)(2,1)S(1)}, f32[4,3,64,512]{3,2,1,0:T(8,128)}, bf16[4,3,64,512]{3,2,1,0:T(8,128)(2,1)S(1)}) custom-call(s32[23]{0:T(128)S(1)} %copy-done.4, bf16[4,128,512]{2,1,0:T(8,128)(2,1)S(1)} %bitcast.53, bf16[2,128,512]{2,1,0:T(8,128)(2,1)S(1)} %collective-permute-done.1.cot_next, ...), custom_call_target="tpu_custom_call" | custom-call | tf_op jit(solution)/shard_map/backward/pallas_call | solution.py:240
  45.9 2.5 %collective-permute-start.11 = (bf16[4,3,64,512]{3,2,1,0:T(8,128)(2,1)S(1)}, bf16[4,3,64,512]{3,2,1,0:T(8,128)(2,1)S(1)}, u32[]{:S(2)}, u32[]{:S(2)}) collective-permute-start(bf16[4,3,64,512]{3,2,1,0:T(8,128)(2,1)S(1)} %get-tuple-element.19), channel_id=1, source_target_pairs={{0,4},{4,0},{8,12},{12,8},{16,20},{20,16},{24,28},{28,24},{1,5},{5... | collective-permute-start | bytes 2359304 | tf_op jit(solution)/shard_map/ppermute | solution.py:19
  48.4 1.6 %copy-done.2 = f32[8,128,512]{2,1,0:T(8,128)S(1)} copy-done((f32[8,128,512]{2,1,0:T(8,128)S(1)}, f32[8,128,512]{2,1,0:T(8,128)}, u32[]{:S(2)}) %copy-start.2) | copy-done | bytes 2097176
  50.0 4.3 %clips.1 = bf16[8,128,512]{2,1,0:T(8,128)(2,1)} custom-call(s32[23]{0:T(128)S(1)} %copy-done.4, bf16[8,128,512]{2,1,0:T(8,128)(2,1)S(1)} %bitcast.51, f32[8,128,512]{2,1,0:T(8,128)S(1)} %copy-done.2, bf16[10,128,512]{2,1,0:T(8,128)(2,1)S(1)} %get-tuple-element.17.gm, bf16[4,3,64,512]{3,2,1,0:T(8,128)(2,1)S(1)} %pad_maximum_fusion.own, ...), custom_call_target="tpu_custom_call" | custom-call | tf_op jit(solution)/shard_map/clips/pallas_call | solution.py:277
  54.3 2.4 %reduced.1 = bf16[4,128,512]{2,1,0:T(8,128)(2,1)} custom-call(s32[23]{0:T(128)S(1)} %copy-done.4, bf16[2,128,512]{2,1,0:T(8,128)(2,1)S(1)} %collective-permute-done.6.before, bf16[8,128,512]{2,1,0:T(8,128)(2,1)S(1)} %get-tuple-element.14.hidden, bf16[4,3,64,512]{3,2,1,0:T(8,128)(2,1)S(1)} %pad_maximum_fusion.1.own, ...), custom_call_target="tpu_custom_call" | custom-call | tf_op jit(solution)/shard_map/reduced/pallas_call | solution.py:288
  59.2 1.5 %collective-permute-start.19 = (bf16[3,64,512]{2,1,0:T(8,128)(2,1)S(1)}, bf16[3,64,512]{2,1,0:T(8,128)(2,1)S(1)}, u32[]{:S(2)}, u32[]{:S(2)}) collective-permute-start(bf16[3,64,512]{2,1,0:T(8,128)(2,1)S(1)} %get-tuple-element.28), channel_id=1, source_target_pairs={{0,16},{4,20},{8,24},{12,28},{16,0},{20,4},{24,8},{28,12},{1,17},{... | collective-permute-start | bytes 589832 | tf_op jit(solution)/shard_map/ppermute | solution.py:19
  63.2 1.8 %collective-permute-done.18 = bf16[3,64,512]{2,1,0:T(8,128)(2,1)S(1)} collective-permute-done((bf16[3,64,512]{2,1,0:T(8,128)(2,1)S(1)}, bf16[3,64,512]{2,1,0:T(8,128)(2,1)S(1)}, u32[]{:S(2)}, u32[]{:S(2)}) %collective-permute-start.18) | collective-permute-done | bytes 196640 | tf_op jit(solution)/shard_map/ppermute | solution.py:19
  65.5 3.7 %collective-permute-done.20 = bf16[3,64,512]{2,1,0:T(8,128)(2,1)S(1)} collective-permute-done((bf16[3,64,512]{2,1,0:T(8,128)(2,1)S(1)}, bf16[3,64,512]{2,1,0:T(8,128)(2,1)S(1)}, u32[]{:S(2)}, u32[]{:S(2)}) %collective-permute-start.20) | collective-permute-done | bytes 196640 | tf_op jit(solution)/shard_map/ppermute | solution.py:19
  69.2 1.8 %collective-permute-done.19 = bf16[3,64,512]{2,1,0:T(8,128)(2,1)S(1)} collective-permute-done((bf16[3,64,512]{2,1,0:T(8,128)(2,1)S(1)}, bf16[3,64,512]{2,1,0:T(8,128)(2,1)S(1)}, u32[]{:S(2)}, u32[]{:S(2)}) %collective-permute-start.19) | collective-permute-done | bytes 196640 | tf_op jit(solution)/shard_map/ppermute | solution.py:19
  71.1 1.9 %collective-permute-start.21 = (bf16[3,64,512]{2,1,0:T(8,128)(2,1)S(1)}, bf16[3,64,512]{2,1,0:T(8,128)(2,1)S(1)}, u32[]{:S(2)}, u32[]{:S(2)}) collective-permute-start(bf16[3,64,512]{2,1,0:T(8,128)(2,1)S(1)} %fusion.3), channel_id=1, source_target_pairs={{0,1},{1,0},{2,3},{3,2},{4,5},{5,4},{6,7},{7,6},{8,9},{9,8},{10,11... | collective-permute-start | bytes 589832 | tf_op jit(solution)/shard_map/ppermute | solution.py:19
  73.4 3.3 %collective-permute-done.14 = bf16[3,64,512]{2,1,0:T(8,128)(2,1)S(1)} collective-permute-done((bf16[3,64,512]{2,1,0:T(8,128)(2,1)S(1)}, bf16[3,64,512]{2,1,0:T(8,128)(2,1)S(1)}, u32[]{:S(2)}, u32[]{:S(2)}) %collective-permute-start.14) | collective-permute-done | bytes 196640 | tf_op jit(solution)/shard_map/ppermute | solution.py:19
  76.8 1.3 %collective-permute-done.13 = bf16[3,64,512]{2,1,0:T(8,128)(2,1)S(1)} collective-permute-done((bf16[3,64,512]{2,1,0:T(8,128)(2,1)S(1)}, bf16[3,64,512]{2,1,0:T(8,128)(2,1)S(1)}, u32[]{:S(2)}, u32[]{:S(2)}) %collective-permute-start.13) | collective-permute-done | bytes 196640 | tf_op jit(solution)/shard_map/ppermute | solution.py:19
  78.2 1.9 %collective-permute-start.15 = (bf16[3,64,512]{2,1,0:T(8,128)(2,1)S(1)}, bf16[3,64,512]{2,1,0:T(8,128)(2,1)S(1)}, u32[]{:S(2)}, u32[]{:S(2)}) collective-permute-start(bf16[3,64,512]{2,1,0:T(8,128)(2,1)S(1)} %fusion.7), channel_id=1, source_target_pairs={{0,1},{1,0},{2,3},{3,2},{4,5},{5,4},{6,7},{7,6},{8,9},{9,8},{10,11... | collective-permute-start | bytes 589832 | tf_op jit(solution)/shard_map/ppermute | solution.py:19
  80.2 2.7 %collective-permute-start.22 = (bf16[3,64,512]{2,1,0:T(8,128)(2,1)S(1)}, bf16[3,64,512]{2,1,0:T(8,128)(2,1)S(1)}, u32[]{:S(2)}, u32[]{:S(2)}) collective-permute-start(bf16[3,64,512]{2,1,0:T(8,128)(2,1)S(1)} %add_convert_fusion), channel_id=1, source_target_pairs={{0,2},{1,3},{2,0},{3,1},{4,6},{5,7},{6,4},{7,5},{8,10},{9,11},{10,... | collective-permute-start | bytes 589832 | tf_op jit(solution)/shard_map/ppermute | solution.py:19
  82.8 4.6 %collective-permute-done.15 = bf16[3,64,512]{2,1,0:T(8,128)(2,1)S(1)} collective-permute-done((bf16[3,64,512]{2,1,0:T(8,128)(2,1)S(1)}, bf16[3,64,512]{2,1,0:T(8,128)(2,1)S(1)}, u32[]{:S(2)}, u32[]{:S(2)}) %collective-permute-start.15) | collective-permute-done | bytes 196640 | tf_op jit(solution)/shard_map/ppermute | solution.py:19
  87.5 1.5 %collective-permute-start.16 = (bf16[3,64,512]{2,1,0:T(8,128)(2,1)S(1)}, bf16[3,64,512]{2,1,0:T(8,128)(2,1)S(1)}, u32[]{:S(2)}, u32[]{:S(2)}) collective-permute-start(bf16[3,64,512]{2,1,0:T(8,128)(2,1)S(1)} %add_convert_fusion.1), channel_id=1, source_target_pairs={{0,2},{1,3},{2,0},{3,1},{4,6},{5,7},{6,4},{7,5},{8,10},{9,11},{10,... | collective-permute-start | bytes 589832 | tf_op jit(solution)/shard_map/ppermute | solution.py:19
  89.0 6.5 %collective-permute-done.22 = bf16[3,64,512]{2,1,0:T(8,128)(2,1)S(1)} collective-permute-done((bf16[3,64,512]{2,1,0:T(8,128)(2,1)S(1)}, bf16[3,64,512]{2,1,0:T(8,128)(2,1)S(1)}, u32[]{:S(2)}, u32[]{:S(2)}) %collective-permute-start.22) | collective-permute-done | bytes 196640 | tf_op jit(solution)/shard_map/ppermute | solution.py:19
  96.4 2.8 %collective-permute-done.16 = bf16[3,64,512]{2,1,0:T(8,128)(2,1)S(1)} collective-permute-done((bf16[3,64,512]{2,1,0:T(8,128)(2,1)S(1)}, bf16[3,64,512]{2,1,0:T(8,128)(2,1)S(1)}, u32[]{:S(2)}, u32[]{:S(2)}) %collective-permute-start.16) | collective-permute-done | bytes 196640 | tf_op jit(solution)/shard_map/ppermute | solution.py:19
  (54 shorter events, 13.1 us)
Async XLA Ops:
  0.6 10.6 %collective-permute-start.2 = (bf16[3,64,512]{2,1,0:T(8,128)(2,1)}, bf16[3,64,512]{2,1,0:T(8,128)(2,1)S(1)}, u32[]{:S(2)}, u32[]{:S(2)}) collective-permute-start(bf16[3,64,512]{2,1,0:T(8,128)(2,1)} %param.7), channel_id=1, source_target_pairs={{0,8},{4,12},{8,0},{12,4},{16,24},{20,28},{24,16},{28,20},{1,9},{5... | collective-permute-start | bytes 589832 | tf_op jit(solution)/shard_map/ppermute | solution.py:19
  3.6 11.7 %collective-permute-start.4 = (bf16[3,64,512]{2,1,0:T(8,128)(2,1)}, bf16[3,64,512]{2,1,0:T(8,128)(2,1)S(1)}, u32[]{:S(2)}, u32[]{:S(2)}) collective-permute-start(bf16[3,64,512]{2,1,0:T(8,128)(2,1)} %param.7), channel_id=1, source_target_pairs={{0,24},{4,28},{8,16},{12,20},{16,8},{20,12},{24,0},{28,4},{1,25},{... | collective-permute-start | bytes 589832 | tf_op jit(solution)/shard_map/ppermute | solution.py:19
  5.1 11.8 %collective-permute-start.3 = (bf16[3,64,512]{2,1,0:T(8,128)(2,1)}, bf16[3,64,512]{2,1,0:T(8,128)(2,1)S(1)}, u32[]{:S(2)}, u32[]{:S(2)}) collective-permute-start(bf16[3,64,512]{2,1,0:T(8,128)(2,1)} %param.7), channel_id=1, source_target_pairs={{0,16},{4,20},{8,24},{12,28},{16,0},{20,4},{24,8},{28,12},{1,17},{... | collective-permute-start | bytes 589832 | tf_op jit(solution)/shard_map/ppermute | solution.py:19
  5.2 21.4 %collective-permute-start.7 = (bf16[3,64,512]{2,1,0:T(8,128)(2,1)}, bf16[3,64,512]{2,1,0:T(8,128)(2,1)}, u32[]{:S(2)}, u32[]{:S(2)}) collective-permute-start(bf16[3,64,512]{2,1,0:T(8,128)(2,1)} %param.8), channel_id=1, source_target_pairs={{0,8},{4,12},{8,0},{12,4},{16,24},{20,28},{24,16},{28,20},{1,9},{5... | collective-permute-start | bytes 589832 | tf_op jit(solution)/shard_map/ppermute | solution.py:19
  7.1 21.4 %collective-permute-start.9 = (bf16[3,64,512]{2,1,0:T(8,128)(2,1)}, bf16[3,64,512]{2,1,0:T(8,128)(2,1)}, u32[]{:S(2)}, u32[]{:S(2)}) collective-permute-start(bf16[3,64,512]{2,1,0:T(8,128)(2,1)} %param.8), channel_id=1, source_target_pairs={{0,24},{4,28},{8,16},{12,20},{16,8},{20,12},{24,0},{28,4},{1,25},{... | collective-permute-start | bytes 589832 | tf_op jit(solution)/shard_map/ppermute | solution.py:19
  11.2 17.4 %collective-permute-start.8 = (bf16[3,64,512]{2,1,0:T(8,128)(2,1)}, bf16[3,64,512]{2,1,0:T(8,128)(2,1)}, u32[]{:S(2)}, u32[]{:S(2)}) collective-permute-start(bf16[3,64,512]{2,1,0:T(8,128)(2,1)} %param.8), channel_id=1, source_target_pairs={{0,16},{4,20},{8,24},{12,28},{16,0},{20,4},{24,8},{28,12},{1,17},{... | collective-permute-start | bytes 589832 | tf_op jit(solution)/shard_map/ppermute | solution.py:19
  15.4 16.2 %collective-permute-start.1 = (bf16[2,128,512]{2,1,0:T(8,128)(2,1)}, bf16[2,128,512]{2,1,0:T(8,128)(2,1)S(1)}, u32[]{:S(2)}, u32[]{:S(2)}) collective-permute-start(bf16[2,128,512]{2,1,0:T(8,128)(2,1)} %slice_bitcast_fusion.2), channel_id=1, source_target_pairs={{4,0},{8,4},{12,8},{16,12},{20,16},{24,20},{28,24},{5,1},{9,5},{13... | collective-permute-start | bytes 786440 | tf_op jit(solution)/shard_map/ppermute | solution.py:25
  18.0 13.6 %collective-permute-start.5 = (bf16[4,3,64,512]{3,2,1,0:T(8,128)(2,1)S(1)}, bf16[4,3,64,512]{3,2,1,0:T(8,128)(2,1)S(1)}, u32[]{:S(2)}, u32[]{:S(2)}) collective-permute-start(bf16[4,3,64,512]{3,2,1,0:T(8,128)(2,1)S(1)} %pad_maximum_fusion.own), channel_id=1, source_target_pairs={{0,4},{4,0},{8,12},{12,8},{16,20},{20,16},{24,28},{28,24},{1,5},{5... | collective-permute-start | bytes 2359304 | tf_op jit(solution)/shard_map/ppermute | solution.py:19
  19.6 12.0 %copy-start = (bf16[1,8,128,512]{3,2,1,0:T(8,128)(2,1)S(1)}, bf16[1,8,128,512]{3,2,1,0:T(8,128)(2,1)}, u32[]{:S(2)}) copy-start(bf16[1,8,128,512]{3,2,1,0:T(8,128)(2,1)} %param.5) | copy-start | bytes 3145732
  19.6 12.0 %copy-start.1 = (bf16[1,4,128,512]{3,2,1,0:T(8,128)(2,1)S(1)}, bf16[1,4,128,512]{3,2,1,0:T(8,128)(2,1)}, u32[]{:S(2)}) copy-start(bf16[1,4,128,512]{3,2,1,0:T(8,128)(2,1)} %param.9) | copy-start | bytes 1572868
  19.6 12.0 %copy-start.4 = (s32[23]{0:T(128)S(1)}, s32[23]{0:T(128)}, u32[]{:S(2)}) copy-start(s32[23]{0:T(128)} %pad_add_fusion.meta) | copy-start | bytes 280
  26.6 4.9 %collective-permute-start = (bf16[2,128,512]{2,1,0:T(8,128)(2,1)S(1)}, bf16[2,128,512]{2,1,0:T(8,128)(2,1)S(1)}, u32[]{:S(2)}, u32[]{:S(2)}) collective-permute-start(bf16[2,128,512]{2,1,0:T(8,128)(2,1)S(1)} %slice.55), channel_id=1, source_target_pairs={{0,4},{4,8},{8,12},{12,16},{16,20},{20,24},{24,28},{1,5},{5,9},{9,... | collective-permute-start | bytes 786440 | tf_op jit(solution)/shard_map/ppermute | solution.py:25
  29.9 10.9 %collective-permute-start.10 = (bf16[4,3,64,512]{3,2,1,0:T(8,128)(2,1)S(1)}, bf16[4,3,64,512]{3,2,1,0:T(8,128)(2,1)S(1)}, u32[]{:S(2)}, u32[]{:S(2)}) collective-permute-start(bf16[4,3,64,512]{3,2,1,0:T(8,128)(2,1)S(1)} %pad_maximum_fusion.1.own), channel_id=1, source_target_pairs={{0,4},{4,0},{8,12},{12,8},{16,20},{20,16},{24,28},{28,24},{1,5},{5... | collective-permute-start | bytes 2359304 | tf_op jit(solution)/shard_map/ppermute | solution.py:19
  31.6 9.2 %copy-start.3 = (bf16[512,1024]{1,0:T(8,128)(2,1)S(1)}, bf16[512,1024]{1,0:T(8,128)(2,1)}, u32[]{:S(2)}) copy-start(bf16[512,1024]{1,0:T(8,128)(2,1)} %get-tuple-element.15.ht) | copy-start | bytes 3145732
  37.0 19.8 %collective-permute-start.17 = (bf16[4,3,64,512]{3,2,1,0:T(8,128)(2,1)S(1)}, bf16[4,3,64,512]{3,2,1,0:T(8,128)(2,1)S(1)}, u32[]{:S(2)}, u32[]{:S(2)}) collective-permute-start(bf16[4,3,64,512]{3,2,1,0:T(8,128)(2,1)S(1)} %get-tuple-element.21), channel_id=1, source_target_pairs={{0,4},{4,0},{8,12},{12,8},{16,20},{20,16},{24,28},{28,24},{1,5},{5... | collective-permute-start | bytes 2359304 | tf_op jit(solution)/shard_map/ppermute | solution.py:19
  38.9 15.5 %collective-permute-start.6 = (bf16[2,128,512]{2,1,0:T(8,128)(2,1)S(1)}, bf16[2,128,512]{2,1,0:T(8,128)(2,1)S(1)}, u32[]{:S(2)}, u32[]{:S(2)}) collective-permute-start(bf16[2,128,512]{2,1,0:T(8,128)(2,1)S(1)} %slice.58), channel_id=1, source_target_pairs={{0,4},{4,8},{8,12},{12,16},{16,20},{20,24},{24,28},{1,5},{5,9},{9,... | collective-permute-start | bytes 786440 | tf_op jit(solution)/shard_map/ppermute | solution.py:25
  45.9 14.8 %collective-permute-start.11 = (bf16[4,3,64,512]{3,2,1,0:T(8,128)(2,1)S(1)}, bf16[4,3,64,512]{3,2,1,0:T(8,128)(2,1)S(1)}, u32[]{:S(2)}, u32[]{:S(2)}) collective-permute-start(bf16[4,3,64,512]{3,2,1,0:T(8,128)(2,1)S(1)} %get-tuple-element.19), channel_id=1, source_target_pairs={{0,4},{4,0},{8,12},{12,8},{16,20},{20,16},{24,28},{28,24},{1,5},{5... | collective-permute-start | bytes 2359304 | tf_op jit(solution)/shard_map/ppermute | solution.py:19
  48.4 1.6 %copy-start.2 = (f32[8,128,512]{2,1,0:T(8,128)S(1)}, f32[8,128,512]{2,1,0:T(8,128)}, u32[]{:S(2)}) copy-start(f32[8,128,512]{2,1,0:T(8,128)} %get-tuple-element.16.gh) | copy-start | bytes 6291460
  54.3 2.4 %copy-start.6 = (f32[4,3,64,512]{3,2,1,0:T(8,128)S(1)}, f32[4,3,64,512]{3,2,1,0:T(8,128)}, u32[]{:S(2)}) copy-start(f32[4,3,64,512]{3,2,1,0:T(8,128)} %get-tuple-element.20) | copy-start | bytes 4718596
  56.8 3.9 %copy-start.5 = (f32[4,3,64,512]{3,2,1,0:T(8,128)S(1)}, f32[4,3,64,512]{3,2,1,0:T(8,128)}, u32[]{:S(2)}) copy-start(f32[4,3,64,512]{3,2,1,0:T(8,128)} %get-tuple-element.18) | copy-start | bytes 4718596
  57.1 7.8 %collective-permute-start.18 = (bf16[3,64,512]{2,1,0:T(8,128)(2,1)S(1)}, bf16[3,64,512]{2,1,0:T(8,128)(2,1)S(1)}, u32[]{:S(2)}, u32[]{:S(2)}) collective-permute-start(bf16[3,64,512]{2,1,0:T(8,128)(2,1)S(1)} %get-tuple-element.26), channel_id=1, source_target_pairs={{0,8},{4,12},{8,0},{12,4},{16,24},{20,28},{24,16},{28,20},{1,9},{5... | collective-permute-start | bytes 589832 | tf_op jit(solution)/shard_map/ppermute | solution.py:19
  58.0 11.2 %collective-permute-start.20 = (bf16[3,64,512]{2,1,0:T(8,128)(2,1)S(1)}, bf16[3,64,512]{2,1,0:T(8,128)(2,1)S(1)}, u32[]{:S(2)}, u32[]{:S(2)}) collective-permute-start(bf16[3,64,512]{2,1,0:T(8,128)(2,1)S(1)} %get-tuple-element.27), channel_id=1, source_target_pairs={{0,24},{4,28},{8,16},{12,20},{16,8},{20,12},{24,0},{28,4},{1,25},{... | collective-permute-start | bytes 589832 | tf_op jit(solution)/shard_map/ppermute | solution.py:19
  59.2 11.8 %collective-permute-start.19 = (bf16[3,64,512]{2,1,0:T(8,128)(2,1)S(1)}, bf16[3,64,512]{2,1,0:T(8,128)(2,1)S(1)}, u32[]{:S(2)}, u32[]{:S(2)}) collective-permute-start(bf16[3,64,512]{2,1,0:T(8,128)(2,1)S(1)} %get-tuple-element.28), channel_id=1, source_target_pairs={{0,16},{4,20},{8,24},{12,28},{16,0},{20,4},{24,8},{28,12},{1,17},{... | collective-permute-start | bytes 589832 | tf_op jit(solution)/shard_map/ppermute | solution.py:19
  61.1 12.4 %collective-permute-start.12 = (bf16[3,64,512]{2,1,0:T(8,128)(2,1)S(1)}, bf16[3,64,512]{2,1,0:T(8,128)(2,1)S(1)}, u32[]{:S(2)}, u32[]{:S(2)}) collective-permute-start(bf16[3,64,512]{2,1,0:T(8,128)(2,1)S(1)} %get-tuple-element.29), channel_id=1, source_target_pairs={{0,8},{4,12},{8,0},{12,4},{16,24},{20,28},{24,16},{28,20},{1,9},{5... | collective-permute-start | bytes 589832 | tf_op jit(solution)/shard_map/ppermute | solution.py:19
  62.0 14.8 %collective-permute-start.14 = (bf16[3,64,512]{2,1,0:T(8,128)(2,1)S(1)}, bf16[3,64,512]{2,1,0:T(8,128)(2,1)S(1)}, u32[]{:S(2)}, u32[]{:S(2)}) collective-permute-start(bf16[3,64,512]{2,1,0:T(8,128)(2,1)S(1)} %get-tuple-element.30), channel_id=1, source_target_pairs={{0,24},{4,28},{8,16},{12,20},{16,8},{20,12},{24,0},{28,4},{1,25},{... | collective-permute-start | bytes 589832 | tf_op jit(solution)/shard_map/ppermute | solution.py:19
  65.0 13.1 %collective-permute-start.13 = (bf16[3,64,512]{2,1,0:T(8,128)(2,1)S(1)}, bf16[3,64,512]{2,1,0:T(8,128)(2,1)S(1)}, u32[]{:S(2)}, u32[]{:S(2)}) collective-permute-start(bf16[3,64,512]{2,1,0:T(8,128)(2,1)S(1)} %get-tuple-element.31), channel_id=1, source_target_pairs={{0,16},{4,20},{8,24},{12,28},{16,0},{20,4},{24,8},{28,12},{1,17},{... | collective-permute-start | bytes 589832 | tf_op jit(solution)/shard_map/ppermute | solution.py:19
  71.1 9.1 %collective-permute-start.21 = (bf16[3,64,512]{2,1,0:T(8,128)(2,1)S(1)}, bf16[3,64,512]{2,1,0:T(8,128)(2,1)S(1)}, u32[]{:S(2)}, u32[]{:S(2)}) collective-permute-start(bf16[3,64,512]{2,1,0:T(8,128)(2,1)S(1)} %fusion.3), channel_id=1, source_target_pairs={{0,1},{1,0},{2,3},{3,2},{4,5},{5,4},{6,7},{7,6},{8,9},{9,8},{10,11... | collective-permute-start | bytes 589832 | tf_op jit(solution)/shard_map/ppermute | solution.py:19
  78.2 9.2 %collective-permute-start.15 = (bf16[3,64,512]{2,1,0:T(8,128)(2,1)S(1)}, bf16[3,64,512]{2,1,0:T(8,128)(2,1)S(1)}, u32[]{:S(2)}, u32[]{:S(2)}) collective-permute-start(bf16[3,64,512]{2,1,0:T(8,128)(2,1)S(1)} %fusion.7), channel_id=1, source_target_pairs={{0,1},{1,0},{2,3},{3,2},{4,5},{5,4},{6,7},{7,6},{8,9},{9,8},{10,11... | collective-permute-start | bytes 589832 | tf_op jit(solution)/shard_map/ppermute | solution.py:19
  80.2 15.4 %collective-permute-start.22 = (bf16[3,64,512]{2,1,0:T(8,128)(2,1)S(1)}, bf16[3,64,512]{2,1,0:T(8,128)(2,1)S(1)}, u32[]{:S(2)}, u32[]{:S(2)}) collective-permute-start(bf16[3,64,512]{2,1,0:T(8,128)(2,1)S(1)} %add_convert_fusion), channel_id=1, source_target_pairs={{0,2},{1,3},{2,0},{3,1},{4,6},{5,7},{6,4},{7,5},{8,10},{9,11},{10,... | collective-permute-start | bytes 589832 | tf_op jit(solution)/shard_map/ppermute | solution.py:19
  87.5 11.7 %collective-permute-start.16 = (bf16[3,64,512]{2,1,0:T(8,128)(2,1)S(1)}, bf16[3,64,512]{2,1,0:T(8,128)(2,1)S(1)}, u32[]{:S(2)}, u32[]{:S(2)}) collective-permute-start(bf16[3,64,512]{2,1,0:T(8,128)(2,1)S(1)} %add_convert_fusion.1), channel_id=1, source_target_pairs={{0,2},{1,3},{2,0},{3,1},{4,6},{5,7},{6,4},{7,5},{8,10},{9,11},{10,... | collective-permute-start | bytes 589832 | tf_op jit(solution)/shard_map/ppermute | solution.py:19

commit v2 on v1

v2 whole, which is shorter than its diff:
```python
import functools

import jax
import jax.numpy as jnp
from jax import lax
from jax.experimental import pallas as pl
from jax.experimental.pallas import tpu as pltpu
from jax.sharding import PartitionSpec as P

EPS = 1e-06
DOWN, TIME = 0, 1
FEATURES_COST = 20_000_000_000
VMEM = pl.BlockSpec(memory_space=pltpu.VMEM)
SMEM = pl.BlockSpec(memory_space=pltpu.SMEM)
F32 = jnp.float32
BF16 = jnp.bfloat16


def bits_of(count):
    bits = []
    while 1 << len(bits) < count:
        bits.append(1 << len(bits))
    return bits


def exchange(value, step, name):
    bits = bits_of(lax.axis_size("tm"))[1:]
    turn = [bits[step], bits[(step + 1) % len(bits)]]
    with jax.named_scope(f"{name}_tm_{step}"):
        route = [(i, i ^ turn[i % 2]) for i in range(lax.axis_size("tm"))]
        return lax.ppermute(value, "tm", route)


def core_swap(value, name):
    with jax.named_scope(f"{name}_tm_core"):
        return lax.ppermute(value, "tm", [(i, i ^ 1) for i in range(lax.axis_size("tm"))])


def group_exchange(value, step, name):
    groups = lax.axis_size("group")
    bits = bits_of(groups)
    turn = [bits[step], bits[(step + len(bits) // 2) % len(bits)]]
    route = [
        (t * groups + g, t * groups + (g ^ turn[t % 2]))
        for t in range(lax.axis_size("tm"))
        for g in range(groups)
    ]
    with jax.named_scope(f"{name}_group_{step}"):
        return lax.ppermute(value, ("tm", "group"), route)


def shifted(block, axis, distance):
    devices = range(lax.axis_size(axis))
    route = [(i - distance, i) for i in devices if i - distance in devices]
    with jax.named_scope(f"halo_{axis}{distance}_{block.shape[0]}"):
        return lax.ppermute(block, axis, route)


def after(value, *earlier):
    return lax.optimization_barrier((value,) + earlier)[0]


def dot(left, right):
    return jnp.dot(left, right, preferred_element_type=F32)


def dot_t(left, right):
    return lax.dot_general(left, right, (((1,), (1,)), ((), ())), preferred_element_type=F32)


def kept(flag, block):
    return jnp.where(flag > 0, block, jnp.zeros((), block.dtype))


def live(meta, tap, frame, frames):
    return meta[1 + (tap - 1) * (frames + 3) + frame]


def chip_bit(step, count, core):
    return jnp.where(core == 0, 1 << step, 1 << ((step + 1) % count))


def apart(position, chips, core, last_first):
    count = len(bits_of(chips))
    total = 0
    for step in range(count):
        place = count - 1 - step if last_first else step
        if position >> place & 1:
            total = total ^ chip_bit(step, count, core)
    return total


def block_at(meta, position, chips, rows, other, last_first):
    chip, core = meta[0] // 2, meta[0] % 2
    core = 1 - core if other else core
    block = (chip ^ apart(position, chips, core, last_first)) * 2 + core
    return pl.multiple_of(block * rows, rows)


def assemble(meta, refs, which, full):
    early = next(i for i, ref in enumerate(refs) if len(ref.shape) == 4)
    pieces = list(refs[:early]) + [refs[early].at[which * early + i] for i in range(early)]
    for ref in refs[early + 1:]:
        pieces += [ref.at[i] for i in range(early)] if len(ref.shape) == 4 else [ref]
    taps, rows, _ = pieces[0].shape
    chips = len(pieces) // 2
    for index, source in enumerate(pieces):
        at = block_at(meta, index % chips, chips, rows, index >= chips, False)
        for tap in range(taps):
            full[tap, pl.ds(at, rows), :] = source[tap]


def place_rows(meta, chips, rows, values, target, columns):
    for index in range(2 * chips):
        at = block_at(meta, index % chips, chips, rows, index >= chips, True)
        target[index * rows:(index + 1) * rows, columns] = values[pl.ds(at, rows), :]


def split_rows(value, shares, tap):
    half, _, rows, _ = shares[0].shape
    for index in range(4 * half):
        part = value[index * rows:(index + 1) * rows]
        if index < 2 * half:
            shares[index // half][index % half, tap] = part
        elif len(shares) == 3:
            shares[2][index - 2 * half, tap] = part.astype(BF16)
        else:
            shares[2 + index - 2 * half][tap] = part.astype(BF16)


def features(x):
    x = x.astype(F32)
    scale = lax.rsqrt(jnp.mean(x * x, axis=-1, keepdims=True) + EPS)
    v = x * scale
    return (v * jax.nn.sigmoid(v)).astype(BF16)


def features_kernel(meta, clips, h_out, ht_out, flip, *, chips, rows):
    h = features(clips[0])
    h_out[0] = h
    flip[...] = h.T
    place_rows(meta, chips, rows, flip, ht_out, slice(None))


def backward_kernel(meta, cot, cot_next, ht, *refs):
    *pieces, gh, gm, low, high, send, w, c0, c1, c2, m1, m2 = refs
    shares = (low, high, send)
    half, cells, _ = cot.shape
    frames = 2 * half
    assemble(meta, pieces, DOWN, w)

    def cot_at(j):
        return cot[j] if j < half else cot_next[j - half]

    for m in range(half + 1):
        here = slice(m * cells, (m + 1) * cells)
        c0[here] = cot_at(m)
        ahead = cot_at(m + 1)
        c1[here] = kept(live(meta, 1, 2 * m + 2, frames), ahead)
        c2[here] = kept(live(meta, 2, 2 * m + 2, frames), ahead)
    odd = dot_t(c1[...], w[1])
    for m in range(half + 1):
        here = odd[m * cells:(m + 1) * cells]
        gm[2 * m + 1] = here.astype(BF16)
        if m < half:
            gh[2 * m + 1] = here
    even = dot_t(c0[...], w[0]) + dot_t(c2[...], w[2])
    for m in range(half + 1):
        here = even[m * cells:(m + 1) * cells]
        gm[2 * m] = here.astype(BF16)
        if m < half:
            gh[2 * m] = here
    for g in range(frames):
        here = slice(g * cells, (g + 1) * cells)
        m1[here] = kept(live(meta, 1, g + 1, frames), gm[g + 1])
        m2[here] = kept(live(meta, 2, g + 2, frames), gm[g + 2])
    flat = gm[0:frames].reshape(frames * cells, gm.shape[-1])
    split_rows(dot(ht[...], flat), shares, 0)
    split_rows(dot(ht[...], m1[...]), shares, 1)
    split_rows(dot(ht[...], m2[...]), shares, 2)


def forward_kernel(meta, clips, before, h, cot, cot_next, *refs, chips):
    w, t1, t2, flip, even_t, odd_t, c1, c2 = refs[-8:]
    *pieces, hidden, tail = refs[:-10 - chips]
    shares = refs[-10 - chips:-8]
    frames, cells, width = clips.shape
    half = frames // 2
    rows = shares[0].shape[2]
    assemble(meta, pieces, TIME, w)

    h_before = [features(before[0]), features(before[1])]

    def h_at(f):
        return h[f] if f >= 0 else h_before[f + 2]

    def cot_at(j):
        return cot[j] if j < half else cot_next[j - half]

    for f in range(frames):
        here = slice(f * cells, (f + 1) * cells)
        t1[here] = kept(live(meta, 1, f, frames), h_at(f - 1))
        t2[here] = kept(live(meta, 2, f, frames), h_at(f - 2))
    for j in range(half):
        here = slice(j * cells, (j + 1) * cells)
        c1[here] = kept(live(meta, 1, 2 * j + 2, frames), cot_at(j + 1))
        c2[here] = kept(live(meta, 2, 2 * j + 2, frames), cot_at(j + 1))
    flat = h[...].reshape(frames * cells, width)
    mixed = dot(flat, w[0]) + dot(t1[...], w[1]) + dot(t2[...], w[2])
    for f in range(frames):
        value = (clips[f].astype(F32) + mixed[f * cells:(f + 1) * cells]).astype(BF16)
        hidden[f] = value
        if f >= frames - 2:
            tail[f - frames + 2] = value
        flip[...] = value.T
        columns = slice(f // 2 * cells, (f // 2 + 1) * cells)
        place_rows(meta, chips, rows, flip, odd_t if f % 2 else even_t, columns)
    flat_cot = cot[...].reshape(half * cells, width)
    split_rows(dot(even_t[...], flat_cot), shares, 0)
    split_rows(dot(odd_t[...], c1[...]), shares, 1)
    split_rows(dot(even_t[...], c2[...]), shares, 2)


def reduced_kernel(meta, before, hidden, *refs):
    *pieces, reduced, w, t0, t1, t2 = refs
    frames, cells, width = hidden.shape
    half = frames // 2
    assemble(meta, pieces, DOWN, w)
    for j in range(half):
        here = slice(j * cells, (j + 1) * cells)
        t0[here] = hidden[2 * j]
        t1[here] = kept(live(meta, 1, 2 * j, frames), hidden[2 * j - 1] if j else before[1])
        t2[here] = kept(live(meta, 2, 2 * j, frames), hidden[2 * j - 2] if j else before[0])
    out = dot(t0[...], w[0]) + dot(t1[...], w[1]) + dot(t2[...], w[2])
    for j in range(half):
        reduced[j] = out[j * cells:(j + 1) * cells].astype(BF16)


def clips_kernel(meta, clips, gh, gm, *refs):
    *pieces, out, w, m1, m2 = refs
    frames, cells, width = clips.shape
    assemble(meta, pieces, TIME, w)
    for g in range(frames):
        here = slice(g * cells, (g + 1) * cells)
        m1[here] = kept(live(meta, 1, g + 1, frames), gm[g + 1])
        m2[here] = kept(live(meta, 2, g + 2, frames), gm[g + 2])
    flat = gm[0:frames].reshape(frames * cells, width)
    grad = dot_t(flat, w[0]) + dot_t(m1[...], w[1]) + dot_t(m2[...], w[2])
    for f in range(frames):
        g = grad[f * cells:(f + 1) * cells]
        x = clips[f].astype(F32)
        scale = lax.rsqrt(jnp.mean(x * x, axis=-1, keepdims=True) + EPS)
        v = x * scale
        gate = jax.nn.sigmoid(v)
        gv = g * (gate + v * gate * (1.0 - gate))
        along = jnp.mean(gv * x, axis=-1, keepdims=True)
        out[f] = (gh[f] + scale * gv - (scale * scale * scale) * along * x).astype(BF16)


def shards(clips, lengths, w_time, w_down, cotangent):
    x = clips[0]
    cot = cotangent[0]
    frames, cells, width = x.shape
    half = frames // 2
    devices = lax.axis_size("tm")
    chips = devices // 2
    early = chips // 2
    last = len(bits_of(chips)) - 1
    taps, rows, _ = w_time.shape
    me = lax.axis_index("tm")
    lot = frames * cells

    def sds(shape, dtype=BF16):
        return jax.ShapeDtypeStruct(shape, dtype)

    def scratch(*shape):
        return pltpu.VMEM(shape, BF16)

    def call(kernel, name, inputs, outs, scratches):
        tree = (VMEM,) * len(outs) if isinstance(outs, tuple) else VMEM
        return pl.pallas_call(
            kernel,
            in_specs=[SMEM] + [VMEM] * (len(inputs) - 1),
            out_specs=tree,
            out_shape=outs,
            scratch_shapes=scratches,
            compiler_params=pltpu.CompilerParams(vmem_limit_bytes=36 * 1024 * 1024),
            cost_estimate=pl.CostEstimate(flops=1_000_000, bytes_accessed=1000, transcendentals=0),
            name=name,
        )(*inputs)

    ends = jnp.cumsum(lengths[0])
    local = me * frames + jnp.arange(-2, frames + 3, dtype=jnp.int32)
    clip = jnp.sum((ends[None, :] <= local[:, None]).astype(jnp.int32), axis=1)
    clip = jnp.where(local < 0, -1, clip)
    live_1 = (clip[2:] == clip[1:-1]).astype(jnp.int32)
    live_2 = (clip[2:] == clip[:-2]).astype(jnp.int32)
    meta = jnp.concatenate([me[None].astype(jnp.int32), live_1, live_2])

    down, time = [w_down], [w_time]
    for step in range(last):
        earlier = down[1:] + time[1:]
        down = down + [exchange(after(part, *earlier), step, "down") for part in down]
        time = time + [exchange(after(part, *earlier), step, "time") for part in time]
    first = down[1:] + time[1:]
    late = jnp.stack(down + time)
    cot_next = shifted(after(cot[:2], late), "tm", -1)
    x_before = shifted(after(x[frames - 2:], late), "tm", 1)
    late = exchange(late, last, "late")
    down_other = [core_swap(part, "down") for part in down]
    time_other = [core_swap(part, "time") for part in time]

    h, ht = pl.pallas_call(
        functools.partial(features_kernel, chips=chips, rows=rows),
        grid=(frames,),
        in_specs=[SMEM, pl.BlockSpec((1, cells, width), lambda f: (f, 0, 0))],
        out_specs=(
            pl.BlockSpec((1, cells, width), lambda f: (f, 0, 0)),
            pl.BlockSpec((width, cells), lambda f: (0, f)),
        ),
        out_shape=(sds((frames, cells, width)), sds((width, lot))),
        scratch_shapes=[scratch(width, cells)],
        compiler_params=pltpu.CompilerParams(vmem_limit_bytes=36 * 1024 * 1024),
        cost_estimate=pl.CostEstimate(flops=FEATURES_COST, bytes_accessed=1000, transcendentals=0),
        name="features",
    )(after(meta, *first, *down_other, *time_other), x)

    late = after(late, h)
    down = down + [late] + down_other + [core_swap(late[i], "down") for i in range(early)]
    time_late = core_swap(late[early:], "time")

    shares = (
        sds((early, taps, rows, width), F32),
        sds((early, taps, rows, width), F32),
        sds((chips, taps, rows, width)),
    )
    full = scratch(taps, width, width)
    gh, gm, *time_shares = call(
        backward_kernel,
        "backward",
        [after(meta, x_before), cot, cot_next, ht] + down,
        (sds((frames, cells, width), F32), sds((frames + 2, cells, width))) + shares,
        [full] + [scratch((half + 1) * cells, width)] * 3 + [scratch(lot, width)] * 2,
    )

    def core_sum(shares, name, *earlier):
        low, high, *send = shares
        if len(send) == 1:
            other = after(core_swap(send[0], name), *earlier)
        else:
            other = jnp.stack([after(core_swap(part, name), *earlier) for part in send])
        other = other.astype(F32)
        return low + other[:early], (high + other[early:]).astype(BF16)

    def plane_step(low, other):
        total = low + other.astype(F32)
        count = total.shape[0] // 2
        return total[:count], total[count:].astype(BF16)

    def group_sum(mine, step, name):
        return mine.astype(F32) + group_exchange(mine, step, name).astype(F32)

    time = time + [late] + time_other + [time_late]
    low_time, high_time = core_sum(time_shares, "grad_time")
    hidden, tail, *down_shares = call(
        functools.partial(forward_kernel, chips=chips),
        "forward",
        [after(meta, high_time), x, x_before, h, cot, cot_next] + time,
        (sds((frames, cells, width)), sds((2, cells, width))) + shares[:2]
        + (sds((taps, rows, width)),) * chips,
        [full] + [scratch(lot, width)] * 2 + [scratch(width, cells)]
        + [scratch(width, half * cells)] * 2 + [scratch(half * cells, width)] * 2,
    )

    for step in range(last):
        other = after(exchange(high_time, step, "grad_time"), hidden)
        low_time, high_time = plane_step(low_time, other)
        if step == 0:
            low_down, high_down = core_sum(down_shares, "grad_down", high_time)
            grad_clips = call(
                clips_kernel,
                "clips",
                [after(meta, high_down), x, gh, gm] + time,
                sds((frames, cells, width)),
                [full] + [scratch(lot, width)] * 2,
            )
        other = after(exchange(high_down, step, "grad_down"), grad_clips)
        low_down, high_down = plane_step(low_down, other)

    other = after(exchange(high_time, last, "grad_time"), high_down)
    mine_time = (low_time[0] + other[0].astype(F32)).astype(BF16)
    before = shifted(after(tail, mine_time), "tm", 1)
    other = after(exchange(high_down, last, "grad_down"), mine_time)
    mine_down = (low_down[0] + other[0].astype(F32)).astype(BF16)
    reduced = call(
        reduced_kernel,
        "reduced",
        [after(meta, mine_down), before, hidden] + down,
        sds((half, cells, width)),
        [full] + [scratch(half * cells, width)] * 3,
    )
    steps = len(bits_of(lax.axis_size("group")))
    for step in range(steps):
        grad_time = mine_time.astype(F32) + after(group_exchange(mine_time, step, "grad_time"), reduced).astype(F32)
        if step < steps - 1:
            mine_time = grad_time.astype(BF16)
        grad_down = mine_down.astype(F32) + after(group_exchange(mine_down, step, "grad_down"), mine_time).astype(F32)
        if step < steps - 1:
            mine_down = grad_down.astype(BF16)
    return reduced[None], grad_clips[None], grad_time, grad_down


def solution(mesh):
    in_specs = (
        P("group", "tm", None, None),
        P("group", None),
        P(None, "tm", None),
        P(None, "tm", None),
        P("group", "tm", None, None),
    )
    out_specs = (
        P("group", "tm", None, None),
        P("group", "tm", None, None),
        P(None, "tm", None),
        P(None, "tm", None),
    )
    return jax.shard_map(shards, mesh=mesh, in_specs=in_specs, out_specs=out_specs, check_vma=False)
```

time: 100 us -> 80.5 us (0.81)
  the two profiles are of different devices: /device:TPU:0 before, /device:TPU:1 now
where the time goes in v2:
time: 80.5 us; the launch traced here: 80.2 us
  starting transfers between devices  35.4 us (44%)
  waiting for transfers between devices  20.8 us (26%)
  Pallas kernels  16.5 us (20%)
  other arithmetic  4.49 us (6%)
  local copies, waits for them, and re-layouts  2.07 us (3%)
  between operations  0.91 us (1%)
    pallas_call x4, Pallas kernels, call(): pl.pallas_call(kernel, in_specs=[SMEM] + [VMEM] * (len(inputs) - 1), out_...  13.9 us
    ppermute x7, starting transfers between devices, exchange(): return lax.ppermute(value, 'tm', route)  12.8 us
    ppermute x4, starting transfers between devices, group_exchange(): return lax.ppermute(value, ('tm', 'group'), route)  9.53 us
    ppermute x4, waiting for transfers between devices, group_exchange(): return lax.ppermute(value, ('tm', 'group'), route)  9.51 us
    ppermute x3, starting transfers between devices, shifted(): return lax.ppermute(block, axis, route)  9.16 us
    ppermute x7, waiting for transfers between devices, exchange(): return lax.ppermute(value, 'tm', route)  5.64 us
    ppermute x12, starting transfers between devices, core_swap(): lax.ppermute(value, 'tm', [(i, i ^ 1) for i in range(lax.axis_size('tm'))])  3.9 us
    ppermute x3, waiting for transfers between devices, shifted(): return lax.ppermute(block, axis, route)  3.55 us
  transfers between devices with their start and end apart: 26, of which 13 were waited for; matrix products, arithmetic and copies ran while one was open for 7% of the time, Pallas kernels for 16%

profile of v2, /device:TPU:1, one launch (start us, length us, event | category | flops | bytes accessed | tf_op | source)
XLA Modules:
  0.0 80.2 jit_solution(17301284401440178530)
XLA Ops:
  0.8 2.7 %collective-permute-start = (bf16[3,64,512]{2,1,0:T(8,128)(2,1)}, bf16[3,64,512]{2,1,0:T(8,128)(2,1)S(1)}, u32[]{:S(2)}, u32[]{:S(2)}) collective-permute-start(bf16[3,64,512]{2,1,0:T(8,128)(2,1)} %refs_0_.7), channel_id=1, source_target_pairs={{0,8},{4,20},{8,0},{12,28},{16,24},{20,4},{24,16},{28,12},{1,9},{5... | collective-permute-start | bytes 589832 | tf_op jit(solution)/shard_map/down_tm_0/ppermute | solution.py:31
  3.8 1.2 %collective-permute-start.1 = (bf16[3,64,512]{2,1,0:T(8,128)(2,1)}, bf16[3,64,512]{2,1,0:T(8,128)(2,1)S(1)}, u32[]{:S(2)}, u32[]{:S(2)}) collective-permute-start(bf16[3,64,512]{2,1,0:T(8,128)(2,1)} %refs_0_.6), channel_id=1, source_target_pairs={{0,8},{4,20},{8,0},{12,28},{16,24},{20,4},{24,16},{28,12},{1,9},{5... | collective-permute-start | bytes 589832 | tf_op jit(solution)/shard_map/time_tm_0/ppermute | solution.py:31
  5.0 0.8 %reduce-window.8 = s32[8,1]{0,1:T(1,128)S(1)} reduce-window(s32[8,1]{0,1:T(1,128)} %bitcast.42, s32[]{:T(128)} %constant.16.clone.1), window={size=8x1 pad=7_0x0_0}, to_apply=%region_0.0 | reduce-window | flops 56 | bytes 68 | tf_op jit(solution)/shard_map/reduce-window.3
  6.0 1.0 %slice_bitcast_fusion.1 = bf16[2,128,512]{2,1,0:T(8,128)(2,1)S(1)} fusion(bf16[1,8,128,512]{3,2,1,0:T(8,128)(2,1)} %param.5), kind=kLoop, calls=%fused_computation.21 | loop fusion | bytes 524288 | tf_op jit(solution)/shard_map/slice | solution.py:308
  6.9 1.0 %slice_bitcast_fusion = bf16[2,128,512]{2,1,0:T(8,128)(2,1)S(1)} fusion(bf16[1,4,128,512]{3,2,1,0:T(8,128)(2,1)} %param.9), kind=kLoop, calls=%fused_computation.20 | loop fusion | bytes 524288 | tf_op jit(solution)/shard_map/slice | solution.py:307
  9.1 0.7 collective-permute-start.7
  9.9 1.1 %pad_maximum_fusion = bf16[4,3,64,512]{3,2,1,0:T(8,128)(2,1)S(1)} fusion(bf16[1,3,64,512]{3,2,1,0:T(8,128)(2,1)S(1)} %bitcast.35, bf16[1,3,64,512]{3,2,1,0:T(8,128)(2,1)} %bitcast.34, bf16[1,3,64,512]{3,2,1,0:T(8,128)(2,1)S(1)} %bitcast.33, bf16[1,3,64,512]{3,2,1,0:T(8,128)(2,1)} %bitcast.32), kind=kLoop, calls=%fused_computation.8 | loop fusion | flops 1179648 | bytes 1572864 | tf_op jit(solution)/shard_map/stack | solution.py:306
  11.0 1.7 %collective-permute-start.8 = (bf16[4,3,64,512]{3,2,1,0:T(8,128)(2,1)S(1)}, bf16[4,3,64,512]{3,2,1,0:T(8,128)(2,1)S(1)}, u32[]{:S(2)}, u32[]{:S(2)}) collective-permute-start(bf16[4,3,64,512]{3,2,1,0:T(8,128)(2,1)S(1)} %pad_maximum_fusion), channel_id=1, source_target_pairs={{0,16},{4,12},{8,24},{12,4},{16,0},{20,28},{24,8},{28,20},{1,17},{... | collective-permute-start | bytes 2359304 | tf_op jit(solution)/shard_map/late_tm_1/ppermute | solution.py:31
  12.8 3.3 %collective-permute-start.2 = (bf16[2,128,512]{2,1,0:T(8,128)(2,1)S(1)}, bf16[2,128,512]{2,1,0:T(8,128)(2,1)S(1)}, u32[]{:S(2)}, u32[]{:S(2)}) collective-permute-start(bf16[2,128,512]{2,1,0:T(8,128)(2,1)S(1)} %slice_bitcast_fusion.1), channel_id=1, source_target_pairs={{0,4},{4,8},{8,12},{12,16},{16,20},{20,24},{24,28},{1,5},{5,9},{9,... | collective-permute-start | bytes 786440 | tf_op jit(solution)/shard_map/halo_tm1_2/ppermute | solution.py:56
  16.1 1.9 %collective-permute-start.3 = (bf16[2,128,512]{2,1,0:T(8,128)(2,1)S(1)}, bf16[2,128,512]{2,1,0:T(8,128)(2,1)S(1)}, u32[]{:S(2)}, u32[]{:S(2)}) collective-permute-start(bf16[2,128,512]{2,1,0:T(8,128)(2,1)S(1)} %slice_bitcast_fusion), channel_id=1, source_target_pairs={{4,0},{8,4},{12,8},{16,12},{20,16},{24,20},{28,24},{5,1},{9,5},{13... | collective-permute-start | bytes 786440 | tf_op jit(solution)/shard_map/halo_tm-1_2/ppermute | solution.py:56
  18.1 2.6 %features.1 = (bf16[8,128,512]{2,1,0:T(8,128)(2,1)S(1)}, bf16[512,1024]{1,0:T(8,128)(2,1)S(1)}) custom-call(s32[23]{0:T(128)S(1)} %pad_add_fusion.meta, bf16[8,128,512]{2,1,0:T(8,128)(2,1)S(1)} %bitcast.27), custom_call_target="tpu_custom_call" | custom-call | flops 20000000000 | bytes 1000 | tf_op jit(solution)/shard_map/features/pallas_call | solution.py:313
  20.7 2.5 %collective-permute-done.8.refs_2_ = bf16[4,3,64,512]{3,2,1,0:T(8,128)(2,1)S(1)} collective-permute-done((bf16[4,3,64,512]{3,2,1,0:T(8,128)(2,1)S(1)}, bf16[4,3,64,512]{3,2,1,0:T(8,128)(2,1)S(1)}, u32[]{:S(2)}, u32[]{:S(2)}) %collective-permute-start.8) | collective-permute-done | bytes 786464 | tf_op jit(solution)/shard_map/late_tm_1/ppermute | solution.py:31
  24.5 2.1 %collective-permute-done.3.cot_next = bf16[2,128,512]{2,1,0:T(8,128)(2,1)S(1)} collective-permute-done((bf16[2,128,512]{2,1,0:T(8,128)(2,1)S(1)}, bf16[2,128,512]{2,1,0:T(8,128)(2,1)S(1)}, u32[]{:S(2)}, u32[]{:S(2)}) %collective-permute-start.3) | collective-permute-done | bytes 262176 | tf_op jit(solution)/shard_map/halo_tm-1_2/ppermute | solution.py:56
  26.7 3.5 %backward.1 = (f32[8,128,512]{2,1,0:T(8,128)S(1)}, bf16[10,128,512]{2,1,0:T(8,128)(2,1)S(1)}, f32[2,3,64,512]{3,2,1,0:T(8,128)S(1)}, f32[2,3,64,512]{3,2,1,0:T(8,128)S(1)}, bf16[4,3,64,512]{3,2,1,0:T(8,128)(2,1)S(1)}) custom-call(s32[23]{0:T(128)S(1)} %pad_add_fusion.meta, bf16[4,128,512]{2,1,0:T(8,128)(2,1)S(1)} %bitcast.30, ...), custom_call_target="tpu_custom_call" | custom-call | flops 1000000 | bytes 1000 | tf_op jit(solution)/shard_map/backward/pallas_call | solution.py:281
  30.8 1.7 %collective-permute-done.11 = bf16[4,3,64,512]{3,2,1,0:T(8,128)(2,1)S(1)} collective-permute-done((bf16[4,3,64,512]{3,2,1,0:T(8,128)(2,1)S(1)}, bf16[4,3,64,512]{3,2,1,0:T(8,128)(2,1)S(1)}, u32[]{:S(2)}, u32[]{:S(2)}) %collective-permute-start.11) | collective-permute-done | bytes 786464 | tf_op jit(solution)/shard_map/grad_time_tm_core/ppermute | solution.py:36
  32.9 2.7 %collective-permute-start.14 = (bf16[2,3,64,512]{3,2,1,0:T(8,128)(2,1)S(1)}, bf16[2,3,64,512]{3,2,1,0:T(8,128)(2,1)S(1)}, u32[]{:S(2)}, u32[]{:S(2)}) collective-permute-start(bf16[2,3,64,512]{3,2,1,0:T(8,128)(2,1)S(1)} %fusion.3), channel_id=1, source_target_pairs={{0,8},{4,20},{8,0},{12,28},{16,24},{20,4},{24,16},{28,12},{1,9},{5... | collective-permute-start | bytes 1179656 | tf_op jit(solution)/shard_map/grad_time_tm_0/ppermute | solution.py:31
  35.6 3.6 %forward.1 = (bf16[8,128,512]{2,1,0:T(8,128)(2,1)S(1)}, bf16[2,128,512]{2,1,0:T(8,128)(2,1)S(1)}, f32[2,3,64,512]{3,2,1,0:T(8,128)S(1)}, f32[2,3,64,512]{3,2,1,0...) custom-call(s32[23]{0:T(128)S(1)} %pad_add_fusion.meta, ...), custom_call_target="tpu_custom_call" | custom-call | flops 1000000 | bytes 1000 | tf_op jit(solution)/shard_map/forward/pallas_call | solution.py:281
  41.9 2.0 %collective-permute-start.18 = (bf16[2,3,64,512]{3,2,1,0:T(8,128)(2,1)S(1)}, bf16[2,3,64,512]{3,2,1,0:T(8,128)(2,1)S(1)}, u32[]{:S(2)}, u32[]{:S(2)}) collective-permute-start(bf16[2,3,64,512]{3,2,1,0:T(8,128)(2,1)S(1)} %fusion), channel_id=1, source_target_pairs={{0,8},{4,20},{8,0},{12,28},{16,24},{20,4},{24,16},{28,12},{1,9},{5... | collective-permute-start | bytes 1179656 | tf_op jit(solution)/shard_map/grad_down_tm_0/ppermute | solution.py:31
  43.9 0.9 %collective-permute-start.20 = (bf16[1,3,64,512]{3,2,1,0:T(8,128)(2,1)S(1)}, bf16[1,3,64,512]{3,2,1,0:T(8,128)(2,1)S(1)}, u32[]{:S(2)}, u32[]{:S(2)}) collective-permute-start(bf16[1,3,64,512]{3,2,1,0:T(8,128)(2,1)S(1)} %slice.116), channel_id=1, source_target_pairs={{0,16},{4,12},{8,24},{12,4},{16,0},{20,28},{24,8},{28,20},{1,17},{... | collective-permute-start | bytes 589832 | tf_op jit(solution)/shard_map/grad_time_tm_1/ppermute | solution.py:31
  44.7 4.4 %clips.1 = bf16[8,128,512]{2,1,0:T(8,128)(2,1)} custom-call(s32[23]{0:T(128)S(1)} %pad_add_fusion.meta, bf16[8,128,512]{2,1,0:T(8,128)(2,1)S(1)} %bitcast.29, f32[8,128,512]{2,1,0:T(8,128)S(1)} %get-tuple-element.64.gh, bf16[10,128,512]{2,1,0:T(8,128)(2,1)S(1)} %get-tuple-element.65.gm, bf16[3,64,512]{2,1,0:T(8,128)(2,1)S(1)} %copy-done.3, ...), custom_call_target="tpu_custom_call" | custom-call | flops 1000000 | bytes 1000 | tf_op jit(solution)/shard_map/clips/pallas_call | solution.py:281
  49.1 1.8 %collective-permute-done.18 = bf16[2,3,64,512]{3,2,1,0:T(8,128)(2,1)S(1)} collective-permute-done((bf16[2,3,64,512]{3,2,1,0:T(8,128)(2,1)S(1)}, bf16[2,3,64,512]{3,2,1,0:T(8,128)(2,1)S(1)}, u32[]{:S(2)}, u32[]{:S(2)}) %collective-permute-start.18) | collective-permute-done | bytes 393248 | tf_op jit(solution)/shard_map/grad_down_tm_0/ppermute | solution.py:31
  51.2 1.7 %collective-permute-start.19 = (bf16[1,3,64,512]{3,2,1,0:T(8,128)(2,1)S(1)}, bf16[1,3,64,512]{3,2,1,0:T(8,128)(2,1)S(1)}, u32[]{:S(2)}, u32[]{:S(2)}) collective-permute-start(bf16[1,3,64,512]{3,2,1,0:T(8,128)(2,1)S(1)} %slice.115), channel_id=1, source_target_pairs={{0,16},{4,12},{8,24},{12,4},{16,0},{20,28},{24,8},{28,20},{1,17},{... | collective-permute-start | bytes 589832 | tf_op jit(solution)/shard_map/grad_down_tm_1/ppermute | solution.py:31
  52.9 3.9 %collective-permute-start.21 = (bf16[2,128,512]{2,1,0:T(8,128)(2,1)S(1)}, bf16[2,128,512]{2,1,0:T(8,128)(2,1)S(1)}, u32[]{:S(2)}, u32[]{:S(2)}) collective-permute-start(bf16[2,128,512]{2,1,0:T(8,128)(2,1)S(1)} %get-tuple-element.71), channel_id=1, source_target_pairs={{0,4},{4,8},{8,12},{12,16},{16,20},{20,24},{24,28},{1,5},{5,9},{9,... | collective-permute-start | bytes 786440 | tf_op jit(solution)/shard_map/halo_tm1_2/ppermute | solution.py:56
  56.8 2.4 %collective-permute-start.22 = (bf16[3,64,512]{2,1,0:T(8,128)(2,1)S(1)}, bf16[3,64,512]{2,1,0:T(8,128)(2,1)S(1)}, u32[]{:S(2)}, u32[]{:S(2)}) collective-permute-start(bf16[3,64,512]{2,1,0:T(8,128)(2,1)S(1)} %fusion.7), channel_id=1, source_target_pairs={{0,1},{1,0},{2,3},{3,2},{4,6},{5,7},{6,4},{7,5},{8,9},{9,8},{10,11... | collective-permute-start | bytes 589832 | tf_op jit(solution)/shard_map/grad_time_group_0/ppermute | solution.py:49
  59.4 0.8 collective-permute-done.21.before
  60.1 2.4 %reduced.1 = bf16[4,128,512]{2,1,0:T(8,128)(2,1)} custom-call(s32[23]{0:T(128)S(1)} %pad_add_fusion.meta, bf16[2,128,512]{2,1,0:T(8,128)(2,1)S(1)} %collective-permute-done.21.before, bf16[8,128,512]{2,1,0:T(8,128)(2,1)S(1)} %get-tuple-element.53.hidden, bf16[3,64,512]{2,1,0:T(8,128)(2,1)S(1)} %copy-done.2, ...), custom_call_target="tpu_custom_call" | custom-call | flops 1000000 | bytes 1000 | tf_op jit(solution)/shard_map/reduced/pallas_call | solution.py:281
  62.6 1.0 %collective-permute-done.22 = bf16[3,64,512]{2,1,0:T(8,128)(2,1)S(1)} collective-permute-done((bf16[3,64,512]{2,1,0:T(8,128)(2,1)S(1)}, bf16[3,64,512]{2,1,0:T(8,128)(2,1)S(1)}, u32[]{:S(2)}, u32[]{:S(2)}) %collective-permute-start.22) | collective-permute-done | bytes 196640 | tf_op jit(solution)/shard_map/grad_time_group_0/ppermute | solution.py:49
  63.6 2.5 %collective-permute-start.23 = (bf16[3,64,512]{2,1,0:T(8,128)(2,1)S(1)}, bf16[3,64,512]{2,1,0:T(8,128)(2,1)S(1)}, u32[]{:S(2)}, u32[]{:S(2)}) collective-permute-start(bf16[3,64,512]{2,1,0:T(8,128)(2,1)S(1)} %add_convert_fusion.1), channel_id=1, source_target_pairs={{0,2},{1,3},{2,0},{3,1},{4,5},{5,4},{6,7},{7,6},{8,10},{9,11},{10,... | collective-permute-start | bytes 589832 | tf_op jit(solution)/shard_map/grad_time_group_1/ppermute | solution.py:49
  66.1 5.1 %collective-permute-done.24 = bf16[3,64,512]{2,1,0:T(8,128)(2,1)S(1)} collective-permute-done((bf16[3,64,512]{2,1,0:T(8,128)(2,1)S(1)}, bf16[3,64,512]{2,1,0:T(8,128)(2,1)S(1)}, u32[]{:S(2)}, u32[]{:S(2)}) %collective-permute-start.24) | collective-permute-done | bytes 196640 | tf_op jit(solution)/shard_map/grad_down_group_0/ppermute | solution.py:49
  71.3 4.5 %collective-permute-start.25 = (bf16[3,64,512]{2,1,0:T(8,128)(2,1)S(1)}, bf16[3,64,512]{2,1,0:T(8,128)(2,1)S(1)}, u32[]{:S(2)}, u32[]{:S(2)}) collective-permute-start(bf16[3,64,512]{2,1,0:T(8,128)(2,1)S(1)} %add_convert_fusion), channel_id=1, source_target_pairs={{0,2},{1,3},{2,0},{3,1},{4,5},{5,4},{6,7},{7,6},{8,10},{9,11},{10,... | collective-permute-start | bytes 589832 | tf_op jit(solution)/shard_map/grad_down_group_1/ppermute | solution.py:49
  75.8 3.4 %collective-permute-done.25 = bf16[3,64,512]{2,1,0:T(8,128)(2,1)S(1)} collective-permute-done((bf16[3,64,512]{2,1,0:T(8,128)(2,1)S(1)}, bf16[3,64,512]{2,1,0:T(8,128)(2,1)S(1)}, u32[]{:S(2)}, u32[]{:S(2)}) %collective-permute-start.25) | collective-permute-done | bytes 196640 | tf_op jit(solution)/shard_map/grad_down_group_1/ppermute | solution.py:49
  79.2 1.0 %convert_add_fusion = (f32[3,64,512]{2,1,0:T(8,128)}, f32[3,64,512]{2,1,0:T(8,128)}) fusion(bf16[3,64,512]{2,1,0:T(8,128)(2,1)S(1)} %collective-permute-done.25, bf16[3,64,512]{2,1,0:T(8,128)(2,1)S(1)} %add_convert_fusion, bf16[3,64,512]{2,1,0:T(8,128)(2,1)S(1)} %collective-permute-done.23, bf16[3,64,512]{2,1,0:T(8,128)(2,1)S(1)} %add_convert_fusion.1), kind=kLoop, calls=%fused_computation.16 | loop fusion | flops 589824 | bytes 1572864 | tf_op jit(solution)/shard_map/add | solution.py:407
  (57 shorter events, 7.4 us)
Async XLA Ops:
  0.6 17.4 %copy-start = (bf16[1,8,128,512]{3,2,1,0:T(8,128)(2,1)S(1)}, bf16[1,8,128,512]{3,2,1,0:T(8,128)(2,1)}, u32[]{:S(2)}) copy-start(bf16[1,8,128,512]{3,2,1,0:T(8,128)(2,1)} %param.5) | copy-start | bytes 3145732
  0.6 15.4 %collective-permute-start.4 = (bf16[3,64,512]{2,1,0:T(8,128)(2,1)}, bf16[3,64,512]{2,1,0:T(8,128)(2,1)S(1)}, u32[]{:S(2)}, u32[]{:S(2)}) collective-permute-start(bf16[3,64,512]{2,1,0:T(8,128)(2,1)} %refs_0_.7), channel_id=1, source_target_pairs={{0,4},{4,0},{8,12},{12,8},{16,20},{20,16},{24,28},{28,24},{1,5},{5... | collective-permute-start | bytes 589832 | tf_op jit(solution)/shard_map/down_tm_core/ppermute | solution.py:36
  0.8 7.2 %collective-permute-start = (bf16[3,64,512]{2,1,0:T(8,128)(2,1)}, bf16[3,64,512]{2,1,0:T(8,128)(2,1)S(1)}, u32[]{:S(2)}, u32[]{:S(2)}) collective-permute-start(bf16[3,64,512]{2,1,0:T(8,128)(2,1)} %refs_0_.7), channel_id=1, source_target_pairs={{0,8},{4,20},{8,0},{12,28},{16,24},{20,4},{24,16},{28,12},{1,9},{5... | collective-permute-start | bytes 589832 | tf_op jit(solution)/shard_map/down_tm_0/ppermute | solution.py:31
  3.5 9.3 %collective-permute-start.6 = (bf16[3,64,512]{2,1,0:T(8,128)(2,1)}, bf16[3,64,512]{2,1,0:T(8,128)(2,1)S(1)}, u32[]{:S(2)}, u32[]{:S(2)}) collective-permute-start(bf16[3,64,512]{2,1,0:T(8,128)(2,1)} %refs_0_.6), channel_id=1, source_target_pairs={{0,4},{4,0},{8,12},{12,8},{16,20},{20,16},{24,28},{28,24},{1,5},{5... | collective-permute-start | bytes 589832 | tf_op jit(solution)/shard_map/time_tm_core/ppermute | solution.py:36
  3.8 5.3 %collective-permute-start.1 = (bf16[3,64,512]{2,1,0:T(8,128)(2,1)}, bf16[3,64,512]{2,1,0:T(8,128)(2,1)S(1)}, u32[]{:S(2)}, u32[]{:S(2)}) collective-permute-start(bf16[3,64,512]{2,1,0:T(8,128)(2,1)} %refs_0_.6), channel_id=1, source_target_pairs={{0,8},{4,20},{8,0},{12,28},{16,24},{20,4},{24,16},{28,12},{1,9},{5... | collective-permute-start | bytes 589832 | tf_op jit(solution)/shard_map/time_tm_0/ppermute | solution.py:31
  8.0 10.0 %collective-permute-start.5 = (bf16[3,64,512]{2,1,0:T(8,128)(2,1)S(1)}, bf16[3,64,512]{2,1,0:T(8,128)(2,1)S(1)}, u32[]{:S(2)}, u32[]{:S(2)}) collective-permute-start(bf16[3,64,512]{2,1,0:T(8,128)(2,1)S(1)} %collective-permute-done.refs_1_), channel_id=1, source_target_pairs={{0,4},{4,0},{8,12},{12,8},{16,20},{20,16},{24,28},{28,24},{1,5},{5... | collective-permute-start | bytes 589832 | tf_op jit(solution)/shard_map/down_tm_core/ppermute | solution.py:36
  9.1 8.9 %collective-permute-start.7 = (bf16[3,64,512]{2,1,0:T(8,128)(2,1)S(1)}, bf16[3,64,512]{2,1,0:T(8,128)(2,1)S(1)}, u32[]{:S(2)}, u32[]{:S(2)}) collective-permute-start(bf16[3,64,512]{2,1,0:T(8,128)(2,1)S(1)} %collective-permute-done.1.refs_1_), channel_id=1, source_target_pairs={{0,4},{4,0},{8,12},{12,8},{16,20},{20,16},{24,28},{28,24},{1,5},{5... | collective-permute-start | bytes 589832 | tf_op jit(solution)/shard_map/time_tm_core/ppermute | solution.py:36
  11.0 12.2 %collective-permute-start.8 = (bf16[4,3,64,512]{3,2,1,0:T(8,128)(2,1)S(1)}, bf16[4,3,64,512]{3,2,1,0:T(8,128)(2,1)S(1)}, u32[]{:S(2)}, u32[]{:S(2)}) collective-permute-start(bf16[4,3,64,512]{3,2,1,0:T(8,128)(2,1)S(1)} %pad_maximum_fusion), channel_id=1, source_target_pairs={{0,16},{4,12},{8,24},{12,4},{16,0},{20,28},{24,8},{28,20},{1,17},{... | collective-permute-start | bytes 2359304 | tf_op jit(solution)/shard_map/late_tm_1/ppermute | solution.py:31
  12.8 11.7 %collective-permute-start.2 = (bf16[2,128,512]{2,1,0:T(8,128)(2,1)S(1)}, bf16[2,128,512]{2,1,0:T(8,128)(2,1)S(1)}, u32[]{:S(2)}, u32[]{:S(2)}) collective-permute-start(bf16[2,128,512]{2,1,0:T(8,128)(2,1)S(1)} %slice_bitcast_fusion.1), channel_id=1, source_target_pairs={{0,4},{4,8},{8,12},{12,16},{16,20},{20,24},{24,28},{1,5},{5,9},{9,... | collective-permute-start | bytes 786440 | tf_op jit(solution)/shard_map/halo_tm1_2/ppermute | solution.py:56
  16.1 10.6 %collective-permute-start.3 = (bf16[2,128,512]{2,1,0:T(8,128)(2,1)S(1)}, bf16[2,128,512]{2,1,0:T(8,128)(2,1)S(1)}, u32[]{:S(2)}, u32[]{:S(2)}) collective-permute-start(bf16[2,128,512]{2,1,0:T(8,128)(2,1)S(1)} %slice_bitcast_fusion), channel_id=1, source_target_pairs={{4,0},{8,4},{12,8},{16,12},{20,16},{24,20},{28,24},{5,1},{9,5},{13... | collective-permute-start | bytes 786440 | tf_op jit(solution)/shard_map/halo_tm-1_2/ppermute | solution.py:56
  18.0 8.6 %copy-start.1 = (bf16[1,4,128,512]{3,2,1,0:T(8,128)(2,1)S(1)}, bf16[1,4,128,512]{3,2,1,0:T(8,128)(2,1)}, u32[]{:S(2)}) copy-start(bf16[1,4,128,512]{3,2,1,0:T(8,128)(2,1)} %param.9) | copy-start | bytes 1572868
  18.1 8.6 %copy-start.2 = (bf16[3,64,512]{2,1,0:T(8,128)(2,1)S(1)}, bf16[3,64,512]{2,1,0:T(8,128)(2,1)}, u32[]{:S(2)}) copy-start(bf16[3,64,512]{2,1,0:T(8,128)(2,1)} %refs_0_.7) | copy-start | bytes 589828
  23.3 3.4 %collective-permute-start.10 = (bf16[3,64,512]{2,1,0:T(8,128)(2,1)S(1)}, bf16[3,64,512]{2,1,0:T(8,128)(2,1)S(1)}, u32[]{:S(2)}, u32[]{:S(2)}) collective-permute-start(bf16[3,64,512]{2,1,0:T(8,128)(2,1)S(1)} %get-tuple-element.76), channel_id=1, source_target_pairs={{0,4},{4,0},{8,12},{12,8},{16,20},{20,16},{24,28},{28,24},{1,5},{5... | collective-permute-start | bytes 589832 | tf_op jit(solution)/shard_map/down_tm_core/ppermute | solution.py:36
  23.4 3.3 %collective-permute-start.9 = (bf16[3,64,512]{2,1,0:T(8,128)(2,1)S(1)}, bf16[3,64,512]{2,1,0:T(8,128)(2,1)S(1)}, u32[]{:S(2)}, u32[]{:S(2)}) collective-permute-start(bf16[3,64,512]{2,1,0:T(8,128)(2,1)S(1)} %get-tuple-element.77), channel_id=1, source_target_pairs={{0,4},{4,0},{8,12},{12,8},{16,20},{20,16},{24,28},{28,24},{1,5},{5... | collective-permute-start | bytes 589832 | tf_op jit(solution)/shard_map/down_tm_core/ppermute | solution.py:36
  30.2 2.4 %collective-permute-start.11 = (bf16[4,3,64,512]{3,2,1,0:T(8,128)(2,1)S(1)}, bf16[4,3,64,512]{3,2,1,0:T(8,128)(2,1)S(1)}, u32[]{:S(2)}, u32[]{:S(2)}) collective-permute-start(bf16[4,3,64,512]{3,2,1,0:T(8,128)(2,1)S(1)} %get-tuple-element.48), channel_id=1, source_target_pairs={{0,4},{4,0},{8,12},{12,8},{16,20},{20,16},{24,28},{28,24},{1,5},{5... | collective-permute-start | bytes 2359304 | tf_op jit(solution)/shard_map/grad_time_tm_core/ppermute | solution.py:36
  30.3 5.3 %collective-permute-start.12 = (bf16[2,3,64,512]{3,2,1,0:T(8,128)(2,1)S(1)}, bf16[2,3,64,512]{3,2,1,0:T(8,128)(2,1)S(1)}, u32[]{:S(2)}, u32[]{:S(2)}) collective-permute-start(bf16[2,3,64,512]{3,2,1,0:T(8,128)(2,1)S(1)} %slice.67), channel_id=1, source_target_pairs={{0,4},{4,0},{8,12},{12,8},{16,20},{20,16},{24,28},{28,24},{1,5},{5... | collective-permute-start | bytes 1179656 | tf_op jit(solution)/shard_map/time_tm_core/ppermute | solution.py:36
  32.7 2.9 %copy-start.3 = (bf16[3,64,512]{2,1,0:T(8,128)(2,1)S(1)}, bf16[3,64,512]{2,1,0:T(8,128)(2,1)}, u32[]{:S(2)}) copy-start(bf16[3,64,512]{2,1,0:T(8,128)(2,1)} %refs_0_.6) | copy-start | bytes 589828
  32.9 8.0 %collective-permute-start.14 = (bf16[2,3,64,512]{3,2,1,0:T(8,128)(2,1)S(1)}, bf16[2,3,64,512]{3,2,1,0:T(8,128)(2,1)S(1)}, u32[]{:S(2)}, u32[]{:S(2)}) collective-permute-start(bf16[2,3,64,512]{3,2,1,0:T(8,128)(2,1)S(1)} %fusion.3), channel_id=1, source_target_pairs={{0,8},{4,20},{8,0},{12,28},{16,24},{20,4},{24,16},{28,12},{1,9},{5... | collective-permute-start | bytes 1179656 | tf_op jit(solution)/shard_map/grad_time_tm_0/ppermute | solution.py:31
  39.2 1.9 %collective-permute-start.13 = (bf16[3,64,512]{2,1,0:T(8,128)(2,1)S(1)}, bf16[3,64,512]{2,1,0:T(8,128)(2,1)S(1)}, u32[]{:S(2)}, u32[]{:S(2)}) collective-permute-start(bf16[3,64,512]{2,1,0:T(8,128)(2,1)S(1)} %get-tuple-element.51), channel_id=1, source_target_pairs={{0,4},{4,0},{8,12},{12,8},{16,20},{20,16},{24,28},{28,24},{1,5},{5... | collective-permute-start | bytes 589832 | tf_op jit(solution)/shard_map/grad_down_tm_core/ppermute | solution.py:36
  39.3 1.9 %collective-permute-start.15 = (bf16[3,64,512]{2,1,0:T(8,128)(2,1)S(1)}, bf16[3,64,512]{2,1,0:T(8,128)(2,1)S(1)}, u32[]{:S(2)}, u32[]{:S(2)}) collective-permute-start(bf16[3,64,512]{2,1,0:T(8,128)(2,1)S(1)} %get-tuple-element.56), channel_id=1, source_target_pairs={{0,4},{4,0},{8,12},{12,8},{16,20},{20,16},{24,28},{28,24},{1,5},{5... | collective-permute-start | bytes 589832 | tf_op jit(solution)/shard_map/grad_down_tm_core/ppermute | solution.py:36
  39.8 1.5 %collective-permute-start.16 = (bf16[3,64,512]{2,1,0:T(8,128)(2,1)S(1)}, bf16[3,64,512]{2,1,0:T(8,128)(2,1)S(1)}, u32[]{:S(2)}, u32[]{:S(2)}) collective-permute-start(bf16[3,64,512]{2,1,0:T(8,128)(2,1)S(1)} %get-tuple-element.58), channel_id=1, source_target_pairs={{0,4},{4,0},{8,12},{12,8},{16,20},{20,16},{24,28},{28,24},{1,5},{5... | collective-permute-start | bytes 589832 | tf_op jit(solution)/shard_map/grad_down_tm_core/ppermute | solution.py:36
  39.9 1.7 %collective-permute-start.17 = (bf16[3,64,512]{2,1,0:T(8,128)(2,1)S(1)}, bf16[3,64,512]{2,1,0:T(8,128)(2,1)S(1)}, u32[]{:S(2)}, u32[]{:S(2)}) collective-permute-start(bf16[3,64,512]{2,1,0:T(8,128)(2,1)S(1)} %get-tuple-element.60), channel_id=1, source_target_pairs={{0,4},{4,0},{8,12},{12,8},{16,20},{20,16},{24,28},{28,24},{1,5},{5... | collective-permute-start | bytes 589832 | tf_op jit(solution)/shard_map/grad_down_tm_core/ppermute | solution.py:36
  41.9 9.0 %collective-permute-start.18 = (bf16[2,3,64,512]{3,2,1,0:T(8,128)(2,1)S(1)}, bf16[2,3,64,512]{3,2,1,0:T(8,128)(2,1)S(1)}, u32[]{:S(2)}, u32[]{:S(2)}) collective-permute-start(bf16[2,3,64,512]{3,2,1,0:T(8,128)(2,1)S(1)} %fusion), channel_id=1, source_target_pairs={{0,8},{4,20},{8,0},{12,28},{16,24},{20,4},{24,16},{28,12},{1,9},{5... | collective-permute-start | bytes 1179656 | tf_op jit(solution)/shard_map/grad_down_tm_0/ppermute | solution.py:31
  43.9 9.0 %collective-permute-start.20 = (bf16[1,3,64,512]{3,2,1,0:T(8,128)(2,1)S(1)}, bf16[1,3,64,512]{3,2,1,0:T(8,128)(2,1)S(1)}, u32[]{:S(2)}, u32[]{:S(2)}) collective-permute-start(bf16[1,3,64,512]{3,2,1,0:T(8,128)(2,1)S(1)} %slice.116), channel_id=1, source_target_pairs={{0,16},{4,12},{8,24},{12,4},{16,0},{20,28},{24,8},{28,20},{1,17},{... | collective-permute-start | bytes 589832 | tf_op jit(solution)/shard_map/grad_time_tm_1/ppermute | solution.py:31
  51.2 8.0 %collective-permute-start.19 = (bf16[1,3,64,512]{3,2,1,0:T(8,128)(2,1)S(1)}, bf16[1,3,64,512]{3,2,1,0:T(8,128)(2,1)S(1)}, u32[]{:S(2)}, u32[]{:S(2)}) collective-permute-start(bf16[1,3,64,512]{3,2,1,0:T(8,128)(2,1)S(1)} %slice.115), channel_id=1, source_target_pairs={{0,16},{4,12},{8,24},{12,4},{16,0},{20,28},{24,8},{28,20},{1,17},{... | collective-permute-start | bytes 589832 | tf_op jit(solution)/shard_map/grad_down_tm_1/ppermute | solution.py:31
  52.9 7.2 %collective-permute-start.21 = (bf16[2,128,512]{2,1,0:T(8,128)(2,1)S(1)}, bf16[2,128,512]{2,1,0:T(8,128)(2,1)S(1)}, u32[]{:S(2)}, u32[]{:S(2)}) collective-permute-start(bf16[2,128,512]{2,1,0:T(8,128)(2,1)S(1)} %get-tuple-element.71), channel_id=1, source_target_pairs={{0,4},{4,8},{8,12},{12,16},{16,20},{20,24},{24,28},{1,5},{5,9},{9,... | collective-permute-start | bytes 786440 | tf_op jit(solution)/shard_map/halo_tm1_2/ppermute | solution.py:56
  56.8 6.7 %collective-permute-start.22 = (bf16[3,64,512]{2,1,0:T(8,128)(2,1)S(1)}, bf16[3,64,512]{2,1,0:T(8,128)(2,1)S(1)}, u32[]{:S(2)}, u32[]{:S(2)}) collective-permute-start(bf16[3,64,512]{2,1,0:T(8,128)(2,1)S(1)} %fusion.7), channel_id=1, source_target_pairs={{0,1},{1,0},{2,3},{3,2},{4,6},{5,7},{6,4},{7,5},{8,9},{9,8},{10,11... | collective-permute-start | bytes 589832 | tf_op jit(solution)/shard_map/grad_time_group_0/ppermute | solution.py:49
  59.2 12.0 %collective-permute-start.24 = (bf16[3,64,512]{2,1,0:T(8,128)(2,1)S(1)}, bf16[3,64,512]{2,1,0:T(8,128)(2,1)S(1)}, u32[]{:S(2)}, u32[]{:S(2)}) collective-permute-start(bf16[3,64,512]{2,1,0:T(8,128)(2,1)S(1)} %fusion.6), channel_id=1, source_target_pairs={{0,1},{1,0},{2,3},{3,2},{4,6},{5,7},{6,4},{7,5},{8,9},{9,8},{10,11... | collective-permute-start | bytes 589832 | tf_op jit(solution)/shard_map/grad_down_group_0/ppermute | solution.py:49
  63.6 12.2 %collective-permute-start.23 = (bf16[3,64,512]{2,1,0:T(8,128)(2,1)S(1)}, bf16[3,64,512]{2,1,0:T(8,128)(2,1)S(1)}, u32[]{:S(2)}, u32[]{:S(2)}) collective-permute-start(bf16[3,64,512]{2,1,0:T(8,128)(2,1)S(1)} %add_convert_fusion.1), channel_id=1, source_target_pairs={{0,2},{1,3},{2,0},{3,1},{4,5},{5,4},{6,7},{7,6},{8,10},{9,11},{10,... | collective-permute-start | bytes 589832 | tf_op jit(solution)/shard_map/grad_time_group_1/ppermute | solution.py:49
  71.3 8.0 %collective-permute-start.25 = (bf16[3,64,512]{2,1,0:T(8,128)(2,1)S(1)}, bf16[3,64,512]{2,1,0:T(8,128)(2,1)S(1)}, u32[]{:S(2)}, u32[]{:S(2)}) collective-permute-start(bf16[3,64,512]{2,1,0:T(8,128)(2,1)S(1)} %add_convert_fusion), channel_id=1, source_target_pairs={{0,2},{1,3},{2,0},{3,1},{4,5},{5,4},{6,7},{7,6},{8,10},{9,11},{10,... | collective-permute-start | bytes 589832 | tf_op jit(solution)/shard_map/grad_down_group_1/ppermute | solution.py:49

commit v3 on v2

--- a/solution.py
+++ b/solution.py
@@ -8,7 +8,6 @@
 from jax.sharding import PartitionSpec as P
 
 EPS = 1e-06
-DOWN, TIME = 0, 1
 FEATURES_COST = 20_000_000_000
 VMEM = pl.BlockSpec(memory_space=pltpu.VMEM)
 SMEM = pl.BlockSpec(memory_space=pltpu.SMEM)
@@ -97,11 +96,8 @@
     return pl.multiple_of(block * rows, rows)
 
 
-def assemble(meta, refs, which, full):
-    early = next(i for i, ref in enumerate(refs) if len(ref.shape) == 4)
-    pieces = list(refs[:early]) + [refs[early].at[which * early + i] for i in range(early)]
-    for ref in refs[early + 1:]:
-        pieces += [ref.at[i] for i in range(early)] if len(ref.shape) == 4 else [ref]
+def assemble(meta, pieces, full):
+    pieces = [piece for ref in pieces for piece in ([ref.at[i] for i in range(ref.shape[0])] if len(ref.shape) == 4 else [ref])]
     taps, rows, _ = pieces[0].shape
     chips = len(pieces) // 2
     for index, source in enumerate(pieces):
@@ -122,8 +118,6 @@
         part = value[index * rows:(index + 1) * rows]
         if index < 2 * half:
             shares[index // half][index % half, tap] = part
-        elif len(shares) == 3:
-            shares[2][index - 2 * half, tap] = part.astype(BF16)
         else:
             shares[2 + index - 2 * half][tap] = part.astype(BF16)
 
@@ -142,12 +136,13 @@
     place_rows(meta, chips, rows, flip, ht_out, slice(None))
 
 
-def backward_kernel(meta, cot, cot_next, ht, *refs):
-    *pieces, gh, gm, low, high, send, w, c0, c1, c2, m1, m2 = refs
-    shares = (low, high, send)
+def backward_kernel(meta, cot, cot_next, ht, *refs, chips):
+    w, c0, c1, c2, m1, m2 = refs[-6:]
+    *pieces, gh, gm = refs[:-8 - chips]
+    shares = refs[-8 - chips:-6]
     half, cells, _ = cot.shape
     frames = 2 * half
-    assemble(meta, pieces, DOWN, w)
+    assemble(meta, pieces, w)
 
     def cot_at(j):
         return cot[j] if j < half else cot_next[j - half]
@@ -187,7 +182,7 @@
     frames, cells, width = clips.shape
     half = frames // 2
     rows = shares[0].shape[2]
-    assemble(meta, pieces, TIME, w)
+    assemble(meta, pieces, w)
 
     h_before = [features(before[0]), features(before[1])]
 
@@ -225,7 +220,7 @@
     *pieces, reduced, w, t0, t1, t2 = refs
     frames, cells, width = hidden.shape
     half = frames // 2
-    assemble(meta, pieces, DOWN, w)
+    assemble(meta, pieces, w)
     for j in range(half):
         here = slice(j * cells, (j + 1) * cells)
         t0[here] = hidden[2 * j]
@@ -239,7 +234,7 @@
 def clips_kernel(meta, clips, gh, gm, *refs):
     *pieces, out, w, m1, m2 = refs
     frames, cells, width = clips.shape
-    assemble(meta, pieces, TIME, w)
+    assemble(meta, pieces, w)
     for g in range(frames):
         here = slice(g * cells, (g + 1) * cells)
         m1[here] = kept(live(meta, 1, g + 1, frames), gm[g + 1])
@@ -299,14 +294,17 @@
 
     down, time = [w_down], [w_time]
     for step in range(last):
-        earlier = down[1:] + time[1:]
-        down = down + [exchange(after(part, *earlier), step, "down") for part in down]
-        time = time + [exchange(after(part, *earlier), step, "time") for part in time]
-    first = down[1:] + time[1:]
-    late = jnp.stack(down + time)
-    cot_next = shifted(after(cot[:2], late), "tm", -1)
-    x_before = shifted(after(x[frames - 2:], late), "tm", 1)
-    late = exchange(late, last, "late")
+        down = down + [exchange(part, step, "down") for part in down]
+        time = time + [exchange(part, step, "time") for part in time]
+    down_own = exchange(w_down, last, "down_own")
+    cot_next = shifted(cot[:2], "tm", -1)
+    down_late = [exchange(part, last, "down") for part in down[1:]]
+    time_late = jnp.stack(time)
+    first = [cot_next, down_own] + down[1:] + time[1:]
+    time_late = after(time_late, cot_next, *down)
+    x_before = shifted(after(x[frames - 2:], time_late), "tm", 1)
+    time_late = exchange(time_late, last, "time")
+    down = down + [down_own]
     down_other = [core_swap(part, "down") for part in down]
     time_other = [core_swap(part, "time") for part in time]
 
@@ -323,33 +321,26 @@
         compiler_params=pltpu.CompilerParams(vmem_limit_bytes=36 * 1024 * 1024),
         cost_estimate=pl.CostEstimate(flops=FEATURES_COST, bytes_accessed=1000, transcendentals=0),
         name="features",
-    )(after(meta, *first, *down_other, *time_other), x)
-
-    late = after(late, h)
-    down = down + [late] + down_other + [core_swap(late[i], "down") for i in range(early)]
-    time_late = core_swap(late[early:], "time")
+    )(after(meta, *first, *down_late, *down_other, *time_other), x)
+
+    down = down + down_late + down_other + [after(core_swap(part, "down"), h) for part in down_late]
 
     shares = (
         sds((early, taps, rows, width), F32),
         sds((early, taps, rows, width), F32),
-        sds((chips, taps, rows, width)),
-    )
+    ) + (sds((taps, rows, width)),) * chips
     full = scratch(taps, width, width)
     gh, gm, *time_shares = call(
-        backward_kernel,
+        functools.partial(backward_kernel, chips=chips),
         "backward",
-        [after(meta, x_before), cot, cot_next, ht] + down,
+        [meta, cot, cot_next, ht] + down,
         (sds((frames, cells, width), F32), sds((frames + 2, cells, width))) + shares,
         [full] + [scratch((half + 1) * cells, width)] * 3 + [scratch(lot, width)] * 2,
     )
 
     def core_sum(shares, name, *earlier):
         low, high, *send = shares
-        if len(send) == 1:
-            other = after(core_swap(send[0], name), *earlier)
-        else:
-            other = jnp.stack([after(core_swap(part, name), *earlier) for part in send])
-        other = other.astype(F32)
+        other = jnp.stack([after(core_swap(part, name), *earlier) for part in send]).astype(F32)
         return low + other[:early], (high + other[early:]).astype(BF16)
 
     def plane_step(low, other):
@@ -360,14 +351,14 @@
     def group_sum(mine, step, name):
         return mine.astype(F32) + group_exchange(mine, step, name).astype(F32)
 
-    time = time + [late] + time_other + [time_late]
-    low_time, high_time = core_sum(time_shares, "grad_time")
+    time_late = after(time_late, gm)
+    time = time + [time_late] + time_other + [core_swap(time_late, "time")]
+    low_time, high_time = core_sum(time_shares, "grad_time", x_before)
     hidden, tail, *down_shares = call(
         functools.partial(forward_kernel, chips=chips),
         "forward",
         [after(meta, high_time), x, x_before, h, cot, cot_next] + time,
-        (sds((frames, cells, width)), sds((2, cells, width))) + shares[:2]
-        + (sds((taps, rows, width)),) * chips,
+        (sds((frames, cells, width)), sds((2, cells, width))) + shares,
         [full] + [scratch(lot, width)] * 2 + [scratch(width, cells)]
         + [scratch(width, half * cells)] * 2 + [scratch(half * cells, width)] * 2,
     )
@@ -384,24 +375,28 @@
                 sds((frames, cells, width)),
                 [full] + [scratch(lot, width)] * 2,
             )
-        other = after(exchange(high_down, step, "grad_down"), grad_clips)
+        if step == last - 1:
+            other = after(exchange(high_time, last, "grad_time"), grad_clips)
+            mine_time = (low_time[0] + other[0].astype(F32)).astype(BF16)
+            other = after(exchange(high_down, step, "grad_down"), mine_time)
+        else:
+            other = after(exchange(high_down, step, "grad_down"), grad_clips)
         low_down, high_down = plane_step(low_down, other)
-
-    other = after(exchange(high_time, last, "grad_time"), high_down)
-    mine_time = (low_time[0] + other[0].astype(F32)).astype(BF16)
-    before = shifted(after(tail, mine_time), "tm", 1)
-    other = after(exchange(high_down, last, "grad_down"), mine_time)
+    other = exchange(high_down, last, "grad_down")
     mine_down = (low_down[0] + other[0].astype(F32)).astype(BF16)
-    reduced = call(
-        reduced_kernel,
-        "reduced",
-        [after(meta, mine_down), before, hidden] + down,
-        sds((half, cells, width)),
-        [full] + [scratch(half * cells, width)] * 3,
-    )
+    before = shifted(after(tail, mine_down), "tm", 1)
     steps = len(bits_of(lax.axis_size("group")))
     for step in range(steps):
-        grad_time = mine_time.astype(F32) + after(group_exchange(mine_time, step, "grad_time"), reduced).astype(F32)
+        if step == steps - 1:
+            reduced = call(
+                reduced_kernel,
+                "reduced",
+                [after(meta, mine_down), before, hidden] + down,
+                sds((half, cells, width)),
+                [full] + [scratch(half * cells, width)] * 3,
+            )
+        done = mine_down if step < steps - 1 else reduced
+        grad_time = mine_time.astype(F32) + after(group_exchange(mine_time, step, "grad_time"), done).astype(F32)
         if step < steps - 1:
             mine_time = grad_time.astype(BF16)
         grad_down = mine_down.astype(F32) + after(group_exchange(mine_down, step, "grad_down"), mine_time).astype(F32)

time: 80.5 us -> 71.1 us (0.88)
  the two profiles are of different devices: /device:TPU:1 before, /device:TPU:0 now
where the time goes in v3:
time: 71.1 us; the launch traced here: 70.8 us
  starting transfers between devices  32 us (45%)
  Pallas kernels  16.5 us (23%)
  waiting for transfers between devices  14.3 us (20%)
  other arithmetic  4.87 us (7%)
  local copies, waits for them, and re-layouts  2.16 us (3%)
  between operations  0.88 us (1%)
    pallas_call x4, Pallas kernels, call(): pl.pallas_call(kernel, in_specs=[SMEM] + [VMEM] * (len(inputs) - 1), out_...  13.9 us
    ppermute x9, starting transfers between devices, exchange(): return lax.ppermute(value, 'tm', route)  11.8 us
    ppermute x9, waiting for transfers between devices, exchange(): return lax.ppermute(value, 'tm', route)  9.39 us
    ppermute x4, starting transfers between devices, group_exchange(): return lax.ppermute(value, ('tm', 'group'), route)  8.84 us
    ppermute x15, starting transfers between devices, core_swap(): lax.ppermute(value, 'tm', [(i, i ^ 1) for i in range(lax.axis_size('tm'))])  5.82 us
    ppermute x3, starting transfers between devices, shifted(): return lax.ppermute(block, axis, route)  5.57 us
    ppermute x4, waiting for transfers between devices, group_exchange(): return lax.ppermute(value, ('tm', 'group'), route)  3.78 us
    pallas_call x1, Pallas kernels, shards(): pl.pallas_call(functools.partial(features_kernel, chips=chips, rows=rows)...  2.59 us
  transfers between devices with their start and end apart: 31, of which 13 were waited for; matrix products, arithmetic and copies ran while one was open for 8% of the time, Pallas kernels for 23%

profile of v3, /device:TPU:0, one launch (start us, length us, event | category | flops | bytes accessed | tf_op | source)
XLA Modules:
  0.0 70.8 jit_solution(15439150803332678631)
XLA Ops:
  1.2 2.6 %collective-permute-start.3 = (bf16[3,64,512]{2,1,0:T(8,128)(2,1)}, bf16[3,64,512]{2,1,0:T(8,128)(2,1)S(1)}, u32[]{:S(2)}, u32[]{:S(2)}) collective-permute-start(bf16[3,64,512]{2,1,0:T(8,128)(2,1)} %refs_0_.6), channel_id=1, source_target_pairs={{0,8},{4,20},{8,0},{12,28},{16,24},{20,4},{24,16},{28,12},{1,9},{5... | collective-permute-start | bytes 589832 | tf_op jit(solution)/shard_map/time_tm_0/ppermute | solution.py:30
  3.8 2.0 %collective-permute-start.1 = (bf16[3,64,512]{2,1,0:T(8,128)(2,1)}, bf16[3,64,512]{2,1,0:T(8,128)(2,1)S(1)}, u32[]{:S(2)}, u32[]{:S(2)}) collective-permute-start(bf16[3,64,512]{2,1,0:T(8,128)(2,1)} %refs_0_.7), channel_id=1, source_target_pairs={{0,16},{4,12},{8,24},{12,4},{16,0},{20,28},{24,8},{28,20},{1,17},{... | collective-permute-start | bytes 589832 | tf_op jit(solution)/shard_map/down_own_tm_1/ppermute | solution.py:30
  5.8 1.0 %slice_bitcast_fusion.1 = bf16[2,128,512]{2,1,0:T(8,128)(2,1)S(1)} fusion(bf16[1,4,128,512]{3,2,1,0:T(8,128)(2,1)} %param.9), kind=kLoop, calls=%fused_computation.22 | loop fusion | bytes 524288 | tf_op jit(solution)/shard_map/slice | solution.py:300
  6.8 1.3 %collective-permute-start = (bf16[2,128,512]{2,1,0:T(8,128)(2,1)S(1)}, bf16[2,128,512]{2,1,0:T(8,128)(2,1)S(1)}, u32[]{:S(2)}, u32[]{:S(2)}) collective-permute-start(bf16[2,128,512]{2,1,0:T(8,128)(2,1)S(1)} %slice_bitcast_fusion.1), channel_id=1, source_target_pairs={{4,0},{8,4},{12,8},{16,12},{20,16},{24,20},{28,24},{5,1},{9,5},{13... | collective-permute-start | bytes 786440 | tf_op jit(solution)/shard_map/halo_tm-1_2/ppermute | solution.py:55
  8.1 1.0 %slice_bitcast_fusion = bf16[2,128,512]{2,1,0:T(8,128)(2,1)S(1)} fusion(bf16[1,8,128,512]{3,2,1,0:T(8,128)(2,1)} %param.5), kind=kLoop, calls=%fused_computation.21 | loop fusion | bytes 524288 | tf_op jit(solution)/shard_map/slice | solution.py:305
  9.0 0.8 %reduce-window.8 = s32[8,1]{0,1:T(1,128)S(1)} reduce-window(s32[8,1]{0,1:T(1,128)} %bitcast.42, s32[]{:T(128)} %constant.16.clone.1), window={size=8x1 pad=7_0x0_0}, to_apply=%region_0.0 | reduce-window | flops 56 | bytes 68 | tf_op jit(solution)/shard_map/reduce-window.3
  10.1 1.1 %collective-permute-start.5 = (bf16[3,64,512]{2,1,0:T(8,128)(2,1)}, bf16[3,64,512]{2,1,0:T(8,128)(2,1)S(1)}, u32[]{:S(2)}, u32[]{:S(2)}) collective-permute-start(bf16[3,64,512]{2,1,0:T(8,128)(2,1)} %refs_0_.7), channel_id=1, source_target_pairs={{0,4},{4,0},{8,12},{12,8},{16,20},{20,16},{24,28},{28,24},{1,5},{5... | collective-permute-start | bytes 589832 | tf_op jit(solution)/shard_map/down_tm_core/ppermute | solution.py:35
  11.2 0.6 collective-permute-done.2.refs_1_
  11.8 2.1 %collective-permute-start.4 = (bf16[3,64,512]{2,1,0:T(8,128)(2,1)S(1)}, bf16[3,64,512]{2,1,0:T(8,128)(2,1)S(1)}, u32[]{:S(2)}, u32[]{:S(2)}) collective-permute-start(bf16[3,64,512]{2,1,0:T(8,128)(2,1)S(1)} %collective-permute-done.2.refs_1_), channel_id=1, source_target_pairs={{0,16},{4,12},{8,24},{12,4},{16,0},{20,28},{24,8},{28,20},{1,17},{... | collective-permute-start | bytes 589832 | tf_op jit(solution)/shard_map/down_tm_1/ppermute | solution.py:30
  14.5 1.0 %pad_maximum_fusion = bf16[2,3,64,512]{3,2,1,0:T(8,128)(2,1)S(1)} fusion(bf16[1,3,64,512]{3,2,1,0:T(8,128)(2,1)S(1)} %bitcast.31, bf16[1,3,64,512]{3,2,1,0:T(8,128)(2,1)} %bitcast.30), kind=kLoop, calls=%fused_computation.16 | loop fusion | flops 196608 | bytes 786432 | tf_op jit(solution)/shard_map/stack | solution.py:302
  15.5 2.1 %collective-permute-start.16 = (bf16[2,3,64,512]{3,2,1,0:T(8,128)(2,1)S(1)}, bf16[2,3,64,512]{3,2,1,0:T(8,128)(2,1)S(1)}, u32[]{:S(2)}, u32[]{:S(2)}) collective-permute-start(bf16[2,3,64,512]{3,2,1,0:T(8,128)(2,1)S(1)} %pad_maximum_fusion), channel_id=1, source_target_pairs={{0,16},{4,12},{8,24},{12,4},{16,0},{20,28},{24,8},{28,20},{1,17},{... | collective-permute-start | bytes 1179656 | tf_op jit(solution)/shard_map/time_tm_1/ppermute | solution.py:30
  17.6 2.6 %collective-permute-start.12 = (bf16[2,128,512]{2,1,0:T(8,128)(2,1)S(1)}, bf16[2,128,512]{2,1,0:T(8,128)(2,1)S(1)}, u32[]{:S(2)}, u32[]{:S(2)}) collective-permute-start(bf16[2,128,512]{2,1,0:T(8,128)(2,1)S(1)} %slice_bitcast_fusion), channel_id=1, source_target_pairs={{0,4},{4,8},{8,12},{12,16},{16,20},{20,24},{24,28},{1,5},{5,9},{9,... | collective-permute-start | bytes 786440 | tf_op jit(solution)/shard_map/halo_tm1_2/ppermute | solution.py:55
  20.7 2.6 %features.1 = (bf16[8,128,512]{2,1,0:T(8,128)(2,1)S(1)}, bf16[512,1024]{1,0:T(8,128)(2,1)S(1)}) custom-call(s32[23]{0:T(128)S(1)} %pad_add_fusion.meta, bf16[8,128,512]{2,1,0:T(8,128)(2,1)S(1)} %bitcast.25), custom_call_target="tpu_custom_call" | custom-call | flops 20000000000 | bytes 1000 | tf_op jit(solution)/shard_map/features/pallas_call | solution.py:311
  23.3 3.5 %backward.1 = (f32[8,128,512]{2,1,0:T(8,128)S(1)}, bf16[10,128,512]{2,1,0:T(8,128)(2,1)S(1)}, f32[2,3,64,512]{3,2,1,0:T(8,128)S(1)}, f32[2,3,64,512]{3,2,1,0:T(8...) custom-call(s32[23]{0:T(128)S(1)} %pad_add_fusion.meta, ...), custom_call_target="tpu_custom_call" | custom-call | flops 1000000 | bytes 1000 | tf_op jit(solution)/shard_map/backward/pallas_call | solution.py:276
  29.5 0.6 collective-permute-start.19
  30.3 3.6 %forward.1 = (bf16[8,128,512]{2,1,0:T(8,128)(2,1)S(1)}, bf16[2,128,512]{2,1,0:T(8,128)(2,1)S(1)}, f32[2,3,64,512]{3,2,1,0:T(8,128)S(1)}, f32[2,3,64,512]{3,2,1,0...) custom-call(s32[23]{0:T(128)S(1)} %pad_add_fusion.meta, ...), custom_call_target="tpu_custom_call" | custom-call | flops 1000000 | bytes 1000 | tf_op jit(solution)/shard_map/forward/pallas_call | solution.py:276
  33.9 1.3 %collective-permute-start.18 = (bf16[3,64,512]{2,1,0:T(8,128)(2,1)S(1)}, bf16[3,64,512]{2,1,0:T(8,128)(2,1)S(1)}, u32[]{:S(2)}, u32[]{:S(2)}) collective-permute-start(bf16[3,64,512]{2,1,0:T(8,128)(2,1)S(1)} %get-tuple-element.65), channel_id=1, source_target_pairs={{0,4},{4,0},{8,12},{12,8},{16,20},{20,16},{24,28},{28,24},{1,5},{5... | collective-permute-start | bytes 589832 | tf_op jit(solution)/shard_map/grad_down_tm_core/ppermute | solution.py:35
  35.8 1.6 %collective-permute-done.19 = bf16[2,3,64,512]{3,2,1,0:T(8,128)(2,1)S(1)} collective-permute-done((bf16[2,3,64,512]{3,2,1,0:T(8,128)(2,1)S(1)}, bf16[2,3,64,512]{3,2,1,0:T(8,128)(2,1)S(1)}, u32[]{:S(2)}, u32[]{:S(2)}) %collective-permute-start.19) | collective-permute-done | bytes 393248 | tf_op jit(solution)/shard_map/grad_time_tm_0/ppermute | solution.py:30
  37.6 2.1 %collective-permute-start.24 = (bf16[1,3,64,512]{3,2,1,0:T(8,128)(2,1)S(1)}, bf16[1,3,64,512]{3,2,1,0:T(8,128)(2,1)S(1)}, u32[]{:S(2)}, u32[]{:S(2)}) collective-permute-start(bf16[1,3,64,512]{3,2,1,0:T(8,128)(2,1)S(1)} %slice.102), channel_id=1, source_target_pairs={{0,16},{4,12},{8,24},{12,4},{16,0},{20,28},{24,8},{28,20},{1,17},{... | collective-permute-start | bytes 589832 | tf_op jit(solution)/shard_map/grad_time_tm_1/ppermute | solution.py:30
  40.3 4.4 %clips.1 = bf16[8,128,512]{2,1,0:T(8,128)(2,1)} custom-call(s32[23]{0:T(128)S(1)} %pad_add_fusion.meta, bf16[8,128,512]{2,1,0:T(8,128)(2,1)S(1)} %bitcast.27, f32[8,128,512]{2,1,0:T(8,128)S(1)} %get-tuple-element.78.gh, bf16[10,128,512]{2,1,0:T(8,128)(2,1)S(1)} %get-tuple-element.62.gm, bf16[3,64,512]{2,1,0:T(8,128)(2,1)S(1)} %copy-done.2, ...), custom_call_target="tpu_custom_call" | custom-call | flops 1000000 | bytes 1000 | tf_op jit(solution)/shard_map/clips/pallas_call | solution.py:276
  44.6 0.8 %collective-permute-done.24 = bf16[1,3,64,512]{3,2,1,0:T(8,128)(2,1)S(1)} collective-permute-done((bf16[1,3,64,512]{3,2,1,0:T(8,128)(2,1)S(1)}, bf16[1,3,64,512]{3,2,1,0:T(8,128)(2,1)S(1)}, u32[]{:S(2)}, u32[]{:S(2)}) %collective-permute-start.24) | collective-permute-done | bytes 196640 | tf_op jit(solution)/shard_map/grad_time_tm_1/ppermute | solution.py:30
  45.5 2.4 %collective-permute-done.23 = bf16[2,3,64,512]{3,2,1,0:T(8,128)(2,1)S(1)} collective-permute-done((bf16[2,3,64,512]{3,2,1,0:T(8,128)(2,1)S(1)}, bf16[2,3,64,512]{3,2,1,0:T(8,128)(2,1)S(1)}, u32[]{:S(2)}, u32[]{:S(2)}) %collective-permute-start.23) | collective-permute-done | bytes 393248 | tf_op jit(solution)/shard_map/grad_down_tm_0/ppermute | solution.py:30
  48.3 1.6 %collective-permute-start.27 = (bf16[3,64,512]{2,1,0:T(8,128)(2,1)S(1)}, bf16[3,64,512]{2,1,0:T(8,128)(2,1)S(1)}, u32[]{:S(2)}, u32[]{:S(2)}) collective-permute-start(bf16[3,64,512]{2,1,0:T(8,128)(2,1)S(1)} %fusion.6), channel_id=1, source_target_pairs={{0,1},{1,0},{2,3},{3,2},{4,6},{5,7},{6,4},{7,5},{8,9},{9,8},{10,11... | collective-permute-start | bytes 589832 | tf_op jit(solution)/shard_map/grad_time_group_0/ppermute | solution.py:48
  49.9 4.0 %collective-permute-done.25 = bf16[1,3,64,512]{3,2,1,0:T(8,128)(2,1)S(1)} collective-permute-done((bf16[1,3,64,512]{3,2,1,0:T(8,128)(2,1)S(1)}, bf16[1,3,64,512]{3,2,1,0:T(8,128)(2,1)S(1)}, u32[]{:S(2)}, u32[]{:S(2)}) %collective-permute-start.25) | collective-permute-done | bytes 196640 | tf_op jit(solution)/shard_map/grad_down_tm_1/ppermute | solution.py:30
  53.9 1.6 %collective-permute-start.26 = (bf16[3,64,512]{2,1,0:T(8,128)(2,1)S(1)}, bf16[3,64,512]{2,1,0:T(8,128)(2,1)S(1)}, u32[]{:S(2)}, u32[]{:S(2)}) collective-permute-start(bf16[3,64,512]{2,1,0:T(8,128)(2,1)S(1)} %fusion.7), channel_id=1, source_target_pairs={{0,1},{1,0},{2,3},{3,2},{4,6},{5,7},{6,4},{7,5},{8,9},{9,8},{10,11... | collective-permute-start | bytes 589832 | tf_op jit(solution)/shard_map/grad_down_group_0/ppermute | solution.py:48
  55.9 1.7 %collective-permute-start.28 = (bf16[2,128,512]{2,1,0:T(8,128)(2,1)S(1)}, bf16[2,128,512]{2,1,0:T(8,128)(2,1)S(1)}, u32[]{:S(2)}, u32[]{:S(2)}) collective-permute-start(bf16[2,128,512]{2,1,0:T(8,128)(2,1)S(1)} %get-tuple-element.85), channel_id=1, source_target_pairs={{0,4},{4,8},{8,12},{12,16},{16,20},{20,24},{24,28},{1,5},{5,9},{9,... | collective-permute-start | bytes 786440 | tf_op jit(solution)/shard_map/halo_tm1_2/ppermute | solution.py:55
  57.7 2.7 %collective-permute-start.29 = (bf16[3,64,512]{2,1,0:T(8,128)(2,1)S(1)}, bf16[3,64,512]{2,1,0:T(8,128)(2,1)S(1)}, u32[]{:S(2)}, u32[]{:S(2)}) collective-permute-start(bf16[3,64,512]{2,1,0:T(8,128)(2,1)S(1)} %add_convert_fusion.1), channel_id=1, source_target_pairs={{0,2},{1,3},{2,0},{3,1},{4,5},{5,4},{6,7},{7,6},{8,10},{9,11},{10,... | collective-permute-start | bytes 589832 | tf_op jit(solution)/shard_map/grad_time_group_1/ppermute | solution.py:48
  60.6 2.9 %collective-permute-start.30 = (bf16[3,64,512]{2,1,0:T(8,128)(2,1)S(1)}, bf16[3,64,512]{2,1,0:T(8,128)(2,1)S(1)}, u32[]{:S(2)}, u32[]{:S(2)}) collective-permute-start(bf16[3,64,512]{2,1,0:T(8,128)(2,1)S(1)} %add_convert_fusion), channel_id=1, source_target_pairs={{0,2},{1,3},{2,0},{3,1},{4,5},{5,4},{6,7},{7,6},{8,10},{9,11},{10,... | collective-permute-start | bytes 589832 | tf_op jit(solution)/shard_map/grad_down_group_1/ppermute | solution.py:48
  63.5 2.4 %reduced.1 = bf16[4,128,512]{2,1,0:T(8,128)(2,1)} custom-call(s32[23]{0:T(128)S(1)} %pad_add_fusion.meta, bf16[2,128,512]{2,1,0:T(8,128)(2,1)S(1)} %collective-permute-done.28.before, bf16[8,128,512]{2,1,0:T(8,128)(2,1)S(1)} %get-tuple-element.67.hidden, bf16[3,64,512]{2,1,0:T(8,128)(2,1)S(1)} %copy-done.3, ...), custom_call_target="tpu_custom_call" | custom-call | flops 1000000 | bytes 1000 | tf_op jit(solution)/shard_map/reduced/pallas_call | solution.py:276
  66.0 0.8 %convert_add_fusion.1 = f32[3,64,512]{2,1,0:T(8,128)} fusion(bf16[3,64,512]{2,1,0:T(8,128)(2,1)S(1)} %collective-permute-done.29, bf16[3,64,512]{2,1,0:T(8,128)(2,1)S(1)} %add_convert_fusion.1), kind=kLoop, calls=%fused_computation.18 | loop fusion | flops 294912 | bytes 786432 | tf_op jit(solution)/shard_map/add | solution.py:399
  66.8 3.2 %collective-permute-done.30 = bf16[3,64,512]{2,1,0:T(8,128)(2,1)S(1)} collective-permute-done((bf16[3,64,512]{2,1,0:T(8,128)(2,1)S(1)}, bf16[3,64,512]{2,1,0:T(8,128)(2,1)S(1)}, u32[]{:S(2)}, u32[]{:S(2)}) %collective-permute-start.30) | collective-permute-done | bytes 196640 | tf_op jit(solution)/shard_map/grad_down_group_1/ppermute | solution.py:48
  70.0 0.8 %convert_add_fusion = f32[3,64,512]{2,1,0:T(8,128)} fusion(bf16[3,64,512]{2,1,0:T(8,128)(2,1)S(1)} %collective-permute-done.30, bf16[3,64,512]{2,1,0:T(8,128)(2,1)S(1)} %add_convert_fusion), kind=kLoop, calls=%fused_computation.17 | loop fusion | flops 294912 | bytes 786432 | tf_op jit(solution)/shard_map/add | solution.py:402
  (66 shorter events, 7.3 us)
Async XLA Ops:
  0.6 20.1 %copy-start = (bf16[1,8,128,512]{3,2,1,0:T(8,128)(2,1)S(1)}, bf16[1,8,128,512]{3,2,1,0:T(8,128)(2,1)}, u32[]{:S(2)}) copy-start(bf16[1,8,128,512]{3,2,1,0:T(8,128)(2,1)} %param.5) | copy-start | bytes 3145732
  0.6 9.4 %collective-permute-start.8 = (bf16[3,64,512]{2,1,0:T(8,128)(2,1)}, bf16[3,64,512]{2,1,0:T(8,128)(2,1)S(1)}, u32[]{:S(2)}, u32[]{:S(2)}) collective-permute-start(bf16[3,64,512]{2,1,0:T(8,128)(2,1)} %refs_0_.6), channel_id=1, source_target_pairs={{0,4},{4,0},{8,12},{12,8},{16,20},{20,16},{24,28},{28,24},{1,5},{5... | collective-permute-start | bytes 589832 | tf_op jit(solution)/shard_map/time_tm_core/ppermute | solution.py:35
  1.2 10.6 %collective-permute-start.3 = (bf16[3,64,512]{2,1,0:T(8,128)(2,1)}, bf16[3,64,512]{2,1,0:T(8,128)(2,1)S(1)}, u32[]{:S(2)}, u32[]{:S(2)}) collective-permute-start(bf16[3,64,512]{2,1,0:T(8,128)(2,1)} %refs_0_.6), channel_id=1, source_target_pairs={{0,8},{4,20},{8,0},{12,28},{16,24},{20,4},{24,16},{28,12},{1,9},{5... | collective-permute-start | bytes 589832 | tf_op jit(solution)/shard_map/time_tm_0/ppermute | solution.py:30
  3.7 8.1 %collective-permute-start.2 = (bf16[3,64,512]{2,1,0:T(8,128)(2,1)}, bf16[3,64,512]{2,1,0:T(8,128)(2,1)S(1)}, u32[]{:S(2)}, u32[]{:S(2)}) collective-permute-start(bf16[3,64,512]{2,1,0:T(8,128)(2,1)} %refs_0_.7), channel_id=1, source_target_pairs={{0,8},{4,20},{8,0},{12,28},{16,24},{20,4},{24,16},{28,12},{1,9},{5... | collective-permute-start | bytes 589832 | tf_op jit(solution)/shard_map/down_tm_0/ppermute | solution.py:30
  3.8 10.1 %collective-permute-start.1 = (bf16[3,64,512]{2,1,0:T(8,128)(2,1)}, bf16[3,64,512]{2,1,0:T(8,128)(2,1)S(1)}, u32[]{:S(2)}, u32[]{:S(2)}) collective-permute-start(bf16[3,64,512]{2,1,0:T(8,128)(2,1)} %refs_0_.7), channel_id=1, source_target_pairs={{0,16},{4,12},{8,24},{12,4},{16,0},{20,28},{24,8},{28,20},{1,17},{... | collective-permute-start | bytes 589832 | tf_op jit(solution)/shard_map/down_own_tm_1/ppermute | solution.py:30
  6.8 7.3 %collective-permute-start = (bf16[2,128,512]{2,1,0:T(8,128)(2,1)S(1)}, bf16[2,128,512]{2,1,0:T(8,128)(2,1)S(1)}, u32[]{:S(2)}, u32[]{:S(2)}) collective-permute-start(bf16[2,128,512]{2,1,0:T(8,128)(2,1)S(1)} %slice_bitcast_fusion.1), channel_id=1, source_target_pairs={{4,0},{8,4},{12,8},{16,12},{20,16},{24,20},{28,24},{5,1},{9,5},{13... | collective-permute-start | bytes 786440 | tf_op jit(solution)/shard_map/halo_tm-1_2/ppermute | solution.py:55
  10.1 5.4 %collective-permute-start.5 = (bf16[3,64,512]{2,1,0:T(8,128)(2,1)}, bf16[3,64,512]{2,1,0:T(8,128)(2,1)S(1)}, u32[]{:S(2)}, u32[]{:S(2)}) collective-permute-start(bf16[3,64,512]{2,1,0:T(8,128)(2,1)} %refs_0_.7), channel_id=1, source_target_pairs={{0,4},{4,0},{8,12},{12,8},{16,20},{20,16},{24,28},{28,24},{1,5},{5... | collective-permute-start | bytes 589832 | tf_op jit(solution)/shard_map/down_tm_core/ppermute | solution.py:35
  11.8 8.4 %collective-permute-start.6 = (bf16[3,64,512]{2,1,0:T(8,128)(2,1)S(1)}, bf16[3,64,512]{2,1,0:T(8,128)(2,1)S(1)}, u32[]{:S(2)}, u32[]{:S(2)}) collective-permute-start(bf16[3,64,512]{2,1,0:T(8,128)(2,1)S(1)} %collective-permute-done.2.refs_1_), channel_id=1, source_target_pairs={{0,4},{4,0},{8,12},{12,8},{16,20},{20,16},{24,28},{28,24},{1,5},{5... | collective-permute-start | bytes 589832 | tf_op jit(solution)/shard_map/down_tm_core/ppermute | solution.py:35
  11.8 8.4 %collective-permute-start.4 = (bf16[3,64,512]{2,1,0:T(8,128)(2,1)S(1)}, bf16[3,64,512]{2,1,0:T(8,128)(2,1)S(1)}, u32[]{:S(2)}, u32[]{:S(2)}) collective-permute-start(bf16[3,64,512]{2,1,0:T(8,128)(2,1)S(1)} %collective-permute-done.2.refs_1_), channel_id=1, source_target_pairs={{0,16},{4,12},{8,24},{12,4},{16,0},{20,28},{24,8},{28,20},{1,17},{... | collective-permute-start | bytes 589832 | tf_op jit(solution)/shard_map/down_tm_1/ppermute | solution.py:30
  13.9 3.7 %collective-permute-start.9 = (bf16[3,64,512]{2,1,0:T(8,128)(2,1)S(1)}, bf16[3,64,512]{2,1,0:T(8,128)(2,1)S(1)}, u32[]{:S(2)}, u32[]{:S(2)}) collective-permute-start(bf16[3,64,512]{2,1,0:T(8,128)(2,1)S(1)} %collective-permute-done.3.refs_1_), channel_id=1, source_target_pairs={{0,4},{4,0},{8,12},{12,8},{16,20},{20,16},{24,28},{28,24},{1,5},{5... | collective-permute-start | bytes 589832 | tf_op jit(solution)/shard_map/time_tm_core/ppermute | solution.py:35
  14.1 6.1 %collective-permute-start.7 = (bf16[3,64,512]{2,1,0:T(8,128)(2,1)S(1)}, bf16[3,64,512]{2,1,0:T(8,128)(2,1)S(1)}, u32[]{:S(2)}, u32[]{:S(2)}) collective-permute-start(bf16[3,64,512]{2,1,0:T(8,128)(2,1)S(1)} %collective-permute-done.1.refs_2_), channel_id=1, source_target_pairs={{0,4},{4,0},{8,12},{12,8},{16,20},{20,16},{24,28},{28,24},{1,5},{5... | collective-permute-start | bytes 589832 | tf_op jit(solution)/shard_map/down_tm_core/ppermute | solution.py:35
  15.5 12.1 %collective-permute-start.16 = (bf16[2,3,64,512]{3,2,1,0:T(8,128)(2,1)S(1)}, bf16[2,3,64,512]{3,2,1,0:T(8,128)(2,1)S(1)}, u32[]{:S(2)}, u32[]{:S(2)}) collective-permute-start(bf16[2,3,64,512]{3,2,1,0:T(8,128)(2,1)S(1)} %pad_maximum_fusion), channel_id=1, source_target_pairs={{0,16},{4,12},{8,24},{12,4},{16,0},{20,28},{24,8},{28,20},{1,17},{... | collective-permute-start | bytes 1179656 | tf_op jit(solution)/shard_map/time_tm_1/ppermute | solution.py:30
  17.6 10.3 %collective-permute-start.12 = (bf16[2,128,512]{2,1,0:T(8,128)(2,1)S(1)}, bf16[2,128,512]{2,1,0:T(8,128)(2,1)S(1)}, u32[]{:S(2)}, u32[]{:S(2)}) collective-permute-start(bf16[2,128,512]{2,1,0:T(8,128)(2,1)S(1)} %slice_bitcast_fusion), channel_id=1, source_target_pairs={{0,4},{4,8},{8,12},{12,16},{16,20},{20,24},{24,28},{1,5},{5,9},{9,... | collective-permute-start | bytes 786440 | tf_op jit(solution)/shard_map/halo_tm1_2/ppermute | solution.py:55
  20.2 3.1 %collective-permute-start.10 = (bf16[3,64,512]{2,1,0:T(8,128)(2,1)S(1)}, bf16[3,64,512]{2,1,0:T(8,128)(2,1)S(1)}, u32[]{:S(2)}, u32[]{:S(2)}) collective-permute-start(bf16[3,64,512]{2,1,0:T(8,128)(2,1)S(1)} %collective-permute-done.4.refs_3_), channel_id=1, source_target_pairs={{0,4},{4,0},{8,12},{12,8},{16,20},{20,16},{24,28},{28,24},{1,5},{5... | collective-permute-start | bytes 589832 | tf_op jit(solution)/shard_map/down_tm_core/ppermute | solution.py:35
  26.9 1.5 %collective-permute-start.11 = (bf16[3,64,512]{2,1,0:T(8,128)(2,1)S(1)}, bf16[3,64,512]{2,1,0:T(8,128)(2,1)S(1)}, u32[]{:S(2)}, u32[]{:S(2)}) collective-permute-start(bf16[3,64,512]{2,1,0:T(8,128)(2,1)S(1)} %get-tuple-element.51), channel_id=1, source_target_pairs={{0,4},{4,0},{8,12},{12,8},{16,20},{20,16},{24,28},{28,24},{1,5},{5... | collective-permute-start | bytes 589832 | tf_op jit(solution)/shard_map/grad_time_tm_core/ppermute | solution.py:35
  27.0 1.6 %collective-permute-start.13 = (bf16[3,64,512]{2,1,0:T(8,128)(2,1)S(1)}, bf16[3,64,512]{2,1,0:T(8,128)(2,1)S(1)}, u32[]{:S(2)}, u32[]{:S(2)}) collective-permute-start(bf16[3,64,512]{2,1,0:T(8,128)(2,1)S(1)} %get-tuple-element.55), channel_id=1, source_target_pairs={{0,4},{4,0},{8,12},{12,8},{16,20},{20,16},{24,28},{28,24},{1,5},{5... | collective-permute-start | bytes 589832 | tf_op jit(solution)/shard_map/grad_time_tm_core/ppermute | solution.py:35
  27.4 1.5 %collective-permute-start.14 = (bf16[3,64,512]{2,1,0:T(8,128)(2,1)S(1)}, bf16[3,64,512]{2,1,0:T(8,128)(2,1)S(1)}, u32[]{:S(2)}, u32[]{:S(2)}) collective-permute-start(bf16[3,64,512]{2,1,0:T(8,128)(2,1)S(1)} %get-tuple-element.57), channel_id=1, source_target_pairs={{0,4},{4,0},{8,12},{12,8},{16,20},{20,16},{24,28},{28,24},{1,5},{5... | collective-permute-start | bytes 589832 | tf_op jit(solution)/shard_map/grad_time_tm_core/ppermute | solution.py:35
  27.5 1.7 %collective-permute-start.15 = (bf16[3,64,512]{2,1,0:T(8,128)(2,1)S(1)}, bf16[3,64,512]{2,1,0:T(8,128)(2,1)S(1)}, u32[]{:S(2)}, u32[]{:S(2)}) collective-permute-start(bf16[3,64,512]{2,1,0:T(8,128)(2,1)S(1)} %get-tuple-element.59), channel_id=1, source_target_pairs={{0,4},{4,0},{8,12},{12,8},{16,20},{20,16},{24,28},{28,24},{1,5},{5... | collective-permute-start | bytes 589832 | tf_op jit(solution)/shard_map/grad_time_tm_core/ppermute | solution.py:35
  27.9 2.2 %collective-permute-start.17 = (bf16[2,3,64,512]{3,2,1,0:T(8,128)(2,1)S(1)}, bf16[2,3,64,512]{3,2,1,0:T(8,128)(2,1)S(1)}, u32[]{:S(2)}, u32[]{:S(2)}) collective-permute-start(bf16[2,3,64,512]{3,2,1,0:T(8,128)(2,1)S(1)} %collective-permute-done.16.refs_2_), channel_id=1, source_target_pairs={{0,4},{4,0},{8,12},{12,8},{16,20},{20,16},{24,28},{28,24},{1,5},{5... | collective-permute-start | bytes 1179656 | tf_op jit(solution)/shard_map/time_tm_core/ppermute | solution.py:35
  29.5 7.8 %collective-permute-start.19 = (bf16[2,3,64,512]{3,2,1,0:T(8,128)(2,1)S(1)}, bf16[2,3,64,512]{3,2,1,0:T(8,128)(2,1)S(1)}, u32[]{:S(2)}, u32[]{:S(2)}) collective-permute-start(bf16[2,3,64,512]{3,2,1,0:T(8,128)(2,1)S(1)} %fusion.3), channel_id=1, source_target_pairs={{0,8},{4,20},{8,0},{12,28},{16,24},{20,4},{24,16},{28,12},{1,9},{5... | collective-permute-start | bytes 1179656 | tf_op jit(solution)/shard_map/grad_time_tm_0/ppermute | solution.py:30
  33.9 5.8 %collective-permute-start.18 = (bf16[3,64,512]{2,1,0:T(8,128)(2,1)S(1)}, bf16[3,64,512]{2,1,0:T(8,128)(2,1)S(1)}, u32[]{:S(2)}, u32[]{:S(2)}) collective-permute-start(bf16[3,64,512]{2,1,0:T(8,128)(2,1)S(1)} %get-tuple-element.65), channel_id=1, source_target_pairs={{0,4},{4,0},{8,12},{12,8},{16,20},{20,16},{24,28},{28,24},{1,5},{5... | collective-permute-start | bytes 589832 | tf_op jit(solution)/shard_map/grad_down_tm_core/ppermute | solution.py:35
  35.2 4.5 %collective-permute-start.20 = (bf16[3,64,512]{2,1,0:T(8,128)(2,1)S(1)}, bf16[3,64,512]{2,1,0:T(8,128)(2,1)S(1)}, u32[]{:S(2)}, u32[]{:S(2)}) collective-permute-start(bf16[3,64,512]{2,1,0:T(8,128)(2,1)S(1)} %get-tuple-element.70), channel_id=1, source_target_pairs={{0,4},{4,0},{8,12},{12,8},{16,20},{20,16},{24,28},{28,24},{1,5},{5... | collective-permute-start | bytes 589832 | tf_op jit(solution)/shard_map/grad_down_tm_core/ppermute | solution.py:35
  35.3 4.4 %collective-permute-start.21 = (bf16[3,64,512]{2,1,0:T(8,128)(2,1)S(1)}, bf16[3,64,512]{2,1,0:T(8,128)(2,1)S(1)}, u32[]{:S(2)}, u32[]{:S(2)}) collective-permute-start(bf16[3,64,512]{2,1,0:T(8,128)(2,1)S(1)} %get-tuple-element.72), channel_id=1, source_target_pairs={{0,4},{4,0},{8,12},{12,8},{16,20},{20,16},{24,28},{28,24},{1,5},{5... | collective-permute-start | bytes 589832 | tf_op jit(solution)/shard_map/grad_down_tm_core/ppermute | solution.py:35
  35.7 4.0 %collective-permute-start.22 = (bf16[3,64,512]{2,1,0:T(8,128)(2,1)S(1)}, bf16[3,64,512]{2,1,0:T(8,128)(2,1)S(1)}, u32[]{:S(2)}, u32[]{:S(2)}) collective-permute-start(bf16[3,64,512]{2,1,0:T(8,128)(2,1)S(1)} %get-tuple-element.74), channel_id=1, source_target_pairs={{0,4},{4,0},{8,12},{12,8},{16,20},{20,16},{24,28},{28,24},{1,5},{5... | collective-permute-start | bytes 589832 | tf_op jit(solution)/shard_map/grad_down_tm_core/ppermute | solution.py:35
  37.6 7.8 %collective-permute-start.24 = (bf16[1,3,64,512]{3,2,1,0:T(8,128)(2,1)S(1)}, bf16[1,3,64,512]{3,2,1,0:T(8,128)(2,1)S(1)}, u32[]{:S(2)}, u32[]{:S(2)}) collective-permute-start(bf16[1,3,64,512]{3,2,1,0:T(8,128)(2,1)S(1)} %slice.102), channel_id=1, source_target_pairs={{0,16},{4,12},{8,24},{12,4},{16,0},{20,28},{24,8},{28,20},{1,17},{... | collective-permute-start | bytes 589832 | tf_op jit(solution)/shard_map/grad_time_tm_1/ppermute | solution.py:30
  40.0 7.8 %collective-permute-start.23 = (bf16[2,3,64,512]{3,2,1,0:T(8,128)(2,1)S(1)}, bf16[2,3,64,512]{3,2,1,0:T(8,128)(2,1)S(1)}, u32[]{:S(2)}, u32[]{:S(2)}) collective-permute-start(bf16[2,3,64,512]{3,2,1,0:T(8,128)(2,1)S(1)} %fusion), channel_id=1, source_target_pairs={{0,8},{4,20},{8,0},{12,28},{16,24},{20,4},{24,16},{28,12},{1,9},{5... | collective-permute-start | bytes 1179656 | tf_op jit(solution)/shard_map/grad_down_tm_0/ppermute | solution.py:30
  48.1 5.7 %collective-permute-start.25 = (bf16[1,3,64,512]{3,2,1,0:T(8,128)(2,1)S(1)}, bf16[1,3,64,512]{3,2,1,0:T(8,128)(2,1)S(1)}, u32[]{:S(2)}, u32[]{:S(2)}) collective-permute-start(bf16[1,3,64,512]{3,2,1,0:T(8,128)(2,1)S(1)} %slice.101), channel_id=1, source_target_pairs={{0,16},{4,12},{8,24},{12,4},{16,0},{20,28},{24,8},{28,20},{1,17},{... | collective-permute-start | bytes 589832 | tf_op jit(solution)/shard_map/grad_down_tm_1/ppermute | solution.py:30
  48.3 7.6 %collective-permute-start.27 = (bf16[3,64,512]{2,1,0:T(8,128)(2,1)S(1)}, bf16[3,64,512]{2,1,0:T(8,128)(2,1)S(1)}, u32[]{:S(2)}, u32[]{:S(2)}) collective-permute-start(bf16[3,64,512]{2,1,0:T(8,128)(2,1)S(1)} %fusion.6), channel_id=1, source_target_pairs={{0,1},{1,0},{2,3},{3,2},{4,6},{5,7},{6,4},{7,5},{8,9},{9,8},{10,11... | collective-permute-start | bytes 589832 | tf_op jit(solution)/shard_map/grad_time_group_0/ppermute | solution.py:48
  53.9 6.6 %collective-permute-start.26 = (bf16[3,64,512]{2,1,0:T(8,128)(2,1)S(1)}, bf16[3,64,512]{2,1,0:T(8,128)(2,1)S(1)}, u32[]{:S(2)}, u32[]{:S(2)}) collective-permute-start(bf16[3,64,512]{2,1,0:T(8,128)(2,1)S(1)} %fusion.7), channel_id=1, source_target_pairs={{0,1},{1,0},{2,3},{3,2},{4,6},{5,7},{6,4},{7,5},{8,9},{9,8},{10,11... | collective-permute-start | bytes 589832 | tf_op jit(solution)/shard_map/grad_down_group_0/ppermute | solution.py:48
  55.9 7.6 %collective-permute-start.28 = (bf16[2,128,512]{2,1,0:T(8,128)(2,1)S(1)}, bf16[2,128,512]{2,1,0:T(8,128)(2,1)S(1)}, u32[]{:S(2)}, u32[]{:S(2)}) collective-permute-start(bf16[2,128,512]{2,1,0:T(8,128)(2,1)S(1)} %get-tuple-element.85), channel_id=1, source_target_pairs={{0,4},{4,8},{8,12},{12,16},{16,20},{20,24},{24,28},{1,5},{5,9},{9,... | collective-permute-start | bytes 786440 | tf_op jit(solution)/shard_map/halo_tm1_2/ppermute | solution.py:55
  57.7 8.4 %collective-permute-start.29 = (bf16[3,64,512]{2,1,0:T(8,128)(2,1)S(1)}, bf16[3,64,512]{2,1,0:T(8,128)(2,1)S(1)}, u32[]{:S(2)}, u32[]{:S(2)}) collective-permute-start(bf16[3,64,512]{2,1,0:T(8,128)(2,1)S(1)} %add_convert_fusion.1), channel_id=1, source_target_pairs={{0,2},{1,3},{2,0},{3,1},{4,5},{5,4},{6,7},{7,6},{8,10},{9,11},{10,... | collective-permute-start | bytes 589832 | tf_op jit(solution)/shard_map/grad_time_group_1/ppermute | solution.py:48
  60.6 9.4 %collective-permute-start.30 = (bf16[3,64,512]{2,1,0:T(8,128)(2,1)S(1)}, bf16[3,64,512]{2,1,0:T(8,128)(2,1)S(1)}, u32[]{:S(2)}, u32[]{:S(2)}) collective-permute-start(bf16[3,64,512]{2,1,0:T(8,128)(2,1)S(1)} %add_convert_fusion), channel_id=1, source_target_pairs={{0,2},{1,3},{2,0},{3,1},{4,5},{5,4},{6,7},{7,6},{8,10},{9,11},{10,... | collective-permute-start | bytes 589832 | tf_op jit(solution)/shard_map/grad_down_group_1/ppermute | solution.py:48
  (3 other events, 6.2 us)

commit v4 on v3

--- a/solution.py
+++ b/solution.py
@@ -8,6 +8,8 @@
 from jax.sharding import PartitionSpec as P
 
 EPS = 1e-06
+PARTS = 2
+TAIL = -1
 FEATURES_COST = 20_000_000_000
 VMEM = pl.BlockSpec(memory_space=pltpu.VMEM)
 SMEM = pl.BlockSpec(memory_space=pltpu.SMEM)
@@ -368,40 +370,56 @@
         low_time, high_time = plane_step(low_time, other)
         if step == 0:
             low_down, high_down = core_sum(down_shares, "grad_down", high_time)
+            cuts = [slice(i * rows // PARTS, (i + 1) * rows // PARTS) for i in range(PARTS)]
+            lows = [low_down[:, :, cut] for cut in cuts]
+            highs = [high_down[:, :, cut] for cut in cuts]
             grad_clips = call(
                 clips_kernel,
                 "clips",
-                [after(meta, high_down), x, gh, gm] + time,
+                [after(meta, *highs), x, gh, gm] + time,
                 sds((frames, cells, width)),
                 [full] + [scratch(lot, width)] * 2,
             )
+        earlier = grad_clips
         if step == last - 1:
             other = after(exchange(high_time, last, "grad_time"), grad_clips)
             mine_time = (low_time[0] + other[0].astype(F32)).astype(BF16)
-            other = after(exchange(high_down, step, "grad_down"), mine_time)
-        else:
-            other = after(exchange(high_down, step, "grad_down"), grad_clips)
-        low_down, high_down = plane_step(low_down, other)
-    other = exchange(high_down, last, "grad_down")
-    mine_down = (low_down[0] + other[0].astype(F32)).astype(BF16)
-    before = shifted(after(tail, mine_down), "tm", 1)
+            earlier = mine_time
+        for i in range(PARTS):
+            other = after(exchange(highs[i], step, f"grad_down{i}"), earlier)
+            lows[i], highs[i] = plane_step(lows[i], other)
+            earlier = highs[i]
+    mine = [None] * PARTS
+    for i in range(PARTS):
+        other = after(exchange(highs[i], last, f"grad_down{i}"), earlier)
+        mine[i] = (lows[i][0] + other[0].astype(F32)).astype(BF16)
+        earlier = mine[i]
+    before = shifted(after(tail, mine[TAIL]), "tm", 1)
     steps = len(bits_of(lax.axis_size("group")))
     for step in range(steps):
         if step == steps - 1:
             reduced = call(
                 reduced_kernel,
                 "reduced",
-                [after(meta, mine_down), before, hidden] + down,
+                [after(meta, *mine), before, hidden] + down,
                 sds((half, cells, width)),
                 [full] + [scratch(half * cells, width)] * 3,
             )
-        done = mine_down if step < steps - 1 else reduced
-        grad_time = mine_time.astype(F32) + after(group_exchange(mine_time, step, "grad_time"), done).astype(F32)
+            earlier = reduced
+        grad_time = mine_time.astype(F32) + after(group_exchange(mine_time, step, "grad_time"), earlier).astype(F32)
         if step < steps - 1:
             mine_time = grad_time.astype(BF16)
-        grad_down = mine_down.astype(F32) + after(group_exchange(mine_down, step, "grad_down"), mine_time).astype(F32)
-        if step < steps - 1:
-            mine_down = grad_down.astype(BF16)
+            earlier = mine_time
+        else:
+            earlier = grad_time
+        sums = []
+        for i in range(PARTS):
+            other = after(group_exchange(mine[i], step, f"grad_down{i}"), earlier)
+            sums.append(mine[i].astype(F32) + other.astype(F32))
+            if step < steps - 1:
+                mine[i] = sums[i].astype(BF16)
+                earlier = mine[i]
+    grad_down = jnp.concatenate(sums, axis=1)
     return reduced[None], grad_clips[None], grad_time, grad_down
 
 

time: 71.1 us -> 70.6 us (level)
  waiting for transfers between devices: 14.3 us -> 9.31 us
  starting transfers between devices: 32 us -> 36.3 us
    ppermute x9 -> x11, waiting for transfers between devices: 9.39 us -> 4.63 us  [exchange(): return lax.ppermute(value, 'tm', route)]
    ppermute x9 -> x11, starting transfers between devices: 11.8 us -> 15.7 us  [exchange(): return lax.ppermute(value, 'tm', route)]
    ppermute x4 -> x6, starting transfers between devices: 8.84 us -> 9.69 us  [group_exchange(): return lax.ppermute(value, ('tm', 'group'), route)]
    concatenate x0 -> x1, other arithmetic: none -> 0.77 us  [shards(): grad_down = jnp.concatenate(sums, axis=1)]
    add x1, other arithmetic: 0.8 us -> 0.05 us  [shards(): sums.append(mine[i].astype(F32) + other.astype(F32))]
    ppermute x4 -> x6, waiting for transfers between devices: 3.78 us -> 3.5 us  [group_exchange(): return lax.ppermute(value, ('tm', 'group'), route)]
  transfers between devices with their start and end apart: 31 -> 35, of which waited for: 13 -> 10; matrix products, arithmetic and copies ran while one was open for 8% -> 9% of each run, Pallas kernels for 23% -> 23%
where the time goes in v4:
time: 70.6 us; the launch traced here: 70.3 us
  starting transfers between devices  36.3 us (51%)
  Pallas kernels  16.5 us (23%)
  waiting for transfers between devices  9.31 us (13%)
  other arithmetic  5.01 us (7%)
  local copies, waits for them, and re-layouts  2.19 us (3%)
  between operations  0.94 us (1%)
    ppermute x11, starting transfers between devices, exchange(): return lax.ppermute(value, 'tm', route)  15.7 us
    pallas_call x4, Pallas kernels, call(): pl.pallas_call(kernel, in_specs=[SMEM] + [VMEM] * (len(inputs) - 1), out_...  13.9 us
    ppermute x6, starting transfers between devices, group_exchange(): return lax.ppermute(value, ('tm', 'group'), route)  9.69 us
    ppermute x15, starting transfers between devices, core_swap(): lax.ppermute(value, 'tm', [(i, i ^ 1) for i in range(lax.axis_size('tm'))])  5.82 us
    ppermute x3, starting transfers between devices, shifted(): return lax.ppermute(block, axis, route)  5.16 us
    ppermute x11, waiting for transfers between devices, exchange(): return lax.ppermute(value, 'tm', route)  4.63 us
    ppermute x6, waiting for transfers between devices, group_exchange(): return lax.ppermute(value, ('tm', 'group'), route)  3.5 us
    pallas_call x1, Pallas kernels, shards(): pl.pallas_call(functools.partial(features_kernel, chips=chips, rows=rows)...  2.59 us
  transfers between devices with their start and end apart: 35, of which 10 were waited for; matrix products, arithmetic and copies ran while one was open for 9% of the time, Pallas kernels for 23%

profile of v4, /device:TPU:0, one launch (start us, length us, event | category | flops | bytes accessed | tf_op | source)
XLA Modules:
  0.0 70.3 jit_solution(16638827793829506215)
XLA Ops:
  1.2 2.6 %collective-permute-start.3 = (bf16[3,64,512]{2,1,0:T(8,128)(2,1)}, bf16[3,64,512]{2,1,0:T(8,128)(2,1)S(1)}, u32[]{:S(2)}, u32[]{:S(2)}) collective-permute-start(bf16[3,64,512]{2,1,0:T(8,128)(2,1)} %refs_0_.6), channel_id=1, source_target_pairs={{0,8},{4,20},{8,0},{12,28},{16,24},{20,4},{24,16},{28,12},{1,9},{5... | collective-permute-start | bytes 589832 | tf_op jit(solution)/shard_map/time_tm_0/ppermute | solution.py:32
  3.8 2.0 %collective-permute-start.1 = (bf16[3,64,512]{2,1,0:T(8,128)(2,1)}, bf16[3,64,512]{2,1,0:T(8,128)(2,1)S(1)}, u32[]{:S(2)}, u32[]{:S(2)}) collective-permute-start(bf16[3,64,512]{2,1,0:T(8,128)(2,1)} %refs_0_.7), channel_id=1, source_target_pairs={{0,16},{4,12},{8,24},{12,4},{16,0},{20,28},{24,8},{28,20},{1,17},{... | collective-permute-start | bytes 589832 | tf_op jit(solution)/shard_map/down_own_tm_1/ppermute | solution.py:32
  5.8 1.0 %slice_bitcast_fusion.1 = bf16[2,128,512]{2,1,0:T(8,128)(2,1)S(1)} fusion(bf16[1,4,128,512]{3,2,1,0:T(8,128)(2,1)} %param.9), kind=kLoop, calls=%fused_computation.19 | loop fusion | bytes 524288 | tf_op jit(solution)/shard_map/slice | solution.py:302
  6.8 1.3 %collective-permute-start = (bf16[2,128,512]{2,1,0:T(8,128)(2,1)S(1)}, bf16[2,128,512]{2,1,0:T(8,128)(2,1)S(1)}, u32[]{:S(2)}, u32[]{:S(2)}) collective-permute-start(bf16[2,128,512]{2,1,0:T(8,128)(2,1)S(1)} %slice_bitcast_fusion.1), channel_id=1, source_target_pairs={{4,0},{8,4},{12,8},{16,12},{20,16},{24,20},{28,24},{5,1},{9,5},{13... | collective-permute-start | bytes 786440 | tf_op jit(solution)/shard_map/halo_tm-1_2/ppermute | solution.py:57
  8.1 1.0 %slice_bitcast_fusion = bf16[2,128,512]{2,1,0:T(8,128)(2,1)S(1)} fusion(bf16[1,8,128,512]{3,2,1,0:T(8,128)(2,1)} %param.5), kind=kLoop, calls=%fused_computation.18 | loop fusion | bytes 524288 | tf_op jit(solution)/shard_map/slice | solution.py:307
  9.0 0.8 %reduce-window.8 = s32[8,1]{0,1:T(1,128)S(1)} reduce-window(s32[8,1]{0,1:T(1,128)} %bitcast.44, s32[]{:T(128)} %constant.16.clone.1), window={size=8x1 pad=7_0x0_0}, to_apply=%region_0.0 | reduce-window | flops 56 | bytes 68 | tf_op jit(solution)/shard_map/reduce-window.3
  10.1 1.1 %collective-permute-start.5 = (bf16[3,64,512]{2,1,0:T(8,128)(2,1)}, bf16[3,64,512]{2,1,0:T(8,128)(2,1)S(1)}, u32[]{:S(2)}, u32[]{:S(2)}) collective-permute-start(bf16[3,64,512]{2,1,0:T(8,128)(2,1)} %refs_0_.7), channel_id=1, source_target_pairs={{0,4},{4,0},{8,12},{12,8},{16,20},{20,16},{24,28},{28,24},{1,5},{5... | collective-permute-start | bytes 589832 | tf_op jit(solution)/shard_map/down_tm_core/ppermute | solution.py:37
  11.8 2.1 %collective-permute-start.4 = (bf16[3,64,512]{2,1,0:T(8,128)(2,1)S(1)}, bf16[3,64,512]{2,1,0:T(8,128)(2,1)S(1)}, u32[]{:S(2)}, u32[]{:S(2)}) collective-permute-start(bf16[3,64,512]{2,1,0:T(8,128)(2,1)S(1)} %collective-permute-done.2.refs_1_), channel_id=1, source_target_pairs={{0,16},{4,12},{8,24},{12,4},{16,0},{20,28},{24,8},{28,20},{1,17},{... | collective-permute-start | bytes 589832 | tf_op jit(solution)/shard_map/down_tm_1/ppermute | solution.py:32
  14.5 1.0 %pad_maximum_fusion = bf16[2,3,64,512]{3,2,1,0:T(8,128)(2,1)S(1)} fusion(bf16[1,3,64,512]{3,2,1,0:T(8,128)(2,1)S(1)} %bitcast.33, bf16[1,3,64,512]{3,2,1,0:T(8,128)(2,1)} %bitcast.32), kind=kLoop, calls=%fused_computation.14 | loop fusion | flops 196608 | bytes 786432 | tf_op jit(solution)/shard_map/stack | solution.py:304
  15.5 2.1 %collective-permute-start.16 = (bf16[2,3,64,512]{3,2,1,0:T(8,128)(2,1)S(1)}, bf16[2,3,64,512]{3,2,1,0:T(8,128)(2,1)S(1)}, u32[]{:S(2)}, u32[]{:S(2)}) collective-permute-start(bf16[2,3,64,512]{3,2,1,0:T(8,128)(2,1)S(1)} %pad_maximum_fusion), channel_id=1, source_target_pairs={{0,16},{4,12},{8,24},{12,4},{16,0},{20,28},{24,8},{28,20},{1,17},{... | collective-permute-start | bytes 1179656 | tf_op jit(solution)/shard_map/time_tm_1/ppermute | solution.py:32
  17.6 2.6 %collective-permute-start.12 = (bf16[2,128,512]{2,1,0:T(8,128)(2,1)S(1)}, bf16[2,128,512]{2,1,0:T(8,128)(2,1)S(1)}, u32[]{:S(2)}, u32[]{:S(2)}) collective-permute-start(bf16[2,128,512]{2,1,0:T(8,128)(2,1)S(1)} %slice_bitcast_fusion), channel_id=1, source_target_pairs={{0,4},{4,8},{8,12},{12,16},{16,20},{20,24},{24,28},{1,5},{5,9},{9,... | collective-permute-start | bytes 786440 | tf_op jit(solution)/shard_map/halo_tm1_2/ppermute | solution.py:57
  20.7 2.6 %features.1 = (bf16[8,128,512]{2,1,0:T(8,128)(2,1)S(1)}, bf16[512,1024]{1,0:T(8,128)(2,1)S(1)}) custom-call(s32[23]{0:T(128)S(1)} %pad_add_fusion.meta, bf16[8,128,512]{2,1,0:T(8,128)(2,1)S(1)} %bitcast.27), custom_call_target="tpu_custom_call" | custom-call | flops 20000000000 | bytes 1000 | tf_op jit(solution)/shard_map/features/pallas_call | solution.py:313
  23.3 3.5 %backward.1 = (f32[8,128,512]{2,1,0:T(8,128)S(1)}, bf16[10,128,512]{2,1,0:T(8,128)(2,1)S(1)}, f32[2,3,64,512]{3,2,1,0:T(8,128)S(1)}, f32[2,3,64,512]{3,2,1,0:T(8...) custom-call(s32[23]{0:T(128)S(1)} %pad_add_fusion.meta, ...), custom_call_target="tpu_custom_call" | custom-call | flops 1000000 | bytes 1000 | tf_op jit(solution)/shard_map/backward/pallas_call | solution.py:278
  30.3 3.6 %forward.1 = (bf16[8,128,512]{2,1,0:T(8,128)(2,1)S(1)}, bf16[2,128,512]{2,1,0:T(8,128)(2,1)S(1)}, f32[2,3,64,512]{3,2,1,0:T(8,128)S(1)}, f32[2,3,64,512]{3,2,1,0...) custom-call(s32[23]{0:T(128)S(1)} %pad_add_fusion.meta, ...), custom_call_target="tpu_custom_call" | custom-call | flops 1000000 | bytes 1000 | tf_op jit(solution)/shard_map/forward/pallas_call | solution.py:278
  33.9 1.3 %collective-permute-start.18 = (bf16[3,64,512]{2,1,0:T(8,128)(2,1)S(1)}, bf16[3,64,512]{2,1,0:T(8,128)(2,1)S(1)}, u32[]{:S(2)}, u32[]{:S(2)}) collective-permute-start(bf16[3,64,512]{2,1,0:T(8,128)(2,1)S(1)} %get-tuple-element.70), channel_id=1, source_target_pairs={{0,4},{4,0},{8,12},{12,8},{16,20},{20,16},{24,28},{28,24},{1,5},{5... | collective-permute-start | bytes 589832 | tf_op jit(solution)/shard_map/grad_down_tm_core/ppermute | solution.py:37
  35.8 1.6 %collective-permute-done.19 = bf16[2,3,64,512]{3,2,1,0:T(8,128)(2,1)S(1)} collective-permute-done((bf16[2,3,64,512]{3,2,1,0:T(8,128)(2,1)S(1)}, bf16[2,3,64,512]{3,2,1,0:T(8,128)(2,1)S(1)}, u32[]{:S(2)}, u32[]{:S(2)}) %collective-permute-start.19) | collective-permute-done | bytes 393248 | tf_op jit(solution)/shard_map/grad_time_tm_0/ppermute | solution.py:32
  37.6 2.1 %collective-permute-start.24 = (bf16[1,3,64,512]{3,2,1,0:T(8,128)(2,1)S(1)}, bf16[1,3,64,512]{3,2,1,0:T(8,128)(2,1)S(1)}, u32[]{:S(2)}, u32[]{:S(2)}) collective-permute-start(bf16[1,3,64,512]{3,2,1,0:T(8,128)(2,1)S(1)} %slice.138), channel_id=1, source_target_pairs={{0,16},{4,12},{8,24},{12,4},{16,0},{20,28},{24,8},{28,20},{1,17},{... | collective-permute-start | bytes 589832 | tf_op jit(solution)/shard_map/grad_time_tm_1/ppermute | solution.py:32
  40.5 1.9 %collective-permute-start.23 = (bf16[2,3,32,512]{3,2,1,0:T(8,128)(2,1)S(1)}, bf16[2,3,32,512]{3,2,1,0:T(8,128)(2,1)S(1)}, u32[]{:S(2)}, u32[]{:S(2)}) collective-permute-start(bf16[2,3,32,512]{3,2,1,0:T(8,128)(2,1)S(1)} %get-tuple-element.101), channel_id=1, source_target_pairs={{0,8},{4,20},{8,0},{12,28},{16,24},{20,4},{24,16},{28,12},{1,9},{5... | collective-permute-start | bytes 589832 | tf_op jit(solution)/shard_map/grad_down0_tm_0/ppermute | solution.py:32
  42.4 4.4 %clips.1 = bf16[8,128,512]{2,1,0:T(8,128)(2,1)} custom-call(s32[23]{0:T(128)S(1)} %pad_add_fusion.meta, bf16[8,128,512]{2,1,0:T(8,128)(2,1)S(1)} %bitcast.29, f32[8,128,512]{2,1,0:T(8,128)S(1)} %get-tuple-element.83.gh, bf16[10,128,512]{2,1,0:T(8,128)(2,1)S(1)} %get-tuple-element.67.gm, bf16[3,64,512]{2,1,0:T(8,128)(2,1)S(1)} %copy-done.2, ...), custom_call_target="tpu_custom_call" | custom-call | flops 1000000 | bytes 1000 | tf_op jit(solution)/shard_map/clips/pallas_call | solution.py:278
  46.8 1.6 %collective-permute-start.28 = (bf16[3,64,512]{2,1,0:T(8,128)(2,1)S(1)}, bf16[3,64,512]{2,1,0:T(8,128)(2,1)S(1)}, u32[]{:S(2)}, u32[]{:S(2)}) collective-permute-start(bf16[3,64,512]{2,1,0:T(8,128)(2,1)S(1)} %fusion.4), channel_id=1, source_target_pairs={{0,1},{1,0},{2,3},{3,2},{4,6},{5,7},{6,4},{7,5},{8,9},{9,8},{10,11... | collective-permute-start | bytes 589832 | tf_op jit(solution)/shard_map/grad_time_group_0/ppermute | solution.py:50
  48.5 0.8 %collective-permute-start.25 = (bf16[1,3,32,512]{3,2,1,0:T(8,128)(2,1)S(1)}, bf16[1,3,32,512]{3,2,1,0:T(8,128)(2,1)S(1)}, u32[]{:S(2)}, u32[]{:S(2)}) collective-permute-start(bf16[1,3,32,512]{3,2,1,0:T(8,128)(2,1)S(1)} %slice.140), channel_id=1, source_target_pairs={{0,16},{4,12},{8,24},{12,4},{16,0},{20,28},{24,8},{28,20},{1,17},{... | collective-permute-start | bytes 294920 | tf_op jit(solution)/shard_map/grad_down0_tm_1/ppermute | solution.py:32
  49.4 1.4 %collective-permute-start.29 = (bf16[1,3,32,512]{3,2,1,0:T(8,128)(2,1)S(1)}, bf16[1,3,32,512]{3,2,1,0:T(8,128)(2,1)S(1)}, u32[]{:S(2)}, u32[]{:S(2)}) collective-permute-start(bf16[1,3,32,512]{3,2,1,0:T(8,128)(2,1)S(1)} %slice.139), channel_id=1, source_target_pairs={{0,16},{4,12},{8,24},{12,4},{16,0},{20,28},{24,8},{28,20},{1,17},{... | collective-permute-start | bytes 294920 | tf_op jit(solution)/shard_map/grad_down1_tm_1/ppermute | solution.py:32
  50.8 2.4 %collective-permute-done.25 = bf16[1,3,32,512]{3,2,1,0:T(8,128)(2,1)S(1)} collective-permute-done((bf16[1,3,32,512]{3,2,1,0:T(8,128)(2,1)S(1)}, bf16[1,3,32,512]{3,2,1,0:T(8,128)(2,1)S(1)}, u32[]{:S(2)}, u32[]{:S(2)}) %collective-permute-start.25) | collective-permute-done | bytes 98336 | tf_op jit(solution)/shard_map/grad_down0_tm_1/ppermute | solution.py:32
  53.2 1.3 %collective-permute-start.27 = (bf16[3,32,512]{2,1,0:T(8,128)(2,1)S(1)}, bf16[3,32,512]{2,1,0:T(8,128)(2,1)S(1)}, u32[]{:S(2)}, u32[]{:S(2)}) collective-permute-start(bf16[3,32,512]{2,1,0:T(8,128)(2,1)S(1)} %fusion.7), channel_id=1, source_target_pairs={{0,1},{1,0},{2,3},{3,2},{4,6},{5,7},{6,4},{7,5},{8,9},{9,8},{10,11... | collective-permute-start | bytes 294920 | tf_op jit(solution)/shard_map/grad_down0_group_0/ppermute | solution.py:50
  54.6 1.0 %collective-permute-start.30 = (bf16[3,32,512]{2,1,0:T(8,128)(2,1)S(1)}, bf16[3,32,512]{2,1,0:T(8,128)(2,1)S(1)}, u32[]{:S(2)}, u32[]{:S(2)}) collective-permute-start(bf16[3,32,512]{2,1,0:T(8,128)(2,1)S(1)} %fusion.8), channel_id=1, source_target_pairs={{0,1},{1,0},{2,3},{3,2},{4,6},{5,7},{6,4},{7,5},{8,9},{9,8},{10,11... | collective-permute-start | bytes 294920 | tf_op jit(solution)/shard_map/grad_down1_group_0/ppermute | solution.py:50
  55.6 1.3 %collective-permute-start.31 = (bf16[2,128,512]{2,1,0:T(8,128)(2,1)S(1)}, bf16[2,128,512]{2,1,0:T(8,128)(2,1)S(1)}, u32[]{:S(2)}, u32[]{:S(2)}) collective-permute-start(bf16[2,128,512]{2,1,0:T(8,128)(2,1)S(1)} %get-tuple-element.94), channel_id=1, source_target_pairs={{0,4},{4,8},{8,12},{12,16},{16,20},{20,24},{24,28},{1,5},{5,9},{9,... | collective-permute-start | bytes 786440 | tf_op jit(solution)/shard_map/halo_tm1_2/ppermute | solution.py:57
  57.0 2.7 %collective-permute-start.32 = (bf16[3,64,512]{2,1,0:T(8,128)(2,1)S(1)}, bf16[3,64,512]{2,1,0:T(8,128)(2,1)S(1)}, u32[]{:S(2)}, u32[]{:S(2)}) collective-permute-start(bf16[3,64,512]{2,1,0:T(8,128)(2,1)S(1)} %add_convert_fusion), channel_id=1, source_target_pairs={{0,2},{1,3},{2,0},{3,1},{4,5},{5,4},{6,7},{7,6},{8,10},{9,11},{10,... | collective-permute-start | bytes 589832 | tf_op jit(solution)/shard_map/grad_time_group_1/ppermute | solution.py:50
  60.0 3.0 %collective-permute-start.34 = (bf16[3,32,512]{2,1,0:T(8,128)(2,1)S(1)}, bf16[3,32,512]{2,1,0:T(8,128)(2,1)S(1)}, u32[]{:S(2)}, u32[]{:S(2)}) collective-permute-start(bf16[3,32,512]{2,1,0:T(8,128)(2,1)S(1)} %add_convert_fusion.1), channel_id=1, source_target_pairs={{0,2},{1,3},{2,0},{3,1},{4,5},{5,4},{6,7},{7,6},{8,10},{9,11},{10,... | collective-permute-start | bytes 294920 | tf_op jit(solution)/shard_map/grad_down1_group_1/ppermute | solution.py:50
  63.1 2.4 %reduced.1 = bf16[4,128,512]{2,1,0:T(8,128)(2,1)} custom-call(s32[23]{0:T(128)S(1)} %pad_add_fusion.meta, bf16[2,128,512]{2,1,0:T(8,128)(2,1)S(1)} %collective-permute-done.31.before, bf16[8,128,512]{2,1,0:T(8,128)(2,1)S(1)} %get-tuple-element.72.hidden, bf16[3,64,512]{2,1,0:T(8,128)(2,1)S(1)} %copy-done.3, ...), custom_call_target="tpu_custom_call" | custom-call | flops 1000000 | bytes 1000 | tf_op jit(solution)/shard_map/reduced/pallas_call | solution.py:278
  65.5 0.8 %convert_add_fusion = f32[3,64,512]{2,1,0:T(8,128)} fusion(bf16[3,64,512]{2,1,0:T(8,128)(2,1)S(1)} %collective-permute-done.32, bf16[3,64,512]{2,1,0:T(8,128)(2,1)S(1)} %add_convert_fusion), kind=kLoop, calls=%fused_computation.16 | loop fusion | flops 294912 | bytes 786432 | tf_op jit(solution)/shard_map/add | solution.py:409
  66.8 2.6 %collective-permute-done.33 = bf16[3,32,512]{2,1,0:T(8,128)(2,1)S(1)} collective-permute-done((bf16[3,32,512]{2,1,0:T(8,128)(2,1)S(1)}, bf16[3,32,512]{2,1,0:T(8,128)(2,1)S(1)}, u32[]{:S(2)}, u32[]{:S(2)}) %collective-permute-start.33) | collective-permute-done | bytes 98336 | tf_op jit(solution)/shard_map/grad_down0_group_1/ppermute | solution.py:50
  69.5 0.8 %pad_maximum_fusion.1 = f32[3,64,512]{2,1,0:T(8,128)} fusion(f32[3,32,512]{2,1,0:T(8,128)S(1)} %get-tuple-element.104, f32[3,32,512]{2,1,0:T(8,128)S(1)} %get-tuple-element.105), kind=kLoop, calls=%fused_computation.15 | loop fusion | flops 98304 | bytes 786432 | tf_op jit(solution)/shard_map/concatenate | solution.py:422
  (80 shorter events, 8.9 us)
Async XLA Ops:
  0.6 9.4 %collective-permute-start.8 = (bf16[3,64,512]{2,1,0:T(8,128)(2,1)}, bf16[3,64,512]{2,1,0:T(8,128)(2,1)S(1)}, u32[]{:S(2)}, u32[]{:S(2)}) collective-permute-start(bf16[3,64,512]{2,1,0:T(8,128)(2,1)} %refs_0_.6), channel_id=1, source_target_pairs={{0,4},{4,0},{8,12},{12,8},{16,20},{20,16},{24,28},{28,24},{1,5},{5... | collective-permute-start | bytes 589832 | tf_op jit(solution)/shard_map/time_tm_core/ppermute | solution.py:37
  1.2 10.6 %collective-permute-start.3 = (bf16[3,64,512]{2,1,0:T(8,128)(2,1)}, bf16[3,64,512]{2,1,0:T(8,128)(2,1)S(1)}, u32[]{:S(2)}, u32[]{:S(2)}) collective-permute-start(bf16[3,64,512]{2,1,0:T(8,128)(2,1)} %refs_0_.6), channel_id=1, source_target_pairs={{0,8},{4,20},{8,0},{12,28},{16,24},{20,4},{24,16},{28,12},{1,9},{5... | collective-permute-start | bytes 589832 | tf_op jit(solution)/shard_map/time_tm_0/ppermute | solution.py:32
  3.7 8.1 %collective-permute-start.2 = (bf16[3,64,512]{2,1,0:T(8,128)(2,1)}, bf16[3,64,512]{2,1,0:T(8,128)(2,1)S(1)}, u32[]{:S(2)}, u32[]{:S(2)}) collective-permute-start(bf16[3,64,512]{2,1,0:T(8,128)(2,1)} %refs_0_.7), channel_id=1, source_target_pairs={{0,8},{4,20},{8,0},{12,28},{16,24},{20,4},{24,16},{28,12},{1,9},{5... | collective-permute-start | bytes 589832 | tf_op jit(solution)/shard_map/down_tm_0/ppermute | solution.py:32
  3.8 10.1 %collective-permute-start.1 = (bf16[3,64,512]{2,1,0:T(8,128)(2,1)}, bf16[3,64,512]{2,1,0:T(8,128)(2,1)S(1)}, u32[]{:S(2)}, u32[]{:S(2)}) collective-permute-start(bf16[3,64,512]{2,1,0:T(8,128)(2,1)} %refs_0_.7), channel_id=1, source_target_pairs={{0,16},{4,12},{8,24},{12,4},{16,0},{20,28},{24,8},{28,20},{1,17},{... | collective-permute-start | bytes 589832 | tf_op jit(solution)/shard_map/down_own_tm_1/ppermute | solution.py:32
  6.8 7.3 %collective-permute-start = (bf16[2,128,512]{2,1,0:T(8,128)(2,1)S(1)}, bf16[2,128,512]{2,1,0:T(8,128)(2,1)S(1)}, u32[]{:S(2)}, u32[]{:S(2)}) collective-permute-start(bf16[2,128,512]{2,1,0:T(8,128)(2,1)S(1)} %slice_bitcast_fusion.1), channel_id=1, source_target_pairs={{4,0},{8,4},{12,8},{16,12},{20,16},{24,20},{28,24},{5,1},{9,5},{13... | collective-permute-start | bytes 786440 | tf_op jit(solution)/shard_map/halo_tm-1_2/ppermute | solution.py:57
  10.1 5.4 %collective-permute-start.5 = (bf16[3,64,512]{2,1,0:T(8,128)(2,1)}, bf16[3,64,512]{2,1,0:T(8,128)(2,1)S(1)}, u32[]{:S(2)}, u32[]{:S(2)}) collective-permute-start(bf16[3,64,512]{2,1,0:T(8,128)(2,1)} %refs_0_.7), channel_id=1, source_target_pairs={{0,4},{4,0},{8,12},{12,8},{16,20},{20,16},{24,28},{28,24},{1,5},{5... | collective-permute-start | bytes 589832 | tf_op jit(solution)/shard_map/down_tm_core/ppermute | solution.py:37
  11.8 8.4 %collective-permute-start.6 = (bf16[3,64,512]{2,1,0:T(8,128)(2,1)S(1)}, bf16[3,64,512]{2,1,0:T(8,128)(2,1)S(1)}, u32[]{:S(2)}, u32[]{:S(2)}) collective-permute-start(bf16[3,64,512]{2,1,0:T(8,128)(2,1)S(1)} %collective-permute-done.2.refs_1_), channel_id=1, source_target_pairs={{0,4},{4,0},{8,12},{12,8},{16,20},{20,16},{24,28},{28,24},{1,5},{5... | collective-permute-start | bytes 589832 | tf_op jit(solution)/shard_map/down_tm_core/ppermute | solution.py:37
  11.8 8.4 %collective-permute-start.4 = (bf16[3,64,512]{2,1,0:T(8,128)(2,1)S(1)}, bf16[3,64,512]{2,1,0:T(8,128)(2,1)S(1)}, u32[]{:S(2)}, u32[]{:S(2)}) collective-permute-start(bf16[3,64,512]{2,1,0:T(8,128)(2,1)S(1)} %collective-permute-done.2.refs_1_), channel_id=1, source_target_pairs={{0,16},{4,12},{8,24},{12,4},{16,0},{20,28},{24,8},{28,20},{1,17},{... | collective-permute-start | bytes 589832 | tf_op jit(solution)/shard_map/down_tm_1/ppermute | solution.py:32
  13.9 3.7 %collective-permute-start.9 = (bf16[3,64,512]{2,1,0:T(8,128)(2,1)S(1)}, bf16[3,64,512]{2,1,0:T(8,128)(2,1)S(1)}, u32[]{:S(2)}, u32[]{:S(2)}) collective-permute-start(bf16[3,64,512]{2,1,0:T(8,128)(2,1)S(1)} %collective-permute-done.3.refs_1_), channel_id=1, source_target_pairs={{0,4},{4,0},{8,12},{12,8},{16,20},{20,16},{24,28},{28,24},{1,5},{5... | collective-permute-start | bytes 589832 | tf_op jit(solution)/shard_map/time_tm_core/ppermute | solution.py:37
  14.1 6.1 %collective-permute-start.7 = (bf16[3,64,512]{2,1,0:T(8,128)(2,1)S(1)}, bf16[3,64,512]{2,1,0:T(8,128)(2,1)S(1)}, u32[]{:S(2)}, u32[]{:S(2)}) collective-permute-start(bf16[3,64,512]{2,1,0:T(8,128)(2,1)S(1)} %collective-permute-done.1.refs_2_), channel_id=1, source_target_pairs={{0,4},{4,0},{8,12},{12,8},{16,20},{20,16},{24,28},{28,24},{1,5},{5... | collective-permute-start | bytes 589832 | tf_op jit(solution)/shard_map/down_tm_core/ppermute | solution.py:37
  15.5 12.1 %collective-permute-start.16 = (bf16[2,3,64,512]{3,2,1,0:T(8,128)(2,1)S(1)}, bf16[2,3,64,512]{3,2,1,0:T(8,128)(2,1)S(1)}, u32[]{:S(2)}, u32[]{:S(2)}) collective-permute-start(bf16[2,3,64,512]{3,2,1,0:T(8,128)(2,1)S(1)} %pad_maximum_fusion), channel_id=1, source_target_pairs={{0,16},{4,12},{8,24},{12,4},{16,0},{20,28},{24,8},{28,20},{1,17},{... | collective-permute-start | bytes 1179656 | tf_op jit(solution)/shard_map/time_tm_1/ppermute | solution.py:32
  17.6 10.3 %collective-permute-start.12 = (bf16[2,128,512]{2,1,0:T(8,128)(2,1)S(1)}, bf16[2,128,512]{2,1,0:T(8,128)(2,1)S(1)}, u32[]{:S(2)}, u32[]{:S(2)}) collective-permute-start(bf16[2,128,512]{2,1,0:T(8,128)(2,1)S(1)} %slice_bitcast_fusion), channel_id=1, source_target_pairs={{0,4},{4,8},{8,12},{12,16},{16,20},{20,24},{24,28},{1,5},{5,9},{9,... | collective-permute-start | bytes 786440 | tf_op jit(solution)/shard_map/halo_tm1_2/ppermute | solution.py:57
  20.2 3.1 %collective-permute-start.10 = (bf16[3,64,512]{2,1,0:T(8,128)(2,1)S(1)}, bf16[3,64,512]{2,1,0:T(8,128)(2,1)S(1)}, u32[]{:S(2)}, u32[]{:S(2)}) collective-permute-start(bf16[3,64,512]{2,1,0:T(8,128)(2,1)S(1)} %collective-permute-done.4.refs_3_), channel_id=1, source_target_pairs={{0,4},{4,0},{8,12},{12,8},{16,20},{20,16},{24,28},{28,24},{1,5},{5... | collective-permute-start | bytes 589832 | tf_op jit(solution)/shard_map/down_tm_core/ppermute | solution.py:37
  27.5 1.7 %collective-permute-start.15 = (bf16[3,64,512]{2,1,0:T(8,128)(2,1)S(1)}, bf16[3,64,512]{2,1,0:T(8,128)(2,1)S(1)}, u32[]{:S(2)}, u32[]{:S(2)}) collective-permute-start(bf16[3,64,512]{2,1,0:T(8,128)(2,1)S(1)} %get-tuple-element.64), channel_id=1, source_target_pairs={{0,4},{4,0},{8,12},{12,8},{16,20},{20,16},{24,28},{28,24},{1,5},{5... | collective-permute-start | bytes 589832 | tf_op jit(solution)/shard_map/grad_time_tm_core/ppermute | solution.py:37
  27.9 2.2 %collective-permute-start.17 = (bf16[2,3,64,512]{3,2,1,0:T(8,128)(2,1)S(1)}, bf16[2,3,64,512]{3,2,1,0:T(8,128)(2,1)S(1)}, u32[]{:S(2)}, u32[]{:S(2)}) collective-permute-start(bf16[2,3,64,512]{3,2,1,0:T(8,128)(2,1)S(1)} %collective-permute-done.16.refs_2_), channel_id=1, source_target_pairs={{0,4},{4,0},{8,12},{12,8},{16,20},{20,16},{24,28},{28,24},{1,5},{5... | collective-permute-start | bytes 1179656 | tf_op jit(solution)/shard_map/time_tm_core/ppermute | solution.py:37
  29.5 7.8 %collective-permute-start.19 = (bf16[2,3,64,512]{3,2,1,0:T(8,128)(2,1)S(1)}, bf16[2,3,64,512]{3,2,1,0:T(8,128)(2,1)S(1)}, u32[]{:S(2)}, u32[]{:S(2)}) collective-permute-start(bf16[2,3,64,512]{3,2,1,0:T(8,128)(2,1)S(1)} %fusion.2), channel_id=1, source_target_pairs={{0,8},{4,20},{8,0},{12,28},{16,24},{20,4},{24,16},{28,12},{1,9},{5... | collective-permute-start | bytes 1179656 | tf_op jit(solution)/shard_map/grad_time_tm_0/ppermute | solution.py:32
  33.9 5.8 %collective-permute-start.18 = (bf16[3,64,512]{2,1,0:T(8,128)(2,1)S(1)}, bf16[3,64,512]{2,1,0:T(8,128)(2,1)S(1)}, u32[]{:S(2)}, u32[]{:S(2)}) collective-permute-start(bf16[3,64,512]{2,1,0:T(8,128)(2,1)S(1)} %get-tuple-element.70), channel_id=1, source_target_pairs={{0,4},{4,0},{8,12},{12,8},{16,20},{20,16},{24,28},{28,24},{1,5},{5... | collective-permute-start | bytes 589832 | tf_op jit(solution)/shard_map/grad_down_tm_core/ppermute | solution.py:37
  35.2 4.5 %collective-permute-start.20 = (bf16[3,64,512]{2,1,0:T(8,128)(2,1)S(1)}, bf16[3,64,512]{2,1,0:T(8,128)(2,1)S(1)}, u32[]{:S(2)}, u32[]{:S(2)}) collective-permute-start(bf16[3,64,512]{2,1,0:T(8,128)(2,1)S(1)} %get-tuple-element.75), channel_id=1, source_target_pairs={{0,4},{4,0},{8,12},{12,8},{16,20},{20,16},{24,28},{28,24},{1,5},{5... | collective-permute-start | bytes 589832 | tf_op jit(solution)/shard_map/grad_down_tm_core/ppermute | solution.py:37
  35.3 4.4 %collective-permute-start.21 = (bf16[3,64,512]{2,1,0:T(8,128)(2,1)S(1)}, bf16[3,64,512]{2,1,0:T(8,128)(2,1)S(1)}, u32[]{:S(2)}, u32[]{:S(2)}) collective-permute-start(bf16[3,64,512]{2,1,0:T(8,128)(2,1)S(1)} %get-tuple-element.77), channel_id=1, source_target_pairs={{0,4},{4,0},{8,12},{12,8},{16,20},{20,16},{24,28},{28,24},{1,5},{5... | collective-permute-start | bytes 589832 | tf_op jit(solution)/shard_map/grad_down_tm_core/ppermute | solution.py:37
  35.7 4.0 %collective-permute-start.22 = (bf16[3,64,512]{2,1,0:T(8,128)(2,1)S(1)}, bf16[3,64,512]{2,1,0:T(8,128)(2,1)S(1)}, u32[]{:S(2)}, u32[]{:S(2)}) collective-permute-start(bf16[3,64,512]{2,1,0:T(8,128)(2,1)S(1)} %get-tuple-element.79), channel_id=1, source_target_pairs={{0,4},{4,0},{8,12},{12,8},{16,20},{20,16},{24,28},{28,24},{1,5},{5... | collective-permute-start | bytes 589832 | tf_op jit(solution)/shard_map/grad_down_tm_core/ppermute | solution.py:37
  37.6 9.1 %collective-permute-start.24 = (bf16[1,3,64,512]{3,2,1,0:T(8,128)(2,1)S(1)}, bf16[1,3,64,512]{3,2,1,0:T(8,128)(2,1)S(1)}, u32[]{:S(2)}, u32[]{:S(2)}) collective-permute-start(bf16[1,3,64,512]{3,2,1,0:T(8,128)(2,1)S(1)} %slice.138), channel_id=1, source_target_pairs={{0,16},{4,12},{8,24},{12,4},{16,0},{20,28},{24,8},{28,20},{1,17},{... | collective-permute-start | bytes 589832 | tf_op jit(solution)/shard_map/grad_time_tm_1/ppermute | solution.py:32
  40.3 9.0 %collective-permute-start.26 = (bf16[2,3,32,512]{3,2,1,0:T(8,128)(2,1)S(1)}, bf16[2,3,32,512]{3,2,1,0:T(8,128)(2,1)S(1)}, u32[]{:S(2)}, u32[]{:S(2)}) collective-permute-start(bf16[2,3,32,512]{3,2,1,0:T(8,128)(2,1)S(1)} %get-tuple-element.100), channel_id=1, source_target_pairs={{0,8},{4,20},{8,0},{12,28},{16,24},{20,4},{24,16},{28,12},{1,9},{5... | collective-permute-start | bytes 589832 | tf_op jit(solution)/shard_map/grad_down1_tm_0/ppermute | solution.py:32
  40.5 7.9 %collective-permute-start.23 = (bf16[2,3,32,512]{3,2,1,0:T(8,128)(2,1)S(1)}, bf16[2,3,32,512]{3,2,1,0:T(8,128)(2,1)S(1)}, u32[]{:S(2)}, u32[]{:S(2)}) collective-permute-start(bf16[2,3,32,512]{3,2,1,0:T(8,128)(2,1)S(1)} %get-tuple-element.101), channel_id=1, source_target_pairs={{0,8},{4,20},{8,0},{12,28},{16,24},{20,4},{24,16},{28,12},{1,9},{5... | collective-permute-start | bytes 589832 | tf_op jit(solution)/shard_map/grad_down0_tm_0/ppermute | solution.py:32
  46.8 10.1 %collective-permute-start.28 = (bf16[3,64,512]{2,1,0:T(8,128)(2,1)S(1)}, bf16[3,64,512]{2,1,0:T(8,128)(2,1)S(1)}, u32[]{:S(2)}, u32[]{:S(2)}) collective-permute-start(bf16[3,64,512]{2,1,0:T(8,128)(2,1)S(1)} %fusion.4), channel_id=1, source_target_pairs={{0,1},{1,0},{2,3},{3,2},{4,6},{5,7},{6,4},{7,5},{8,9},{9,8},{10,11... | collective-permute-start | bytes 589832 | tf_op jit(solution)/shard_map/grad_time_group_0/ppermute | solution.py:50
  48.5 4.7 %collective-permute-start.25 = (bf16[1,3,32,512]{3,2,1,0:T(8,128)(2,1)S(1)}, bf16[1,3,32,512]{3,2,1,0:T(8,128)(2,1)S(1)}, u32[]{:S(2)}, u32[]{:S(2)}) collective-permute-start(bf16[1,3,32,512]{3,2,1,0:T(8,128)(2,1)S(1)} %slice.140), channel_id=1, source_target_pairs={{0,16},{4,12},{8,24},{12,4},{16,0},{20,28},{24,8},{28,20},{1,17},{... | collective-permute-start | bytes 294920 | tf_op jit(solution)/shard_map/grad_down0_tm_1/ppermute | solution.py:32
  49.4 5.2 %collective-permute-start.29 = (bf16[1,3,32,512]{3,2,1,0:T(8,128)(2,1)S(1)}, bf16[1,3,32,512]{3,2,1,0:T(8,128)(2,1)S(1)}, u32[]{:S(2)}, u32[]{:S(2)}) collective-permute-start(bf16[1,3,32,512]{3,2,1,0:T(8,128)(2,1)S(1)} %slice.139), channel_id=1, source_target_pairs={{0,16},{4,12},{8,24},{12,4},{16,0},{20,28},{24,8},{28,20},{1,17},{... | collective-permute-start | bytes 294920 | tf_op jit(solution)/shard_map/grad_down1_tm_1/ppermute | solution.py:32
  53.2 6.4 %collective-permute-start.27 = (bf16[3,32,512]{2,1,0:T(8,128)(2,1)S(1)}, bf16[3,32,512]{2,1,0:T(8,128)(2,1)S(1)}, u32[]{:S(2)}, u32[]{:S(2)}) collective-permute-start(bf16[3,32,512]{2,1,0:T(8,128)(2,1)S(1)} %fusion.7), channel_id=1, source_target_pairs={{0,1},{1,0},{2,3},{3,2},{4,6},{5,7},{6,4},{7,5},{8,9},{9,8},{10,11... | collective-permute-start | bytes 294920 | tf_op jit(solution)/shard_map/grad_down0_group_0/ppermute | solution.py:50
  54.6 5.4 %collective-permute-start.30 = (bf16[3,32,512]{2,1,0:T(8,128)(2,1)S(1)}, bf16[3,32,512]{2,1,0:T(8,128)(2,1)S(1)}, u32[]{:S(2)}, u32[]{:S(2)}) collective-permute-start(bf16[3,32,512]{2,1,0:T(8,128)(2,1)S(1)} %fusion.8), channel_id=1, source_target_pairs={{0,1},{1,0},{2,3},{3,2},{4,6},{5,7},{6,4},{7,5},{8,9},{9,8},{10,11... | collective-permute-start | bytes 294920 | tf_op jit(solution)/shard_map/grad_down1_group_0/ppermute | solution.py:50
  55.6 7.5 %collective-permute-start.31 = (bf16[2,128,512]{2,1,0:T(8,128)(2,1)S(1)}, bf16[2,128,512]{2,1,0:T(8,128)(2,1)S(1)}, u32[]{:S(2)}, u32[]{:S(2)}) collective-permute-start(bf16[2,128,512]{2,1,0:T(8,128)(2,1)S(1)} %get-tuple-element.94), channel_id=1, source_target_pairs={{0,4},{4,8},{8,12},{12,16},{16,20},{20,24},{24,28},{1,5},{5,9},{9,... | collective-permute-start | bytes 786440 | tf_op jit(solution)/shard_map/halo_tm1_2/ppermute | solution.py:57
  57.0 8.5 %collective-permute-start.32 = (bf16[3,64,512]{2,1,0:T(8,128)(2,1)S(1)}, bf16[3,64,512]{2,1,0:T(8,128)(2,1)S(1)}, u32[]{:S(2)}, u32[]{:S(2)}) collective-permute-start(bf16[3,64,512]{2,1,0:T(8,128)(2,1)S(1)} %add_convert_fusion), channel_id=1, source_target_pairs={{0,2},{1,3},{2,0},{3,1},{4,5},{5,4},{6,7},{7,6},{8,10},{9,11},{10,... | collective-permute-start | bytes 589832 | tf_op jit(solution)/shard_map/grad_time_group_1/ppermute | solution.py:50
  60.0 6.8 %collective-permute-start.34 = (bf16[3,32,512]{2,1,0:T(8,128)(2,1)S(1)}, bf16[3,32,512]{2,1,0:T(8,128)(2,1)S(1)}, u32[]{:S(2)}, u32[]{:S(2)}) collective-permute-start(bf16[3,32,512]{2,1,0:T(8,128)(2,1)S(1)} %add_convert_fusion.1), channel_id=1, source_target_pairs={{0,2},{1,3},{2,0},{3,1},{4,5},{5,4},{6,7},{7,6},{8,10},{9,11},{10,... | collective-permute-start | bytes 294920 | tf_op jit(solution)/shard_map/grad_down1_group_1/ppermute | solution.py:50
  63.0 6.5 %collective-permute-start.33 = (bf16[3,32,512]{2,1,0:T(8,128)(2,1)S(1)}, bf16[3,32,512]{2,1,0:T(8,128)(2,1)S(1)}, u32[]{:S(2)}, u32[]{:S(2)}) collective-permute-start(bf16[3,32,512]{2,1,0:T(8,128)(2,1)S(1)} %add_convert_fusion.2), channel_id=1, source_target_pairs={{0,2},{1,3},{2,0},{3,1},{4,5},{5,4},{6,7},{7,6},{8,10},{9,11},{10,... | collective-permute-start | bytes 294920 | tf_op jit(solution)/shard_map/grad_down0_group_1/ppermute | solution.py:50
  (7 other events, 30.8 us)

commit v5 on v4

--- a/solution.py
+++ b/solution.py
@@ -132,10 +132,12 @@
 
 
 def features_kernel(meta, clips, h_out, ht_out, flip, *, chips, rows):
-    h = features(clips[0])
-    h_out[0] = h
-    flip[...] = h.T
-    place_rows(meta, chips, rows, flip, ht_out, slice(None))
+    cells = clips.shape[1]
+    for i in range(clips.shape[0]):
+        h = features(clips[i])
+        h_out[i] = h
+        flip[...] = h.T
+        place_rows(meta, chips, rows, flip, ht_out, slice(i * cells, (i + 1) * cells))
 
 
 def backward_kernel(meta, cot, cot_next, ht, *refs, chips):
@@ -273,7 +275,7 @@
     def scratch(*shape):
         return pltpu.VMEM(shape, BF16)
 
-    def call(kernel, name, inputs, outs, scratches):
+    def call(kernel, name, inputs, outs, scratches, flops=1_000_000):
         tree = (VMEM,) * len(outs) if isinstance(outs, tuple) else VMEM
         return pl.pallas_call(
             kernel,
@@ -282,11 +284,12 @@
             out_shape=outs,
             scratch_shapes=scratches,
             compiler_params=pltpu.CompilerParams(vmem_limit_bytes=36 * 1024 * 1024),
-            cost_estimate=pl.CostEstimate(flops=1_000_000, bytes_accessed=1000, transcendentals=0),
+            cost_estimate=pl.CostEstimate(flops=flops, bytes_accessed=1000, transcendentals=0),
             name=name,
         )(*inputs)
 
-    ends = jnp.cumsum(lengths[0])
+    clips_up_to = jnp.tri(lengths.shape[1], dtype=jnp.int32)
+    ends = jnp.sum(clips_up_to * lengths, axis=1)
     local = me * frames + jnp.arange(-2, frames + 3, dtype=jnp.int32)
     clip = jnp.sum((ends[None, :] <= local[:, None]).astype(jnp.int32), axis=1)
     clip = jnp.where(local < 0, -1, clip)
@@ -301,7 +304,9 @@
     down_own = exchange(w_down, last, "down_own")
     cot_next = shifted(cot[:2], "tm", -1)
     down_late = [exchange(part, last, "down") for part in down[1:]]
-    time_late = jnp.stack(time)
+    time_late = after(jnp.pad(w_time[None], ((0, early - 1), (0, 0), (0, 0), (0, 0))), down_own)
+    for i in range(1, early):
+        time_late = lax.dynamic_update_slice(time_late, time[i][None], (i, 0, 0, 0))
     first = [cot_next, down_own] + down[1:] + time[1:]
     time_late = after(time_late, cot_next, *down)
     x_before = shifted(after(x[frames - 2:], time_late), "tm", 1)
@@ -310,20 +315,14 @@
     down_other = [core_swap(part, "down") for part in down]
     time_other = [core_swap(part, "time") for part in time]
 
-    h, ht = pl.pallas_call(
+    h, ht = call(
         functools.partial(features_kernel, chips=chips, rows=rows),
-        grid=(frames,),
-        in_specs=[SMEM, pl.BlockSpec((1, cells, width), lambda f: (f, 0, 0))],
-        out_specs=(
-            pl.BlockSpec((1, cells, width), lambda f: (f, 0, 0)),
-            pl.BlockSpec((width, cells), lambda f: (0, f)),
-        ),
-        out_shape=(sds((frames, cells, width)), sds((width, lot))),
-        scratch_shapes=[scratch(width, cells)],
-        compiler_params=pltpu.CompilerParams(vmem_limit_bytes=36 * 1024 * 1024),
-        cost_estimate=pl.CostEstimate(flops=FEATURES_COST, bytes_accessed=1000, transcendentals=0),
-        name="features",
-    )(after(meta, *first, *down_late, *down_other, *time_other), x)
+        "features",
+        [after(meta, *first, *down_late, *down_other, *time_other), x],
+        (sds((frames, cells, width)), sds((width, lot))),
+        [scratch(width, cells)],
+        FEATURES_COST,
+    )
 
     down = down + down_late + down_other + [after(core_swap(part, "down"), h) for part in down_late]
 

time: 70.6 us -> 68.3 us (0.967)
  starting transfers between devices: 36.3 us -> 34.6 us
  Pallas kernels: 16.5 us -> 15.4 us
  other arithmetic: 5.01 us -> 3.99 us
  local copies, waits for them, and re-layouts: 2.19 us -> 3.15 us
    pallas_call x1 -> x0, Pallas kernels: 2.59 us -> none  [shards(): pl.pallas_call(functools.partial(features_kernel, chips=chips, rows=rows)...]
    another operation x2 -> x0, other arithmetic: 1.8 us -> none  [the longest x1 0.97 us: shards(): time_late = jnp.stack(time)]
    pallas_call x4 -> x5, Pallas kernels: 13.9 us -> 15.4 us  [call(): pl.pallas_call(kernel, in_specs=[SMEM] + [VMEM] * (len(inputs) - 1), out_...]
    ppermute x11, starting transfers between devices: 15.7 us -> 14.2 us  [exchange(): return lax.ppermute(value, 'tm', route)]
    pad x0 -> x1, local copies, waits for them, and re-layouts: none -> 0.96 us  [shards(): jnp.pad(w_time[None], ((0, early - 1), (0, 0), (0, 0), (0, 0)))]
    reduce_sum x0 -> x1, other arithmetic: none -> 0.77 us  [shards(): ends = jnp.sum(clips_up_to * lengths, axis=1)]
    ppermute x11, waiting for transfers between devices: 4.63 us -> 5.4 us  [exchange(): return lax.ppermute(value, 'tm', route)]
where the time goes in v5:
time: 68.3 us; the launch traced here: 68 us
  starting transfers between devices  34.6 us (51%)
  Pallas kernels  15.4 us (23%)
  waiting for transfers between devices  9.92 us (15%)
  other arithmetic  3.99 us (6%)
  local copies, waits for them, and re-layouts  3.15 us (5%)
  between operations  0.94 us (1%)
    pallas_call x5, Pallas kernels, call(): pl.pallas_call(kernel, in_specs=[SMEM] + [VMEM] * (len(inputs) - 1), out_...  15.4 us
    ppermute x11, starting transfers between devices, exchange(): return lax.ppermute(value, 'tm', route)  14.2 us
    ppermute x6, starting transfers between devices, group_exchange(): return lax.ppermute(value, ('tm', 'group'), route)  9.49 us
    ppermute x15, starting transfers between devices, core_swap(): lax.ppermute(value, 'tm', [(i, i ^ 1) for i in range(lax.axis_size('tm'))])  5.51 us
    ppermute x3, starting transfers between devices, shifted(): return lax.ppermute(block, axis, route)  5.42 us
    ppermute x11, waiting for transfers between devices, exchange(): return lax.ppermute(value, 'tm', route)  5.4 us
    ppermute x6, waiting for transfers between devices, group_exchange(): return lax.ppermute(value, ('tm', 'group'), route)  3.31 us
  transfers between devices with their start and end apart: 35, of which 10 were waited for; matrix products, arithmetic and copies ran while one was open for 9% of the time, Pallas kernels for 23%

profile of v5, /device:TPU:0, one launch (start us, length us, event | category | flops | bytes accessed | tf_op | source)
XLA Modules:
  0.0 68.0 jit_solution(7043440673058398628)
XLA Ops:
  1.2 2.6 %collective-permute-start.3 = (bf16[3,64,512]{2,1,0:T(8,128)(2,1)}, bf16[3,64,512]{2,1,0:T(8,128)(2,1)S(1)}, u32[]{:S(2)}, u32[]{:S(2)}) collective-permute-start(bf16[3,64,512]{2,1,0:T(8,128)(2,1)} %refs_0_.6), channel_id=1, source_target_pairs={{0,8},{4,20},{8,0},{12,28},{16,24},{20,4},{24,16},{28,12},{1,9},{5... | collective-permute-start | bytes 589832 | tf_op jit(solution)/shard_map/time_tm_0/ppermute | solution.py:32
  3.8 2.0 %collective-permute-start.1 = (bf16[3,64,512]{2,1,0:T(8,128)(2,1)}, bf16[3,64,512]{2,1,0:T(8,128)(2,1)S(1)}, u32[]{:S(2)}, u32[]{:S(2)}) collective-permute-start(bf16[3,64,512]{2,1,0:T(8,128)(2,1)} %refs_0_.7), channel_id=1, source_target_pairs={{0,16},{4,12},{8,24},{12,4},{16,0},{20,28},{24,8},{28,20},{1,17},{... | collective-permute-start | bytes 589832 | tf_op jit(solution)/shard_map/down_own_tm_1/ppermute | solution.py:32
  5.8 1.0 %slice_bitcast_fusion.1 = bf16[2,128,512]{2,1,0:T(8,128)(2,1)S(1)} fusion(bf16[1,4,128,512]{3,2,1,0:T(8,128)(2,1)} %param.9), kind=kLoop, calls=%fused_computation.18 | loop fusion | bytes 524288 | tf_op jit(solution)/shard_map/slice | solution.py:305
  6.8 1.3 %collective-permute-start = (bf16[2,128,512]{2,1,0:T(8,128)(2,1)S(1)}, bf16[2,128,512]{2,1,0:T(8,128)(2,1)S(1)}, u32[]{:S(2)}, u32[]{:S(2)}) collective-permute-start(bf16[2,128,512]{2,1,0:T(8,128)(2,1)S(1)} %slice_bitcast_fusion.1), channel_id=1, source_target_pairs={{4,0},{8,4},{12,8},{16,12},{20,16},{24,20},{28,24},{5,1},{9,5},{13... | collective-permute-start | bytes 786440 | tf_op jit(solution)/shard_map/halo_tm-1_2/ppermute | solution.py:57
  8.1 0.8 %select_reduce_fusion = s32[8]{0:T(128)S(1)} fusion(s32[8]{0:T(128)} %bitcast.43), kind=kLoop, calls=%fused_computation.34 | loop fusion | flops 184 | bytes 64 | tf_op jit(solution)/shard_map/reduce_sum | solution.py:292
  9.1 1.0 %pad.4 = bf16[2,3,64,512]{3,2,1,0:T(8,128)(2,1)S(1)} pad(bf16[1,3,64,512]{3,2,1,0:T(8,128)(2,1)} %bitcast.32, bf16[]{:T(256)} %constant.18.clone.1), padding=0_1x0_0x0_0x0_0 | pad | bytes 589826 | tf_op jit(solution)/shard_map/jit(_pad)/pad | solution.py:307
  10.1 1.0 %slice_bitcast_fusion = bf16[2,128,512]{2,1,0:T(8,128)(2,1)S(1)} fusion(bf16[1,8,128,512]{3,2,1,0:T(8,128)(2,1)} %param.5), kind=kLoop, calls=%fused_computation.17 | loop fusion | bytes 524288 | tf_op jit(solution)/shard_map/slice | solution.py:312
  12.3 1.5 %collective-permute-start.4 = (bf16[3,64,512]{2,1,0:T(8,128)(2,1)S(1)}, bf16[3,64,512]{2,1,0:T(8,128)(2,1)S(1)}, u32[]{:S(2)}, u32[]{:S(2)}) collective-permute-start(bf16[3,64,512]{2,1,0:T(8,128)(2,1)S(1)} %collective-permute-done.2.refs_1_), channel_id=1, source_target_pairs={{0,16},{4,12},{8,24},{12,4},{16,0},{20,28},{24,8},{28,20},{1,17},{... | collective-permute-start | bytes 589832 | tf_op jit(solution)/shard_map/down_tm_1/ppermute | solution.py:32
  14.5 2.1 %collective-permute-start.16 = (bf16[2,3,64,512]{3,2,1,0:T(8,128)(2,1)S(1)}, bf16[2,3,64,512]{3,2,1,0:T(8,128)(2,1)S(1)}, u32[]{:S(2)}, u32[]{:S(2)}) collective-permute-start(bf16[2,3,64,512]{3,2,1,0:T(8,128)(2,1)S(1)} %bitcast_dynamic-update-slice_fusion), channel_id=1, source_target_pairs={{0,16},{4,12},{8,24},{12,4},{16,0},{20,28},{24,8},{28,20},{1,17},{... | collective-permute-start | bytes 1179656 | tf_op jit(solution)/shard_map/time_tm_1/ppermute | solution.py:32
  16.6 2.6 %collective-permute-start.12 = (bf16[2,128,512]{2,1,0:T(8,128)(2,1)S(1)}, bf16[2,128,512]{2,1,0:T(8,128)(2,1)S(1)}, u32[]{:S(2)}, u32[]{:S(2)}) collective-permute-start(bf16[2,128,512]{2,1,0:T(8,128)(2,1)S(1)} %slice_bitcast_fusion), channel_id=1, source_target_pairs={{0,4},{4,8},{8,12},{12,16},{16,20},{20,24},{24,28},{1,5},{5,9},{9,... | collective-permute-start | bytes 786440 | tf_op jit(solution)/shard_map/halo_tm1_2/ppermute | solution.py:57
  19.2 1.4 %collective-permute-start.10 = (bf16[3,64,512]{2,1,0:T(8,128)(2,1)S(1)}, bf16[3,64,512]{2,1,0:T(8,128)(2,1)S(1)}, u32[]{:S(2)}, u32[]{:S(2)}) collective-permute-start(bf16[3,64,512]{2,1,0:T(8,128)(2,1)S(1)} %collective-permute-done.4.refs_3_), channel_id=1, source_target_pairs={{0,4},{4,0},{8,12},{12,8},{16,20},{20,16},{24,28},{28,24},{1,5},{5... | collective-permute-start | bytes 589832 | tf_op jit(solution)/shard_map/down_tm_core/ppermute | solution.py:37
  20.6 1.5 %features.1 = (bf16[8,128,512]{2,1,0:T(8,128)(2,1)S(1)}, bf16[512,1024]{1,0:T(8,128)(2,1)S(1)}) custom-call(s32[23]{0:T(128)S(1)} %pad_add_fusion.meta, bf16[8,128,512]{2,1,0:T(8,128)(2,1)S(1)} %bitcast.27), custom_call_target="tpu_custom_call" | custom-call | flops 20000000000 | bytes 1000 | tf_op jit(solution)/shard_map/features/pallas_call | solution.py:280
  22.1 3.5 %backward.1 = (f32[8,128,512]{2,1,0:T(8,128)S(1)}, bf16[10,128,512]{2,1,0:T(8,128)(2,1)S(1)}, f32[2,3,64,512]{3,2,1,0:T(8,128)S(1)}, f32[2,3,64,512]{3,2,1,0:T(8...) custom-call(s32[23]{0:T(128)S(1)} %pad_add_fusion.meta, ...), custom_call_target="tpu_custom_call" | custom-call | flops 1000000 | bytes 1000 | tf_op jit(solution)/shard_map/backward/pallas_call | solution.py:280
  29.1 3.6 %forward.1 = (bf16[8,128,512]{2,1,0:T(8,128)(2,1)S(1)}, bf16[2,128,512]{2,1,0:T(8,128)(2,1)S(1)}, f32[2,3,64,512]{3,2,1,0:T(8,128)S(1)}, f32[2,3,64,512]{3,2,1,0...) custom-call(s32[23]{0:T(128)S(1)} %pad_add_fusion.meta, ...), custom_call_target="tpu_custom_call" | custom-call | flops 1000000 | bytes 1000 | tf_op jit(solution)/shard_map/forward/pallas_call | solution.py:280
  33.8 2.4 %collective-permute-done.19 = bf16[2,3,64,512]{3,2,1,0:T(8,128)(2,1)S(1)} collective-permute-done((bf16[2,3,64,512]{3,2,1,0:T(8,128)(2,1)S(1)}, bf16[2,3,64,512]{3,2,1,0:T(8,128)(2,1)S(1)}, u32[]{:S(2)}, u32[]{:S(2)}) %collective-permute-start.19) | collective-permute-done | bytes 393248 | tf_op jit(solution)/shard_map/grad_time_tm_0/ppermute | solution.py:32
  36.4 1.1 %collective-permute-start.24 = (bf16[1,3,64,512]{3,2,1,0:T(8,128)(2,1)S(1)}, bf16[1,3,64,512]{3,2,1,0:T(8,128)(2,1)S(1)}, u32[]{:S(2)}, u32[]{:S(2)}) collective-permute-start(bf16[1,3,64,512]{3,2,1,0:T(8,128)(2,1)S(1)} %slice.138), channel_id=1, source_target_pairs={{0,16},{4,12},{8,24},{12,4},{16,0},{20,28},{24,8},{28,20},{1,17},{... | collective-permute-start | bytes 589832 | tf_op jit(solution)/shard_map/grad_time_tm_1/ppermute | solution.py:32
  38.4 1.9 %collective-permute-start.23 = (bf16[2,3,32,512]{3,2,1,0:T(8,128)(2,1)S(1)}, bf16[2,3,32,512]{3,2,1,0:T(8,128)(2,1)S(1)}, u32[]{:S(2)}, u32[]{:S(2)}) collective-permute-start(bf16[2,3,32,512]{3,2,1,0:T(8,128)(2,1)S(1)} %get-tuple-element.103), channel_id=1, source_target_pairs={{0,8},{4,20},{8,0},{12,28},{16,24},{20,4},{24,16},{28,12},{1,9},{5... | collective-permute-start | bytes 589832 | tf_op jit(solution)/shard_map/grad_down0_tm_0/ppermute | solution.py:32
  40.3 4.4 %clips.1 = bf16[8,128,512]{2,1,0:T(8,128)(2,1)} custom-call(s32[23]{0:T(128)S(1)} %pad_add_fusion.meta, bf16[8,128,512]{2,1,0:T(8,128)(2,1)S(1)} %bitcast.29, f32[8,128,512]{2,1,0:T(8,128)S(1)} %get-tuple-element.85.gh, bf16[10,128,512]{2,1,0:T(8,128)(2,1)S(1)} %get-tuple-element.69.gm, bf16[3,64,512]{2,1,0:T(8,128)(2,1)S(1)} %copy-done.2, ...), custom_call_target="tpu_custom_call" | custom-call | flops 1000000 | bytes 1000 | tf_op jit(solution)/shard_map/clips/pallas_call | solution.py:280
  44.7 1.6 %collective-permute-start.28 = (bf16[3,64,512]{2,1,0:T(8,128)(2,1)S(1)}, bf16[3,64,512]{2,1,0:T(8,128)(2,1)S(1)}, u32[]{:S(2)}, u32[]{:S(2)}) collective-permute-start(bf16[3,64,512]{2,1,0:T(8,128)(2,1)S(1)} %fusion.4), channel_id=1, source_target_pairs={{0,1},{1,0},{2,3},{3,2},{4,6},{5,7},{6,4},{7,5},{8,9},{9,8},{10,11... | collective-permute-start | bytes 589832 | tf_op jit(solution)/shard_map/grad_time_group_0/ppermute | solution.py:50
  46.4 1.0 %collective-permute-start.25 = (bf16[1,3,32,512]{3,2,1,0:T(8,128)(2,1)S(1)}, bf16[1,3,32,512]{3,2,1,0:T(8,128)(2,1)S(1)}, u32[]{:S(2)}, u32[]{:S(2)}) collective-permute-start(bf16[1,3,32,512]{3,2,1,0:T(8,128)(2,1)S(1)} %slice.140), channel_id=1, source_target_pairs={{0,16},{4,12},{8,24},{12,4},{16,0},{20,28},{24,8},{28,20},{1,17},{... | collective-permute-start | bytes 294920 | tf_op jit(solution)/shard_map/grad_down0_tm_1/ppermute | solution.py:32
  47.5 1.1 %collective-permute-start.29 = (bf16[1,3,32,512]{3,2,1,0:T(8,128)(2,1)S(1)}, bf16[1,3,32,512]{3,2,1,0:T(8,128)(2,1)S(1)}, u32[]{:S(2)}, u32[]{:S(2)}) collective-permute-start(bf16[1,3,32,512]{3,2,1,0:T(8,128)(2,1)S(1)} %slice.139), channel_id=1, source_target_pairs={{0,16},{4,12},{8,24},{12,4},{16,0},{20,28},{24,8},{28,20},{1,17},{... | collective-permute-start | bytes 294920 | tf_op jit(solution)/shard_map/grad_down1_tm_1/ppermute | solution.py:32
  48.6 2.4 %collective-permute-done.25 = bf16[1,3,32,512]{3,2,1,0:T(8,128)(2,1)S(1)} collective-permute-done((bf16[1,3,32,512]{3,2,1,0:T(8,128)(2,1)S(1)}, bf16[1,3,32,512]{3,2,1,0:T(8,128)(2,1)S(1)}, u32[]{:S(2)}, u32[]{:S(2)}) %collective-permute-start.25) | collective-permute-done | bytes 98336 | tf_op jit(solution)/shard_map/grad_down0_tm_1/ppermute | solution.py:32
  51.1 1.3 %collective-permute-start.27 = (bf16[3,32,512]{2,1,0:T(8,128)(2,1)S(1)}, bf16[3,32,512]{2,1,0:T(8,128)(2,1)S(1)}, u32[]{:S(2)}, u32[]{:S(2)}) collective-permute-start(bf16[3,32,512]{2,1,0:T(8,128)(2,1)S(1)} %fusion.7), channel_id=1, source_target_pairs={{0,1},{1,0},{2,3},{3,2},{4,6},{5,7},{6,4},{7,5},{8,9},{9,8},{10,11... | collective-permute-start | bytes 294920 | tf_op jit(solution)/shard_map/grad_down0_group_0/ppermute | solution.py:50
  52.5 1.1 %collective-permute-start.30 = (bf16[3,32,512]{2,1,0:T(8,128)(2,1)S(1)}, bf16[3,32,512]{2,1,0:T(8,128)(2,1)S(1)}, u32[]{:S(2)}, u32[]{:S(2)}) collective-permute-start(bf16[3,32,512]{2,1,0:T(8,128)(2,1)S(1)} %fusion.8), channel_id=1, source_target_pairs={{0,1},{1,0},{2,3},{3,2},{4,6},{5,7},{6,4},{7,5},{8,9},{9,8},{10,11... | collective-permute-start | bytes 294920 | tf_op jit(solution)/shard_map/grad_down1_group_0/ppermute | solution.py:50
  53.6 1.6 %collective-permute-start.31 = (bf16[2,128,512]{2,1,0:T(8,128)(2,1)S(1)}, bf16[2,128,512]{2,1,0:T(8,128)(2,1)S(1)}, u32[]{:S(2)}, u32[]{:S(2)}) collective-permute-start(bf16[2,128,512]{2,1,0:T(8,128)(2,1)S(1)} %get-tuple-element.96), channel_id=1, source_target_pairs={{0,4},{4,8},{8,12},{12,16},{16,20},{20,24},{24,28},{1,5},{5,9},{9,... | collective-permute-start | bytes 786440 | tf_op jit(solution)/shard_map/halo_tm1_2/ppermute | solution.py:57
  55.2 2.4 %collective-permute-start.32 = (bf16[3,64,512]{2,1,0:T(8,128)(2,1)S(1)}, bf16[3,64,512]{2,1,0:T(8,128)(2,1)S(1)}, u32[]{:S(2)}, u32[]{:S(2)}) collective-permute-start(bf16[3,64,512]{2,1,0:T(8,128)(2,1)S(1)} %add_convert_fusion), channel_id=1, source_target_pairs={{0,2},{1,3},{2,0},{3,1},{4,5},{5,4},{6,7},{7,6},{8,10},{9,11},{10,... | collective-permute-start | bytes 589832 | tf_op jit(solution)/shard_map/grad_time_group_1/ppermute | solution.py:50
  57.9 2.9 %collective-permute-start.34 = (bf16[3,32,512]{2,1,0:T(8,128)(2,1)S(1)}, bf16[3,32,512]{2,1,0:T(8,128)(2,1)S(1)}, u32[]{:S(2)}, u32[]{:S(2)}) collective-permute-start(bf16[3,32,512]{2,1,0:T(8,128)(2,1)S(1)} %add_convert_fusion.1), channel_id=1, source_target_pairs={{0,2},{1,3},{2,0},{3,1},{4,5},{5,4},{6,7},{7,6},{8,10},{9,11},{10,... | collective-permute-start | bytes 294920 | tf_op jit(solution)/shard_map/grad_down1_group_1/ppermute | solution.py:50
  61.0 2.4 %reduced.1 = bf16[4,128,512]{2,1,0:T(8,128)(2,1)} custom-call(s32[23]{0:T(128)S(1)} %pad_add_fusion.meta, bf16[2,128,512]{2,1,0:T(8,128)(2,1)S(1)} %collective-permute-done.31.before, bf16[8,128,512]{2,1,0:T(8,128)(2,1)S(1)} %get-tuple-element.74.hidden, bf16[3,64,512]{2,1,0:T(8,128)(2,1)S(1)} %copy-done.3, ...), custom_call_target="tpu_custom_call" | custom-call | flops 1000000 | bytes 1000 | tf_op jit(solution)/shard_map/reduced/pallas_call | solution.py:280
  63.4 0.8 %convert_add_fusion = f32[3,64,512]{2,1,0:T(8,128)} fusion(bf16[3,64,512]{2,1,0:T(8,128)(2,1)S(1)} %collective-permute-done.32, bf16[3,64,512]{2,1,0:T(8,128)(2,1)S(1)} %add_convert_fusion), kind=kLoop, calls=%fused_computation.15 | loop fusion | flops 294912 | bytes 786432 | tf_op jit(solution)/shard_map/add | solution.py:408
  64.2 1.1 %collective-permute-done.34 = bf16[3,32,512]{2,1,0:T(8,128)(2,1)S(1)} collective-permute-done((bf16[3,32,512]{2,1,0:T(8,128)(2,1)S(1)}, bf16[3,32,512]{2,1,0:T(8,128)(2,1)S(1)}, u32[]{:S(2)}, u32[]{:S(2)}) %collective-permute-start.34) | collective-permute-done | bytes 98336 | tf_op jit(solution)/shard_map/grad_down1_group_1/ppermute | solution.py:50
  65.2 2.0 %collective-permute-done.33 = bf16[3,32,512]{2,1,0:T(8,128)(2,1)S(1)} collective-permute-done((bf16[3,32,512]{2,1,0:T(8,128)(2,1)S(1)}, bf16[3,32,512]{2,1,0:T(8,128)(2,1)S(1)}, u32[]{:S(2)}, u32[]{:S(2)}) %collective-permute-start.33) | collective-permute-done | bytes 98336 | tf_op jit(solution)/shard_map/grad_down0_group_1/ppermute | solution.py:50
  67.3 0.8 %pad_maximum_fusion = f32[3,64,512]{2,1,0:T(8,128)} fusion(f32[3,32,512]{2,1,0:T(8,128)S(1)} %get-tuple-element.106, f32[3,32,512]{2,1,0:T(8,128)S(1)} %get-tuple-element.107), kind=kLoop, calls=%fused_computation.14 | loop fusion | flops 98304 | bytes 786432 | tf_op jit(solution)/shard_map/concatenate | solution.py:421
  (81 shorter events, 9.0 us)
Async XLA Ops:
  0.7 11.7 %collective-permute-start.8 = (bf16[3,64,512]{2,1,0:T(8,128)(2,1)}, bf16[3,64,512]{2,1,0:T(8,128)(2,1)S(1)}, u32[]{:S(2)}, u32[]{:S(2)}) collective-permute-start(bf16[3,64,512]{2,1,0:T(8,128)(2,1)} %refs_0_.6), channel_id=1, source_target_pairs={{0,4},{4,0},{8,12},{12,8},{16,20},{20,16},{24,28},{28,24},{1,5},{5... | collective-permute-start | bytes 589832 | tf_op jit(solution)/shard_map/time_tm_core/ppermute | solution.py:37
  1.2 12.7 %collective-permute-start.3 = (bf16[3,64,512]{2,1,0:T(8,128)(2,1)}, bf16[3,64,512]{2,1,0:T(8,128)(2,1)S(1)}, u32[]{:S(2)}, u32[]{:S(2)}) collective-permute-start(bf16[3,64,512]{2,1,0:T(8,128)(2,1)} %refs_0_.6), channel_id=1, source_target_pairs={{0,8},{4,20},{8,0},{12,28},{16,24},{20,4},{24,16},{28,12},{1,9},{5... | collective-permute-start | bytes 589832 | tf_op jit(solution)/shard_map/time_tm_0/ppermute | solution.py:32
  3.7 8.5 %collective-permute-start.2 = (bf16[3,64,512]{2,1,0:T(8,128)(2,1)}, bf16[3,64,512]{2,1,0:T(8,128)(2,1)S(1)}, u32[]{:S(2)}, u32[]{:S(2)}) collective-permute-start(bf16[3,64,512]{2,1,0:T(8,128)(2,1)} %refs_0_.7), channel_id=1, source_target_pairs={{0,8},{4,20},{8,0},{12,28},{16,24},{20,4},{24,16},{28,12},{1,9},{5... | collective-permute-start | bytes 589832 | tf_op jit(solution)/shard_map/down_tm_0/ppermute | solution.py:32
  3.8 7.8 %collective-permute-start.1 = (bf16[3,64,512]{2,1,0:T(8,128)(2,1)}, bf16[3,64,512]{2,1,0:T(8,128)(2,1)S(1)}, u32[]{:S(2)}, u32[]{:S(2)}) collective-permute-start(bf16[3,64,512]{2,1,0:T(8,128)(2,1)} %refs_0_.7), channel_id=1, source_target_pairs={{0,16},{4,12},{8,24},{12,4},{16,0},{20,28},{24,8},{28,20},{1,17},{... | collective-permute-start | bytes 589832 | tf_op jit(solution)/shard_map/down_own_tm_1/ppermute | solution.py:32
  6.8 7.3 %collective-permute-start = (bf16[2,128,512]{2,1,0:T(8,128)(2,1)S(1)}, bf16[2,128,512]{2,1,0:T(8,128)(2,1)S(1)}, u32[]{:S(2)}, u32[]{:S(2)}) collective-permute-start(bf16[2,128,512]{2,1,0:T(8,128)(2,1)S(1)} %slice_bitcast_fusion.1), channel_id=1, source_target_pairs={{4,0},{8,4},{12,8},{16,12},{20,16},{24,20},{28,24},{5,1},{9,5},{13... | collective-permute-start | bytes 786440 | tf_op jit(solution)/shard_map/halo_tm-1_2/ppermute | solution.py:57
  11.6 2.9 %collective-permute-start.5 = (bf16[3,64,512]{2,1,0:T(8,128)(2,1)S(1)}, bf16[3,64,512]{2,1,0:T(8,128)(2,1)S(1)}, u32[]{:S(2)}, u32[]{:S(2)}) collective-permute-start(bf16[3,64,512]{2,1,0:T(8,128)(2,1)S(1)} %copy-done.3), channel_id=1, source_target_pairs={{0,4},{4,0},{8,12},{12,8},{16,20},{20,16},{24,28},{28,24},{1,5},{5... | collective-permute-start | bytes 589832 | tf_op jit(solution)/shard_map/down_tm_core/ppermute | solution.py:37
  12.3 6.9 %collective-permute-start.6 = (bf16[3,64,512]{2,1,0:T(8,128)(2,1)S(1)}, bf16[3,64,512]{2,1,0:T(8,128)(2,1)S(1)}, u32[]{:S(2)}, u32[]{:S(2)}) collective-permute-start(bf16[3,64,512]{2,1,0:T(8,128)(2,1)S(1)} %collective-permute-done.2.refs_1_), channel_id=1, source_target_pairs={{0,4},{4,0},{8,12},{12,8},{16,20},{20,16},{24,28},{28,24},{1,5},{5... | collective-permute-start | bytes 589832 | tf_op jit(solution)/shard_map/down_tm_core/ppermute | solution.py:37
  12.3 6.8 %collective-permute-start.4 = (bf16[3,64,512]{2,1,0:T(8,128)(2,1)S(1)}, bf16[3,64,512]{2,1,0:T(8,128)(2,1)S(1)}, u32[]{:S(2)}, u32[]{:S(2)}) collective-permute-start(bf16[3,64,512]{2,1,0:T(8,128)(2,1)S(1)} %collective-permute-done.2.refs_1_), channel_id=1, source_target_pairs={{0,16},{4,12},{8,24},{12,4},{16,0},{20,28},{24,8},{28,20},{1,17},{... | collective-permute-start | bytes 589832 | tf_op jit(solution)/shard_map/down_tm_1/ppermute | solution.py:32
  13.9 5.3 %collective-permute-start.7 = (bf16[3,64,512]{2,1,0:T(8,128)(2,1)S(1)}, bf16[3,64,512]{2,1,0:T(8,128)(2,1)S(1)}, u32[]{:S(2)}, u32[]{:S(2)}) collective-permute-start(bf16[3,64,512]{2,1,0:T(8,128)(2,1)S(1)} %collective-permute-done.1.refs_2_), channel_id=1, source_target_pairs={{0,4},{4,0},{8,12},{12,8},{16,20},{20,16},{24,28},{28,24},{1,5},{5... | collective-permute-start | bytes 589832 | tf_op jit(solution)/shard_map/down_tm_core/ppermute | solution.py:37
  14.1 2.5 %collective-permute-start.9 = (bf16[3,64,512]{2,1,0:T(8,128)(2,1)S(1)}, bf16[3,64,512]{2,1,0:T(8,128)(2,1)S(1)}, u32[]{:S(2)}, u32[]{:S(2)}) collective-permute-start(bf16[3,64,512]{2,1,0:T(8,128)(2,1)S(1)} %collective-permute-done.3.refs_1_), channel_id=1, source_target_pairs={{0,4},{4,0},{8,12},{12,8},{16,20},{20,16},{24,28},{28,24},{1,5},{5... | collective-permute-start | bytes 589832 | tf_op jit(solution)/shard_map/time_tm_core/ppermute | solution.py:37
  14.5 11.9 %collective-permute-start.16 = (bf16[2,3,64,512]{3,2,1,0:T(8,128)(2,1)S(1)}, bf16[2,3,64,512]{3,2,1,0:T(8,128)(2,1)S(1)}, u32[]{:S(2)}, u32[]{:S(2)}) collective-permute-start(bf16[2,3,64,512]{3,2,1,0:T(8,128)(2,1)S(1)} %bitcast_dynamic-update-slice_fusion), channel_id=1, source_target_pairs={{0,16},{4,12},{8,24},{12,4},{16,0},{20,28},{24,8},{28,20},{1,17},{... | collective-permute-start | bytes 1179656 | tf_op jit(solution)/shard_map/time_tm_1/ppermute | solution.py:32
  16.6 10.2 %collective-permute-start.12 = (bf16[2,128,512]{2,1,0:T(8,128)(2,1)S(1)}, bf16[2,128,512]{2,1,0:T(8,128)(2,1)S(1)}, u32[]{:S(2)}, u32[]{:S(2)}) collective-permute-start(bf16[2,128,512]{2,1,0:T(8,128)(2,1)S(1)} %slice_bitcast_fusion), channel_id=1, source_target_pairs={{0,4},{4,8},{8,12},{12,16},{16,20},{20,24},{24,28},{1,5},{5,9},{9,... | collective-permute-start | bytes 786440 | tf_op jit(solution)/shard_map/halo_tm1_2/ppermute | solution.py:57
  19.2 2.9 %collective-permute-start.10 = (bf16[3,64,512]{2,1,0:T(8,128)(2,1)S(1)}, bf16[3,64,512]{2,1,0:T(8,128)(2,1)S(1)}, u32[]{:S(2)}, u32[]{:S(2)}) collective-permute-start(bf16[3,64,512]{2,1,0:T(8,128)(2,1)S(1)} %collective-permute-done.4.refs_3_), channel_id=1, source_target_pairs={{0,4},{4,0},{8,12},{12,8},{16,20},{20,16},{24,28},{28,24},{1,5},{5... | collective-permute-start | bytes 589832 | tf_op jit(solution)/shard_map/down_tm_core/ppermute | solution.py:37
  26.3 1.7 %collective-permute-start.15 = (bf16[3,64,512]{2,1,0:T(8,128)(2,1)S(1)}, bf16[3,64,512]{2,1,0:T(8,128)(2,1)S(1)}, u32[]{:S(2)}, u32[]{:S(2)}) collective-permute-start(bf16[3,64,512]{2,1,0:T(8,128)(2,1)S(1)} %get-tuple-element.66), channel_id=1, source_target_pairs={{0,4},{4,0},{8,12},{12,8},{16,20},{20,16},{24,28},{28,24},{1,5},{5... | collective-permute-start | bytes 589832 | tf_op jit(solution)/shard_map/grad_time_tm_core/ppermute | solution.py:37
  26.8 2.2 %collective-permute-start.17 = (bf16[2,3,64,512]{3,2,1,0:T(8,128)(2,1)S(1)}, bf16[2,3,64,512]{3,2,1,0:T(8,128)(2,1)S(1)}, u32[]{:S(2)}, u32[]{:S(2)}) collective-permute-start(bf16[2,3,64,512]{3,2,1,0:T(8,128)(2,1)S(1)} %collective-permute-done.16.refs_2_), channel_id=1, source_target_pairs={{0,4},{4,0},{8,12},{12,8},{16,20},{20,16},{24,28},{28,24},{1,5},{5... | collective-permute-start | bytes 1179656 | tf_op jit(solution)/shard_map/time_tm_core/ppermute | solution.py:37
  28.3 7.8 %collective-permute-start.19 = (bf16[2,3,64,512]{3,2,1,0:T(8,128)(2,1)S(1)}, bf16[2,3,64,512]{3,2,1,0:T(8,128)(2,1)S(1)}, u32[]{:S(2)}, u32[]{:S(2)}) collective-permute-start(bf16[2,3,64,512]{3,2,1,0:T(8,128)(2,1)S(1)} %fusion.2), channel_id=1, source_target_pairs={{0,8},{4,20},{8,0},{12,28},{16,24},{20,4},{24,16},{28,12},{1,9},{5... | collective-permute-start | bytes 1179656 | tf_op jit(solution)/shard_map/grad_time_tm_0/ppermute | solution.py:32
  32.7 4.9 %collective-permute-start.18 = (bf16[3,64,512]{2,1,0:T(8,128)(2,1)S(1)}, bf16[3,64,512]{2,1,0:T(8,128)(2,1)S(1)}, u32[]{:S(2)}, u32[]{:S(2)}) collective-permute-start(bf16[3,64,512]{2,1,0:T(8,128)(2,1)S(1)} %get-tuple-element.72), channel_id=1, source_target_pairs={{0,4},{4,0},{8,12},{12,8},{16,20},{20,16},{24,28},{28,24},{1,5},{5... | collective-permute-start | bytes 589832 | tf_op jit(solution)/shard_map/grad_down_tm_core/ppermute | solution.py:37
  33.1 4.5 %collective-permute-start.20 = (bf16[3,64,512]{2,1,0:T(8,128)(2,1)S(1)}, bf16[3,64,512]{2,1,0:T(8,128)(2,1)S(1)}, u32[]{:S(2)}, u32[]{:S(2)}) collective-permute-start(bf16[3,64,512]{2,1,0:T(8,128)(2,1)S(1)} %get-tuple-element.77), channel_id=1, source_target_pairs={{0,4},{4,0},{8,12},{12,8},{16,20},{20,16},{24,28},{28,24},{1,5},{5... | collective-permute-start | bytes 589832 | tf_op jit(solution)/shard_map/grad_down_tm_core/ppermute | solution.py:37
  33.3 4.3 %collective-permute-start.21 = (bf16[3,64,512]{2,1,0:T(8,128)(2,1)S(1)}, bf16[3,64,512]{2,1,0:T(8,128)(2,1)S(1)}, u32[]{:S(2)}, u32[]{:S(2)}) collective-permute-start(bf16[3,64,512]{2,1,0:T(8,128)(2,1)S(1)} %get-tuple-element.79), channel_id=1, source_target_pairs={{0,4},{4,0},{8,12},{12,8},{16,20},{20,16},{24,28},{28,24},{1,5},{5... | collective-permute-start | bytes 589832 | tf_op jit(solution)/shard_map/grad_down_tm_core/ppermute | solution.py:37
  33.6 4.0 %collective-permute-start.22 = (bf16[3,64,512]{2,1,0:T(8,128)(2,1)S(1)}, bf16[3,64,512]{2,1,0:T(8,128)(2,1)S(1)}, u32[]{:S(2)}, u32[]{:S(2)}) collective-permute-start(bf16[3,64,512]{2,1,0:T(8,128)(2,1)S(1)} %get-tuple-element.81), channel_id=1, source_target_pairs={{0,4},{4,0},{8,12},{12,8},{16,20},{20,16},{24,28},{28,24},{1,5},{5... | collective-permute-start | bytes 589832 | tf_op jit(solution)/shard_map/grad_down_tm_core/ppermute | solution.py:37
  36.4 8.2 %collective-permute-start.24 = (bf16[1,3,64,512]{3,2,1,0:T(8,128)(2,1)S(1)}, bf16[1,3,64,512]{3,2,1,0:T(8,128)(2,1)S(1)}, u32[]{:S(2)}, u32[]{:S(2)}) collective-permute-start(bf16[1,3,64,512]{3,2,1,0:T(8,128)(2,1)S(1)} %slice.138), channel_id=1, source_target_pairs={{0,16},{4,12},{8,24},{12,4},{16,0},{20,28},{24,8},{28,20},{1,17},{... | collective-permute-start | bytes 589832 | tf_op jit(solution)/shard_map/grad_time_tm_1/ppermute | solution.py:32
  38.2 9.3 %collective-permute-start.26 = (bf16[2,3,32,512]{3,2,1,0:T(8,128)(2,1)S(1)}, bf16[2,3,32,512]{3,2,1,0:T(8,128)(2,1)S(1)}, u32[]{:S(2)}, u32[]{:S(2)}) collective-permute-start(bf16[2,3,32,512]{3,2,1,0:T(8,128)(2,1)S(1)} %get-tuple-element.102), channel_id=1, source_target_pairs={{0,8},{4,20},{8,0},{12,28},{16,24},{20,4},{24,16},{28,12},{1,9},{5... | collective-permute-start | bytes 589832 | tf_op jit(solution)/shard_map/grad_down1_tm_0/ppermute | solution.py:32
  38.4 8.0 %collective-permute-start.23 = (bf16[2,3,32,512]{3,2,1,0:T(8,128)(2,1)S(1)}, bf16[2,3,32,512]{3,2,1,0:T(8,128)(2,1)S(1)}, u32[]{:S(2)}, u32[]{:S(2)}) collective-permute-start(bf16[2,3,32,512]{3,2,1,0:T(8,128)(2,1)S(1)} %get-tuple-element.103), channel_id=1, source_target_pairs={{0,8},{4,20},{8,0},{12,28},{16,24},{20,4},{24,16},{28,12},{1,9},{5... | collective-permute-start | bytes 589832 | tf_op jit(solution)/shard_map/grad_down0_tm_0/ppermute | solution.py:32
  44.7 10.5 %collective-permute-start.28 = (bf16[3,64,512]{2,1,0:T(8,128)(2,1)S(1)}, bf16[3,64,512]{2,1,0:T(8,128)(2,1)S(1)}, u32[]{:S(2)}, u32[]{:S(2)}) collective-permute-start(bf16[3,64,512]{2,1,0:T(8,128)(2,1)S(1)} %fusion.4), channel_id=1, source_target_pairs={{0,1},{1,0},{2,3},{3,2},{4,6},{5,7},{6,4},{7,5},{8,9},{9,8},{10,11... | collective-permute-start | bytes 589832 | tf_op jit(solution)/shard_map/grad_time_group_0/ppermute | solution.py:50
  46.4 4.7 %collective-permute-start.25 = (bf16[1,3,32,512]{3,2,1,0:T(8,128)(2,1)S(1)}, bf16[1,3,32,512]{3,2,1,0:T(8,128)(2,1)S(1)}, u32[]{:S(2)}, u32[]{:S(2)}) collective-permute-start(bf16[1,3,32,512]{3,2,1,0:T(8,128)(2,1)S(1)} %slice.140), channel_id=1, source_target_pairs={{0,16},{4,12},{8,24},{12,4},{16,0},{20,28},{24,8},{28,20},{1,17},{... | collective-permute-start | bytes 294920 | tf_op jit(solution)/shard_map/grad_down0_tm_1/ppermute | solution.py:32
  47.5 4.9 %collective-permute-start.29 = (bf16[1,3,32,512]{3,2,1,0:T(8,128)(2,1)S(1)}, bf16[1,3,32,512]{3,2,1,0:T(8,128)(2,1)S(1)}, u32[]{:S(2)}, u32[]{:S(2)}) collective-permute-start(bf16[1,3,32,512]{3,2,1,0:T(8,128)(2,1)S(1)} %slice.139), channel_id=1, source_target_pairs={{0,16},{4,12},{8,24},{12,4},{16,0},{20,28},{24,8},{28,20},{1,17},{... | collective-permute-start | bytes 294920 | tf_op jit(solution)/shard_map/grad_down1_tm_1/ppermute | solution.py:32
  51.1 6.5 %collective-permute-start.27 = (bf16[3,32,512]{2,1,0:T(8,128)(2,1)S(1)}, bf16[3,32,512]{2,1,0:T(8,128)(2,1)S(1)}, u32[]{:S(2)}, u32[]{:S(2)}) collective-permute-start(bf16[3,32,512]{2,1,0:T(8,128)(2,1)S(1)} %fusion.7), channel_id=1, source_target_pairs={{0,1},{1,0},{2,3},{3,2},{4,6},{5,7},{6,4},{7,5},{8,9},{9,8},{10,11... | collective-permute-start | bytes 294920 | tf_op jit(solution)/shard_map/grad_down0_group_0/ppermute | solution.py:50
  52.5 5.4 %collective-permute-start.30 = (bf16[3,32,512]{2,1,0:T(8,128)(2,1)S(1)}, bf16[3,32,512]{2,1,0:T(8,128)(2,1)S(1)}, u32[]{:S(2)}, u32[]{:S(2)}) collective-permute-start(bf16[3,32,512]{2,1,0:T(8,128)(2,1)S(1)} %fusion.8), channel_id=1, source_target_pairs={{0,1},{1,0},{2,3},{3,2},{4,6},{5,7},{6,4},{7,5},{8,9},{9,8},{10,11... | collective-permute-start | bytes 294920 | tf_op jit(solution)/shard_map/grad_down1_group_0/ppermute | solution.py:50
  53.6 7.4 %collective-permute-start.31 = (bf16[2,128,512]{2,1,0:T(8,128)(2,1)S(1)}, bf16[2,128,512]{2,1,0:T(8,128)(2,1)S(1)}, u32[]{:S(2)}, u32[]{:S(2)}) collective-permute-start(bf16[2,128,512]{2,1,0:T(8,128)(2,1)S(1)} %get-tuple-element.96), channel_id=1, source_target_pairs={{0,4},{4,8},{8,12},{12,16},{16,20},{20,24},{24,28},{1,5},{5,9},{9,... | collective-permute-start | bytes 786440 | tf_op jit(solution)/shard_map/halo_tm1_2/ppermute | solution.py:57
  55.2 8.2 %collective-permute-start.32 = (bf16[3,64,512]{2,1,0:T(8,128)(2,1)S(1)}, bf16[3,64,512]{2,1,0:T(8,128)(2,1)S(1)}, u32[]{:S(2)}, u32[]{:S(2)}) collective-permute-start(bf16[3,64,512]{2,1,0:T(8,128)(2,1)S(1)} %add_convert_fusion), channel_id=1, source_target_pairs={{0,2},{1,3},{2,0},{3,1},{4,5},{5,4},{6,7},{7,6},{8,10},{9,11},{10,... | collective-permute-start | bytes 589832 | tf_op jit(solution)/shard_map/grad_time_group_1/ppermute | solution.py:50
  57.9 7.3 %collective-permute-start.34 = (bf16[3,32,512]{2,1,0:T(8,128)(2,1)S(1)}, bf16[3,32,512]{2,1,0:T(8,128)(2,1)S(1)}, u32[]{:S(2)}, u32[]{:S(2)}) collective-permute-start(bf16[3,32,512]{2,1,0:T(8,128)(2,1)S(1)} %add_convert_fusion.1), channel_id=1, source_target_pairs={{0,2},{1,3},{2,0},{3,1},{4,5},{5,4},{6,7},{7,6},{8,10},{9,11},{10,... | collective-permute-start | bytes 294920 | tf_op jit(solution)/shard_map/grad_down1_group_1/ppermute | solution.py:50
  60.9 6.3 %collective-permute-start.33 = (bf16[3,32,512]{2,1,0:T(8,128)(2,1)S(1)}, bf16[3,32,512]{2,1,0:T(8,128)(2,1)S(1)}, u32[]{:S(2)}, u32[]{:S(2)}) collective-permute-start(bf16[3,32,512]{2,1,0:T(8,128)(2,1)S(1)} %add_convert_fusion.2), channel_id=1, source_target_pairs={{0,2},{1,3},{2,0},{3,1},{4,5},{5,4},{6,7},{7,6},{8,10},{9,11},{10,... | collective-permute-start | bytes 294920 | tf_op jit(solution)/shard_map/grad_down0_group_1/ppermute | solution.py:50
  (7 other events, 38.1 us)

commit v6 on v5

--- a/solution.py
+++ b/solution.py
@@ -318,7 +318,7 @@
     h, ht = call(
         functools.partial(features_kernel, chips=chips, rows=rows),
         "features",
-        [after(meta, *first, *down_late, *down_other, *time_other), x],
+        [after(me[None].astype(jnp.int32), *first, *down_late, *down_other, *time_other), x],
         (sds((frames, cells, width)), sds((width, lot))),
         [scratch(width, cells)],
         FEATURES_COST,

time: 68.3 us -> 68 us (level)
  transfers between devices with their start and end apart: 35 -> 35, of which waited for: 10 -> 10; matrix products, arithmetic and copies ran while one was open for 9% -> 9% of each run, Pallas kernels for 23% -> 22%
where the time goes in v6:
time: 68 us; the launch traced here: 67.6 us
  starting transfers between devices  34.9 us (51%)
  Pallas kernels  14.8 us (22%)
  waiting for transfers between devices  9.84 us (14%)
  other arithmetic  3.99 us (6%)
  local copies, waits for them, and re-layouts  3.14 us (5%)
  between operations  0.92 us (1%)
    pallas_call x5, Pallas kernels, call(): pl.pallas_call(kernel, in_specs=[SMEM] + [VMEM] * (len(inputs) - 1), out_...  14.8 us
    ppermute x11, starting transfers between devices, exchange(): return lax.ppermute(value, 'tm', route)  14.2 us
    ppermute x6, starting transfers between devices, group_exchange(): return lax.ppermute(value, ('tm', 'group'), route)  9.42 us
    ppermute x15, starting transfers between devices, core_swap(): lax.ppermute(value, 'tm', [(i, i ^ 1) for i in range(lax.axis_size('tm'))])  5.8 us
    ppermute x3, starting transfers between devices, shifted(): return lax.ppermute(block, axis, route)  5.45 us
    ppermute x11, waiting for transfers between devices, exchange(): return lax.ppermute(value, 'tm', route)  5.41 us
    ppermute x6, waiting for transfers between devices, group_exchange(): return lax.ppermute(value, ('tm', 'group'), route)  3.32 us
  transfers between devices with their start and end apart: 35, of which 10 were waited for; matrix products, arithmetic and copies ran while one was open for 9% of the time, Pallas kernels for 22%

profile of v6, /device:TPU:0, one launch (start us, length us, event | category | flops | bytes accessed | tf_op | source)
XLA Modules:
  0.0 67.6 jit_solution(10298922316622828922)
XLA Ops:
  1.2 2.6 %collective-permute-start.3 = (bf16[3,64,512]{2,1,0:T(8,128)(2,1)}, bf16[3,64,512]{2,1,0:T(8,128)(2,1)S(1)}, u32[]{:S(2)}, u32[]{:S(2)}) collective-permute-start(bf16[3,64,512]{2,1,0:T(8,128)(2,1)} %refs_0_.6), channel_id=1, source_target_pairs={{0,8},{4,20},{8,0},{12,28},{16,24},{20,4},{24,16},{28,12},{1,9},{5... | collective-permute-start | bytes 589832 | tf_op jit(solution)/shard_map/time_tm_0/ppermute | solution.py:32
  3.8 2.0 %collective-permute-start.1 = (bf16[3,64,512]{2,1,0:T(8,128)(2,1)}, bf16[3,64,512]{2,1,0:T(8,128)(2,1)S(1)}, u32[]{:S(2)}, u32[]{:S(2)}) collective-permute-start(bf16[3,64,512]{2,1,0:T(8,128)(2,1)} %refs_0_.7), channel_id=1, source_target_pairs={{0,16},{4,12},{8,24},{12,4},{16,0},{20,28},{24,8},{28,20},{1,17},{... | collective-permute-start | bytes 589832 | tf_op jit(solution)/shard_map/down_own_tm_1/ppermute | solution.py:32
  5.8 1.0 %slice_bitcast_fusion.1 = bf16[2,128,512]{2,1,0:T(8,128)(2,1)S(1)} fusion(bf16[1,4,128,512]{3,2,1,0:T(8,128)(2,1)} %param.9), kind=kLoop, calls=%fused_computation.18 | loop fusion | bytes 524288 | tf_op jit(solution)/shard_map/slice | solution.py:305
  6.8 1.3 %collective-permute-start = (bf16[2,128,512]{2,1,0:T(8,128)(2,1)S(1)}, bf16[2,128,512]{2,1,0:T(8,128)(2,1)S(1)}, u32[]{:S(2)}, u32[]{:S(2)}) collective-permute-start(bf16[2,128,512]{2,1,0:T(8,128)(2,1)S(1)} %slice_bitcast_fusion.1), channel_id=1, source_target_pairs={{4,0},{8,4},{12,8},{16,12},{20,16},{24,20},{28,24},{5,1},{9,5},{13... | collective-permute-start | bytes 786440 | tf_op jit(solution)/shard_map/halo_tm-1_2/ppermute | solution.py:57
  8.1 0.8 %select_reduce_fusion = s32[8]{0:T(128)S(1)} fusion(s32[8]{0:T(128)} %bitcast.43), kind=kLoop, calls=%fused_computation.34 | loop fusion | flops 184 | bytes 64 | tf_op jit(solution)/shard_map/reduce_sum | solution.py:292
  9.1 1.0 %pad.4 = bf16[2,3,64,512]{3,2,1,0:T(8,128)(2,1)S(1)} pad(bf16[1,3,64,512]{3,2,1,0:T(8,128)(2,1)} %bitcast.32, bf16[]{:T(256)} %constant.18.clone.1), padding=0_1x0_0x0_0x0_0 | pad | bytes 589826 | tf_op jit(solution)/shard_map/jit(_pad)/pad | solution.py:307
  10.1 1.0 %slice_bitcast_fusion = bf16[2,128,512]{2,1,0:T(8,128)(2,1)S(1)} fusion(bf16[1,8,128,512]{3,2,1,0:T(8,128)(2,1)} %param.5), kind=kLoop, calls=%fused_computation.17 | loop fusion | bytes 524288 | tf_op jit(solution)/shard_map/slice | solution.py:312
  12.3 1.5 %collective-permute-start.4 = (bf16[3,64,512]{2,1,0:T(8,128)(2,1)S(1)}, bf16[3,64,512]{2,1,0:T(8,128)(2,1)S(1)}, u32[]{:S(2)}, u32[]{:S(2)}) collective-permute-start(bf16[3,64,512]{2,1,0:T(8,128)(2,1)S(1)} %collective-permute-done.2.refs_1_), channel_id=1, source_target_pairs={{0,16},{4,12},{8,24},{12,4},{16,0},{20,28},{24,8},{28,20},{1,17},{... | collective-permute-start | bytes 589832 | tf_op jit(solution)/shard_map/down_tm_1/ppermute | solution.py:32
  14.5 2.1 %collective-permute-start.16 = (bf16[2,3,64,512]{3,2,1,0:T(8,128)(2,1)S(1)}, bf16[2,3,64,512]{3,2,1,0:T(8,128)(2,1)S(1)}, u32[]{:S(2)}, u32[]{:S(2)}) collective-permute-start(bf16[2,3,64,512]{3,2,1,0:T(8,128)(2,1)S(1)} %bitcast_dynamic-update-slice_fusion), channel_id=1, source_target_pairs={{0,16},{4,12},{8,24},{12,4},{16,0},{20,28},{24,8},{28,20},{1,17},{... | collective-permute-start | bytes 1179656 | tf_op jit(solution)/shard_map/time_tm_1/ppermute | solution.py:32
  16.6 2.6 %collective-permute-start.12 = (bf16[2,128,512]{2,1,0:T(8,128)(2,1)S(1)}, bf16[2,128,512]{2,1,0:T(8,128)(2,1)S(1)}, u32[]{:S(2)}, u32[]{:S(2)}) collective-permute-start(bf16[2,128,512]{2,1,0:T(8,128)(2,1)S(1)} %slice_bitcast_fusion), channel_id=1, source_target_pairs={{0,4},{4,8},{8,12},{12,16},{16,20},{20,24},{24,28},{1,5},{5,9},{9,... | collective-permute-start | bytes 786440 | tf_op jit(solution)/shard_map/halo_tm1_2/ppermute | solution.py:57
  19.2 1.4 %collective-permute-start.10 = (bf16[3,64,512]{2,1,0:T(8,128)(2,1)S(1)}, bf16[3,64,512]{2,1,0:T(8,128)(2,1)S(1)}, u32[]{:S(2)}, u32[]{:S(2)}) collective-permute-start(bf16[3,64,512]{2,1,0:T(8,128)(2,1)S(1)} %collective-permute-done.4.refs_3_), channel_id=1, source_target_pairs={{0,4},{4,0},{8,12},{12,8},{16,20},{20,16},{24,28},{28,24},{1,5},{5... | collective-permute-start | bytes 589832 | tf_op jit(solution)/shard_map/down_tm_core/ppermute | solution.py:37
  20.6 0.9 %features.1 = (bf16[8,128,512]{2,1,0:T(8,128)(2,1)S(1)}, bf16[512,1024]{1,0:T(8,128)(2,1)S(1)}) custom-call(s32[1]{0:T(128)} %bitcast.meta, bf16[8,128,512]{2,1,0:T(8,128)(2,1)S(1)} %bitcast.27), custom_call_target="tpu_custom_call" | custom-call | flops 20000000000 | bytes 1000 | tf_op jit(solution)/shard_map/features/pallas_call | solution.py:280
  21.7 3.5 %backward.1 = (f32[8,128,512]{2,1,0:T(8,128)S(1)}, bf16[10,128,512]{2,1,0:T(8,128)(2,1)S(1)}, f32[2,3,64,512]{3,2,1,0:T(8,128)S(1)}, f32[2,3,64,512]{3,2,1,0:T(8...) custom-call(s32[23]{0:T(128)S(1)} %pad_add_fusion.meta, ...), custom_call_target="tpu_custom_call" | custom-call | flops 1000000 | bytes 1000 | tf_op jit(solution)/shard_map/backward/pallas_call | solution.py:280
  28.7 3.6 %forward.1 = (bf16[8,128,512]{2,1,0:T(8,128)(2,1)S(1)}, bf16[2,128,512]{2,1,0:T(8,128)(2,1)S(1)}, f32[2,3,64,512]{3,2,1,0:T(8,128)S(1)}, f32[2,3,64,512]{3,2,1,0...) custom-call(s32[23]{0:T(128)S(1)} %pad_add_fusion.meta, ...), custom_call_target="tpu_custom_call" | custom-call | flops 1000000 | bytes 1000 | tf_op jit(solution)/shard_map/forward/pallas_call | solution.py:280
  33.4 2.4 %collective-permute-done.19 = bf16[2,3,64,512]{3,2,1,0:T(8,128)(2,1)S(1)} collective-permute-done((bf16[2,3,64,512]{3,2,1,0:T(8,128)(2,1)S(1)}, bf16[2,3,64,512]{3,2,1,0:T(8,128)(2,1)S(1)}, u32[]{:S(2)}, u32[]{:S(2)}) %collective-permute-start.19) | collective-permute-done | bytes 393248 | tf_op jit(solution)/shard_map/grad_time_tm_0/ppermute | solution.py:32
  36.1 1.1 %collective-permute-start.24 = (bf16[1,3,64,512]{3,2,1,0:T(8,128)(2,1)S(1)}, bf16[1,3,64,512]{3,2,1,0:T(8,128)(2,1)S(1)}, u32[]{:S(2)}, u32[]{:S(2)}) collective-permute-start(bf16[1,3,64,512]{3,2,1,0:T(8,128)(2,1)S(1)} %slice.138), channel_id=1, source_target_pairs={{0,16},{4,12},{8,24},{12,4},{16,0},{20,28},{24,8},{28,20},{1,17},{... | collective-permute-start | bytes 589832 | tf_op jit(solution)/shard_map/grad_time_tm_1/ppermute | solution.py:32
  38.0 1.8 %collective-permute-start.23 = (bf16[2,3,32,512]{3,2,1,0:T(8,128)(2,1)S(1)}, bf16[2,3,32,512]{3,2,1,0:T(8,128)(2,1)S(1)}, u32[]{:S(2)}, u32[]{:S(2)}) collective-permute-start(bf16[2,3,32,512]{3,2,1,0:T(8,128)(2,1)S(1)} %get-tuple-element.103), channel_id=1, source_target_pairs={{0,8},{4,20},{8,0},{12,28},{16,24},{20,4},{24,16},{28,12},{1,9},{5... | collective-permute-start | bytes 589832 | tf_op jit(solution)/shard_map/grad_down0_tm_0/ppermute | solution.py:32
  39.9 4.4 %clips.1 = bf16[8,128,512]{2,1,0:T(8,128)(2,1)} custom-call(s32[23]{0:T(128)S(1)} %pad_add_fusion.meta, bf16[8,128,512]{2,1,0:T(8,128)(2,1)S(1)} %bitcast.29, f32[8,128,512]{2,1,0:T(8,128)S(1)} %get-tuple-element.85.gh, bf16[10,128,512]{2,1,0:T(8,128)(2,1)S(1)} %get-tuple-element.69.gm, bf16[3,64,512]{2,1,0:T(8,128)(2,1)S(1)} %copy-done.2, ...), custom_call_target="tpu_custom_call" | custom-call | flops 1000000 | bytes 1000 | tf_op jit(solution)/shard_map/clips/pallas_call | solution.py:280
  44.3 1.6 %collective-permute-start.28 = (bf16[3,64,512]{2,1,0:T(8,128)(2,1)S(1)}, bf16[3,64,512]{2,1,0:T(8,128)(2,1)S(1)}, u32[]{:S(2)}, u32[]{:S(2)}) collective-permute-start(bf16[3,64,512]{2,1,0:T(8,128)(2,1)S(1)} %fusion.4), channel_id=1, source_target_pairs={{0,1},{1,0},{2,3},{3,2},{4,6},{5,7},{6,4},{7,5},{8,9},{9,8},{10,11... | collective-permute-start | bytes 589832 | tf_op jit(solution)/shard_map/grad_time_group_0/ppermute | solution.py:50
  46.0 1.0 %collective-permute-start.25 = (bf16[1,3,32,512]{3,2,1,0:T(8,128)(2,1)S(1)}, bf16[1,3,32,512]{3,2,1,0:T(8,128)(2,1)S(1)}, u32[]{:S(2)}, u32[]{:S(2)}) collective-permute-start(bf16[1,3,32,512]{3,2,1,0:T(8,128)(2,1)S(1)} %slice.140), channel_id=1, source_target_pairs={{0,16},{4,12},{8,24},{12,4},{16,0},{20,28},{24,8},{28,20},{1,17},{... | collective-permute-start | bytes 294920 | tf_op jit(solution)/shard_map/grad_down0_tm_1/ppermute | solution.py:32
  47.1 1.1 %collective-permute-start.29 = (bf16[1,3,32,512]{3,2,1,0:T(8,128)(2,1)S(1)}, bf16[1,3,32,512]{3,2,1,0:T(8,128)(2,1)S(1)}, u32[]{:S(2)}, u32[]{:S(2)}) collective-permute-start(bf16[1,3,32,512]{3,2,1,0:T(8,128)(2,1)S(1)} %slice.139), channel_id=1, source_target_pairs={{0,16},{4,12},{8,24},{12,4},{16,0},{20,28},{24,8},{28,20},{1,17},{... | collective-permute-start | bytes 294920 | tf_op jit(solution)/shard_map/grad_down1_tm_1/ppermute | solution.py:32
  48.3 2.4 %collective-permute-done.25 = bf16[1,3,32,512]{3,2,1,0:T(8,128)(2,1)S(1)} collective-permute-done((bf16[1,3,32,512]{3,2,1,0:T(8,128)(2,1)S(1)}, bf16[1,3,32,512]{3,2,1,0:T(8,128)(2,1)S(1)}, u32[]{:S(2)}, u32[]{:S(2)}) %collective-permute-start.25) | collective-permute-done | bytes 98336 | tf_op jit(solution)/shard_map/grad_down0_tm_1/ppermute | solution.py:32
  50.7 1.3 %collective-permute-start.27 = (bf16[3,32,512]{2,1,0:T(8,128)(2,1)S(1)}, bf16[3,32,512]{2,1,0:T(8,128)(2,1)S(1)}, u32[]{:S(2)}, u32[]{:S(2)}) collective-permute-start(bf16[3,32,512]{2,1,0:T(8,128)(2,1)S(1)} %fusion.7), channel_id=1, source_target_pairs={{0,1},{1,0},{2,3},{3,2},{4,6},{5,7},{6,4},{7,5},{8,9},{9,8},{10,11... | collective-permute-start | bytes 294920 | tf_op jit(solution)/shard_map/grad_down0_group_0/ppermute | solution.py:50
  52.1 1.1 %collective-permute-start.30 = (bf16[3,32,512]{2,1,0:T(8,128)(2,1)S(1)}, bf16[3,32,512]{2,1,0:T(8,128)(2,1)S(1)}, u32[]{:S(2)}, u32[]{:S(2)}) collective-permute-start(bf16[3,32,512]{2,1,0:T(8,128)(2,1)S(1)} %fusion.8), channel_id=1, source_target_pairs={{0,1},{1,0},{2,3},{3,2},{4,6},{5,7},{6,4},{7,5},{8,9},{9,8},{10,11... | collective-permute-start | bytes 294920 | tf_op jit(solution)/shard_map/grad_down1_group_0/ppermute | solution.py:50
  53.2 1.6 %collective-permute-start.31 = (bf16[2,128,512]{2,1,0:T(8,128)(2,1)S(1)}, bf16[2,128,512]{2,1,0:T(8,128)(2,1)S(1)}, u32[]{:S(2)}, u32[]{:S(2)}) collective-permute-start(bf16[2,128,512]{2,1,0:T(8,128)(2,1)S(1)} %get-tuple-element.96), channel_id=1, source_target_pairs={{0,4},{4,8},{8,12},{12,16},{16,20},{20,24},{24,28},{1,5},{5,9},{9,... | collective-permute-start | bytes 786440 | tf_op jit(solution)/shard_map/halo_tm1_2/ppermute | solution.py:57
  54.8 2.4 %collective-permute-start.32 = (bf16[3,64,512]{2,1,0:T(8,128)(2,1)S(1)}, bf16[3,64,512]{2,1,0:T(8,128)(2,1)S(1)}, u32[]{:S(2)}, u32[]{:S(2)}) collective-permute-start(bf16[3,64,512]{2,1,0:T(8,128)(2,1)S(1)} %add_convert_fusion), channel_id=1, source_target_pairs={{0,2},{1,3},{2,0},{3,1},{4,5},{5,4},{6,7},{7,6},{8,10},{9,11},{10,... | collective-permute-start | bytes 589832 | tf_op jit(solution)/shard_map/grad_time_group_1/ppermute | solution.py:50
  57.5 2.8 %collective-permute-start.34 = (bf16[3,32,512]{2,1,0:T(8,128)(2,1)S(1)}, bf16[3,32,512]{2,1,0:T(8,128)(2,1)S(1)}, u32[]{:S(2)}, u32[]{:S(2)}) collective-permute-start(bf16[3,32,512]{2,1,0:T(8,128)(2,1)S(1)} %add_convert_fusion.1), channel_id=1, source_target_pairs={{0,2},{1,3},{2,0},{3,1},{4,5},{5,4},{6,7},{7,6},{8,10},{9,11},{10,... | collective-permute-start | bytes 294920 | tf_op jit(solution)/shard_map/grad_down1_group_1/ppermute | solution.py:50
  60.5 2.4 %reduced.1 = bf16[4,128,512]{2,1,0:T(8,128)(2,1)} custom-call(s32[23]{0:T(128)S(1)} %pad_add_fusion.meta, bf16[2,128,512]{2,1,0:T(8,128)(2,1)S(1)} %collective-permute-done.31.before, bf16[8,128,512]{2,1,0:T(8,128)(2,1)S(1)} %get-tuple-element.74.hidden, bf16[3,64,512]{2,1,0:T(8,128)(2,1)S(1)} %copy-done.3, ...), custom_call_target="tpu_custom_call" | custom-call | flops 1000000 | bytes 1000 | tf_op jit(solution)/shard_map/reduced/pallas_call | solution.py:280
  63.0 0.8 %convert_add_fusion = f32[3,64,512]{2,1,0:T(8,128)} fusion(bf16[3,64,512]{2,1,0:T(8,128)(2,1)S(1)} %collective-permute-done.32, bf16[3,64,512]{2,1,0:T(8,128)(2,1)S(1)} %add_convert_fusion), kind=kLoop, calls=%fused_computation.15 | loop fusion | flops 294912 | bytes 786432 | tf_op jit(solution)/shard_map/add | solution.py:408
  63.8 1.1 %collective-permute-done.34 = bf16[3,32,512]{2,1,0:T(8,128)(2,1)S(1)} collective-permute-done((bf16[3,32,512]{2,1,0:T(8,128)(2,1)S(1)}, bf16[3,32,512]{2,1,0:T(8,128)(2,1)S(1)}, u32[]{:S(2)}, u32[]{:S(2)}) %collective-permute-start.34) | collective-permute-done | bytes 98336 | tf_op jit(solution)/shard_map/grad_down1_group_1/ppermute | solution.py:50
  64.9 1.9 %collective-permute-done.33 = bf16[3,32,512]{2,1,0:T(8,128)(2,1)S(1)} collective-permute-done((bf16[3,32,512]{2,1,0:T(8,128)(2,1)S(1)}, bf16[3,32,512]{2,1,0:T(8,128)(2,1)S(1)}, u32[]{:S(2)}, u32[]{:S(2)}) %collective-permute-start.33) | collective-permute-done | bytes 98336 | tf_op jit(solution)/shard_map/grad_down0_group_1/ppermute | solution.py:50
  66.9 0.8 %pad_maximum_fusion = f32[3,64,512]{2,1,0:T(8,128)} fusion(f32[3,32,512]{2,1,0:T(8,128)S(1)} %get-tuple-element.106, f32[3,32,512]{2,1,0:T(8,128)S(1)} %get-tuple-element.107), kind=kLoop, calls=%fused_computation.14 | loop fusion | flops 98304 | bytes 786432 | tf_op jit(solution)/shard_map/concatenate | solution.py:421
  (81 shorter events, 9.4 us)
Async XLA Ops:
  0.7 11.7 %collective-permute-start.8 = (bf16[3,64,512]{2,1,0:T(8,128)(2,1)}, bf16[3,64,512]{2,1,0:T(8,128)(2,1)S(1)}, u32[]{:S(2)}, u32[]{:S(2)}) collective-permute-start(bf16[3,64,512]{2,1,0:T(8,128)(2,1)} %refs_0_.6), channel_id=1, source_target_pairs={{0,4},{4,0},{8,12},{12,8},{16,20},{20,16},{24,28},{28,24},{1,5},{5... | collective-permute-start | bytes 589832 | tf_op jit(solution)/shard_map/time_tm_core/ppermute | solution.py:37
  1.2 12.7 %collective-permute-start.3 = (bf16[3,64,512]{2,1,0:T(8,128)(2,1)}, bf16[3,64,512]{2,1,0:T(8,128)(2,1)S(1)}, u32[]{:S(2)}, u32[]{:S(2)}) collective-permute-start(bf16[3,64,512]{2,1,0:T(8,128)(2,1)} %refs_0_.6), channel_id=1, source_target_pairs={{0,8},{4,20},{8,0},{12,28},{16,24},{20,4},{24,16},{28,12},{1,9},{5... | collective-permute-start | bytes 589832 | tf_op jit(solution)/shard_map/time_tm_0/ppermute | solution.py:32
  3.7 8.5 %collective-permute-start.2 = (bf16[3,64,512]{2,1,0:T(8,128)(2,1)}, bf16[3,64,512]{2,1,0:T(8,128)(2,1)S(1)}, u32[]{:S(2)}, u32[]{:S(2)}) collective-permute-start(bf16[3,64,512]{2,1,0:T(8,128)(2,1)} %refs_0_.7), channel_id=1, source_target_pairs={{0,8},{4,20},{8,0},{12,28},{16,24},{20,4},{24,16},{28,12},{1,9},{5... | collective-permute-start | bytes 589832 | tf_op jit(solution)/shard_map/down_tm_0/ppermute | solution.py:32
  3.8 7.8 %collective-permute-start.1 = (bf16[3,64,512]{2,1,0:T(8,128)(2,1)}, bf16[3,64,512]{2,1,0:T(8,128)(2,1)S(1)}, u32[]{:S(2)}, u32[]{:S(2)}) collective-permute-start(bf16[3,64,512]{2,1,0:T(8,128)(2,1)} %refs_0_.7), channel_id=1, source_target_pairs={{0,16},{4,12},{8,24},{12,4},{16,0},{20,28},{24,8},{28,20},{1,17},{... | collective-permute-start | bytes 589832 | tf_op jit(solution)/shard_map/down_own_tm_1/ppermute | solution.py:32
  6.8 7.3 %collective-permute-start = (bf16[2,128,512]{2,1,0:T(8,128)(2,1)S(1)}, bf16[2,128,512]{2,1,0:T(8,128)(2,1)S(1)}, u32[]{:S(2)}, u32[]{:S(2)}) collective-permute-start(bf16[2,128,512]{2,1,0:T(8,128)(2,1)S(1)} %slice_bitcast_fusion.1), channel_id=1, source_target_pairs={{4,0},{8,4},{12,8},{16,12},{20,16},{24,20},{28,24},{5,1},{9,5},{13... | collective-permute-start | bytes 786440 | tf_op jit(solution)/shard_map/halo_tm-1_2/ppermute | solution.py:57
  11.6 2.9 %collective-permute-start.5 = (bf16[3,64,512]{2,1,0:T(8,128)(2,1)S(1)}, bf16[3,64,512]{2,1,0:T(8,128)(2,1)S(1)}, u32[]{:S(2)}, u32[]{:S(2)}) collective-permute-start(bf16[3,64,512]{2,1,0:T(8,128)(2,1)S(1)} %copy-done.3), channel_id=1, source_target_pairs={{0,4},{4,0},{8,12},{12,8},{16,20},{20,16},{24,28},{28,24},{1,5},{5... | collective-permute-start | bytes 589832 | tf_op jit(solution)/shard_map/down_tm_core/ppermute | solution.py:37
  12.2 6.9 %collective-permute-start.6 = (bf16[3,64,512]{2,1,0:T(8,128)(2,1)S(1)}, bf16[3,64,512]{2,1,0:T(8,128)(2,1)S(1)}, u32[]{:S(2)}, u32[]{:S(2)}) collective-permute-start(bf16[3,64,512]{2,1,0:T(8,128)(2,1)S(1)} %collective-permute-done.2.refs_1_), channel_id=1, source_target_pairs={{0,4},{4,0},{8,12},{12,8},{16,20},{20,16},{24,28},{28,24},{1,5},{5... | collective-permute-start | bytes 589832 | tf_op jit(solution)/shard_map/down_tm_core/ppermute | solution.py:37
  12.3 6.8 %collective-permute-start.4 = (bf16[3,64,512]{2,1,0:T(8,128)(2,1)S(1)}, bf16[3,64,512]{2,1,0:T(8,128)(2,1)S(1)}, u32[]{:S(2)}, u32[]{:S(2)}) collective-permute-start(bf16[3,64,512]{2,1,0:T(8,128)(2,1)S(1)} %collective-permute-done.2.refs_1_), channel_id=1, source_target_pairs={{0,16},{4,12},{8,24},{12,4},{16,0},{20,28},{24,8},{28,20},{1,17},{... | collective-permute-start | bytes 589832 | tf_op jit(solution)/shard_map/down_tm_1/ppermute | solution.py:32
  13.9 5.3 %collective-permute-start.7 = (bf16[3,64,512]{2,1,0:T(8,128)(2,1)S(1)}, bf16[3,64,512]{2,1,0:T(8,128)(2,1)S(1)}, u32[]{:S(2)}, u32[]{:S(2)}) collective-permute-start(bf16[3,64,512]{2,1,0:T(8,128)(2,1)S(1)} %collective-permute-done.1.refs_2_), channel_id=1, source_target_pairs={{0,4},{4,0},{8,12},{12,8},{16,20},{20,16},{24,28},{28,24},{1,5},{5... | collective-permute-start | bytes 589832 | tf_op jit(solution)/shard_map/down_tm_core/ppermute | solution.py:37
  14.1 2.5 %collective-permute-start.9 = (bf16[3,64,512]{2,1,0:T(8,128)(2,1)S(1)}, bf16[3,64,512]{2,1,0:T(8,128)(2,1)S(1)}, u32[]{:S(2)}, u32[]{:S(2)}) collective-permute-start(bf16[3,64,512]{2,1,0:T(8,128)(2,1)S(1)} %collective-permute-done.3.refs_1_), channel_id=1, source_target_pairs={{0,4},{4,0},{8,12},{12,8},{16,20},{20,16},{24,28},{28,24},{1,5},{5... | collective-permute-start | bytes 589832 | tf_op jit(solution)/shard_map/time_tm_core/ppermute | solution.py:37
  14.5 11.7 %collective-permute-start.16 = (bf16[2,3,64,512]{3,2,1,0:T(8,128)(2,1)S(1)}, bf16[2,3,64,512]{3,2,1,0:T(8,128)(2,1)S(1)}, u32[]{:S(2)}, u32[]{:S(2)}) collective-permute-start(bf16[2,3,64,512]{3,2,1,0:T(8,128)(2,1)S(1)} %bitcast_dynamic-update-slice_fusion), channel_id=1, source_target_pairs={{0,16},{4,12},{8,24},{12,4},{16,0},{20,28},{24,8},{28,20},{1,17},{... | collective-permute-start | bytes 1179656 | tf_op jit(solution)/shard_map/time_tm_1/ppermute | solution.py:32
  16.6 9.7 %collective-permute-start.12 = (bf16[2,128,512]{2,1,0:T(8,128)(2,1)S(1)}, bf16[2,128,512]{2,1,0:T(8,128)(2,1)S(1)}, u32[]{:S(2)}, u32[]{:S(2)}) collective-permute-start(bf16[2,128,512]{2,1,0:T(8,128)(2,1)S(1)} %slice_bitcast_fusion), channel_id=1, source_target_pairs={{0,4},{4,8},{8,12},{12,16},{16,20},{20,24},{24,28},{1,5},{5,9},{9,... | collective-permute-start | bytes 786440 | tf_op jit(solution)/shard_map/halo_tm1_2/ppermute | solution.py:57
  19.2 2.5 %collective-permute-start.10 = (bf16[3,64,512]{2,1,0:T(8,128)(2,1)S(1)}, bf16[3,64,512]{2,1,0:T(8,128)(2,1)S(1)}, u32[]{:S(2)}, u32[]{:S(2)}) collective-permute-start(bf16[3,64,512]{2,1,0:T(8,128)(2,1)S(1)} %collective-permute-done.4.refs_3_), channel_id=1, source_target_pairs={{0,4},{4,0},{8,12},{12,8},{16,20},{20,16},{24,28},{28,24},{1,5},{5... | collective-permute-start | bytes 589832 | tf_op jit(solution)/shard_map/down_tm_core/ppermute | solution.py:37
  25.8 1.6 %collective-permute-start.14 = (bf16[3,64,512]{2,1,0:T(8,128)(2,1)S(1)}, bf16[3,64,512]{2,1,0:T(8,128)(2,1)S(1)}, u32[]{:S(2)}, u32[]{:S(2)}) collective-permute-start(bf16[3,64,512]{2,1,0:T(8,128)(2,1)S(1)} %get-tuple-element.64), channel_id=1, source_target_pairs={{0,4},{4,0},{8,12},{12,8},{16,20},{20,16},{24,28},{28,24},{1,5},{5... | collective-permute-start | bytes 589832 | tf_op jit(solution)/shard_map/grad_time_tm_core/ppermute | solution.py:37
  26.3 2.3 %collective-permute-start.17 = (bf16[2,3,64,512]{3,2,1,0:T(8,128)(2,1)S(1)}, bf16[2,3,64,512]{3,2,1,0:T(8,128)(2,1)S(1)}, u32[]{:S(2)}, u32[]{:S(2)}) collective-permute-start(bf16[2,3,64,512]{3,2,1,0:T(8,128)(2,1)S(1)} %collective-permute-done.16.refs_2_), channel_id=1, source_target_pairs={{0,4},{4,0},{8,12},{12,8},{16,20},{20,16},{24,28},{28,24},{1,5},{5... | collective-permute-start | bytes 1179656 | tf_op jit(solution)/shard_map/time_tm_core/ppermute | solution.py:37
  28.0 7.8 %collective-permute-start.19 = (bf16[2,3,64,512]{3,2,1,0:T(8,128)(2,1)S(1)}, bf16[2,3,64,512]{3,2,1,0:T(8,128)(2,1)S(1)}, u32[]{:S(2)}, u32[]{:S(2)}) collective-permute-start(bf16[2,3,64,512]{3,2,1,0:T(8,128)(2,1)S(1)} %fusion.2), channel_id=1, source_target_pairs={{0,8},{4,20},{8,0},{12,28},{16,24},{20,4},{24,16},{28,12},{1,9},{5... | collective-permute-start | bytes 1179656 | tf_op jit(solution)/shard_map/grad_time_tm_0/ppermute | solution.py:32
  32.3 4.9 %collective-permute-start.18 = (bf16[3,64,512]{2,1,0:T(8,128)(2,1)S(1)}, bf16[3,64,512]{2,1,0:T(8,128)(2,1)S(1)}, u32[]{:S(2)}, u32[]{:S(2)}) collective-permute-start(bf16[3,64,512]{2,1,0:T(8,128)(2,1)S(1)} %get-tuple-element.72), channel_id=1, source_target_pairs={{0,4},{4,0},{8,12},{12,8},{16,20},{20,16},{24,28},{28,24},{1,5},{5... | collective-permute-start | bytes 589832 | tf_op jit(solution)/shard_map/grad_down_tm_core/ppermute | solution.py:37
  32.8 4.4 %collective-permute-start.20 = (bf16[3,64,512]{2,1,0:T(8,128)(2,1)S(1)}, bf16[3,64,512]{2,1,0:T(8,128)(2,1)S(1)}, u32[]{:S(2)}, u32[]{:S(2)}) collective-permute-start(bf16[3,64,512]{2,1,0:T(8,128)(2,1)S(1)} %get-tuple-element.77), channel_id=1, source_target_pairs={{0,4},{4,0},{8,12},{12,8},{16,20},{20,16},{24,28},{28,24},{1,5},{5... | collective-permute-start | bytes 589832 | tf_op jit(solution)/shard_map/grad_down_tm_core/ppermute | solution.py:37
  32.9 4.3 %collective-permute-start.21 = (bf16[3,64,512]{2,1,0:T(8,128)(2,1)S(1)}, bf16[3,64,512]{2,1,0:T(8,128)(2,1)S(1)}, u32[]{:S(2)}, u32[]{:S(2)}) collective-permute-start(bf16[3,64,512]{2,1,0:T(8,128)(2,1)S(1)} %get-tuple-element.79), channel_id=1, source_target_pairs={{0,4},{4,0},{8,12},{12,8},{16,20},{20,16},{24,28},{28,24},{1,5},{5... | collective-permute-start | bytes 589832 | tf_op jit(solution)/shard_map/grad_down_tm_core/ppermute | solution.py:37
  33.3 3.9 %collective-permute-start.22 = (bf16[3,64,512]{2,1,0:T(8,128)(2,1)S(1)}, bf16[3,64,512]{2,1,0:T(8,128)(2,1)S(1)}, u32[]{:S(2)}, u32[]{:S(2)}) collective-permute-start(bf16[3,64,512]{2,1,0:T(8,128)(2,1)S(1)} %get-tuple-element.81), channel_id=1, source_target_pairs={{0,4},{4,0},{8,12},{12,8},{16,20},{20,16},{24,28},{28,24},{1,5},{5... | collective-permute-start | bytes 589832 | tf_op jit(solution)/shard_map/grad_down_tm_core/ppermute | solution.py:37
  36.1 8.2 %collective-permute-start.24 = (bf16[1,3,64,512]{3,2,1,0:T(8,128)(2,1)S(1)}, bf16[1,3,64,512]{3,2,1,0:T(8,128)(2,1)S(1)}, u32[]{:S(2)}, u32[]{:S(2)}) collective-permute-start(bf16[1,3,64,512]{3,2,1,0:T(8,128)(2,1)S(1)} %slice.138), channel_id=1, source_target_pairs={{0,16},{4,12},{8,24},{12,4},{16,0},{20,28},{24,8},{28,20},{1,17},{... | collective-permute-start | bytes 589832 | tf_op jit(solution)/shard_map/grad_time_tm_1/ppermute | solution.py:32
  37.8 9.3 %collective-permute-start.26 = (bf16[2,3,32,512]{3,2,1,0:T(8,128)(2,1)S(1)}, bf16[2,3,32,512]{3,2,1,0:T(8,128)(2,1)S(1)}, u32[]{:S(2)}, u32[]{:S(2)}) collective-permute-start(bf16[2,3,32,512]{3,2,1,0:T(8,128)(2,1)S(1)} %get-tuple-element.102), channel_id=1, source_target_pairs={{0,8},{4,20},{8,0},{12,28},{16,24},{20,4},{24,16},{28,12},{1,9},{5... | collective-permute-start | bytes 589832 | tf_op jit(solution)/shard_map/grad_down1_tm_0/ppermute | solution.py:32
  38.0 7.9 %collective-permute-start.23 = (bf16[2,3,32,512]{3,2,1,0:T(8,128)(2,1)S(1)}, bf16[2,3,32,512]{3,2,1,0:T(8,128)(2,1)S(1)}, u32[]{:S(2)}, u32[]{:S(2)}) collective-permute-start(bf16[2,3,32,512]{3,2,1,0:T(8,128)(2,1)S(1)} %get-tuple-element.103), channel_id=1, source_target_pairs={{0,8},{4,20},{8,0},{12,28},{16,24},{20,4},{24,16},{28,12},{1,9},{5... | collective-permute-start | bytes 589832 | tf_op jit(solution)/shard_map/grad_down0_tm_0/ppermute | solution.py:32
  44.3 10.5 %collective-permute-start.28 = (bf16[3,64,512]{2,1,0:T(8,128)(2,1)S(1)}, bf16[3,64,512]{2,1,0:T(8,128)(2,1)S(1)}, u32[]{:S(2)}, u32[]{:S(2)}) collective-permute-start(bf16[3,64,512]{2,1,0:T(8,128)(2,1)S(1)} %fusion.4), channel_id=1, source_target_pairs={{0,1},{1,0},{2,3},{3,2},{4,6},{5,7},{6,4},{7,5},{8,9},{9,8},{10,11... | collective-permute-start | bytes 589832 | tf_op jit(solution)/shard_map/grad_time_group_0/ppermute | solution.py:50
  46.0 4.7 %collective-permute-start.25 = (bf16[1,3,32,512]{3,2,1,0:T(8,128)(2,1)S(1)}, bf16[1,3,32,512]{3,2,1,0:T(8,128)(2,1)S(1)}, u32[]{:S(2)}, u32[]{:S(2)}) collective-permute-start(bf16[1,3,32,512]{3,2,1,0:T(8,128)(2,1)S(1)} %slice.140), channel_id=1, source_target_pairs={{0,16},{4,12},{8,24},{12,4},{16,0},{20,28},{24,8},{28,20},{1,17},{... | collective-permute-start | bytes 294920 | tf_op jit(solution)/shard_map/grad_down0_tm_1/ppermute | solution.py:32
  47.1 4.9 %collective-permute-start.29 = (bf16[1,3,32,512]{3,2,1,0:T(8,128)(2,1)S(1)}, bf16[1,3,32,512]{3,2,1,0:T(8,128)(2,1)S(1)}, u32[]{:S(2)}, u32[]{:S(2)}) collective-permute-start(bf16[1,3,32,512]{3,2,1,0:T(8,128)(2,1)S(1)} %slice.139), channel_id=1, source_target_pairs={{0,16},{4,12},{8,24},{12,4},{16,0},{20,28},{24,8},{28,20},{1,17},{... | collective-permute-start | bytes 294920 | tf_op jit(solution)/shard_map/grad_down1_tm_1/ppermute | solution.py:32
  50.7 6.5 %collective-permute-start.27 = (bf16[3,32,512]{2,1,0:T(8,128)(2,1)S(1)}, bf16[3,32,512]{2,1,0:T(8,128)(2,1)S(1)}, u32[]{:S(2)}, u32[]{:S(2)}) collective-permute-start(bf16[3,32,512]{2,1,0:T(8,128)(2,1)S(1)} %fusion.7), channel_id=1, source_target_pairs={{0,1},{1,0},{2,3},{3,2},{4,6},{5,7},{6,4},{7,5},{8,9},{9,8},{10,11... | collective-permute-start | bytes 294920 | tf_op jit(solution)/shard_map/grad_down0_group_0/ppermute | solution.py:50
  52.1 5.4 %collective-permute-start.30 = (bf16[3,32,512]{2,1,0:T(8,128)(2,1)S(1)}, bf16[3,32,512]{2,1,0:T(8,128)(2,1)S(1)}, u32[]{:S(2)}, u32[]{:S(2)}) collective-permute-start(bf16[3,32,512]{2,1,0:T(8,128)(2,1)S(1)} %fusion.8), channel_id=1, source_target_pairs={{0,1},{1,0},{2,3},{3,2},{4,6},{5,7},{6,4},{7,5},{8,9},{9,8},{10,11... | collective-permute-start | bytes 294920 | tf_op jit(solution)/shard_map/grad_down1_group_0/ppermute | solution.py:50
  53.2 7.4 %collective-permute-start.31 = (bf16[2,128,512]{2,1,0:T(8,128)(2,1)S(1)}, bf16[2,128,512]{2,1,0:T(8,128)(2,1)S(1)}, u32[]{:S(2)}, u32[]{:S(2)}) collective-permute-start(bf16[2,128,512]{2,1,0:T(8,128)(2,1)S(1)} %get-tuple-element.96), channel_id=1, source_target_pairs={{0,4},{4,8},{8,12},{12,16},{16,20},{20,24},{24,28},{1,5},{5,9},{9,... | collective-permute-start | bytes 786440 | tf_op jit(solution)/shard_map/halo_tm1_2/ppermute | solution.py:57
  54.8 8.1 %collective-permute-start.32 = (bf16[3,64,512]{2,1,0:T(8,128)(2,1)S(1)}, bf16[3,64,512]{2,1,0:T(8,128)(2,1)S(1)}, u32[]{:S(2)}, u32[]{:S(2)}) collective-permute-start(bf16[3,64,512]{2,1,0:T(8,128)(2,1)S(1)} %add_convert_fusion), channel_id=1, source_target_pairs={{0,2},{1,3},{2,0},{3,1},{4,5},{5,4},{6,7},{7,6},{8,10},{9,11},{10,... | collective-permute-start | bytes 589832 | tf_op jit(solution)/shard_map/grad_time_group_1/ppermute | solution.py:50
  57.5 7.3 %collective-permute-start.34 = (bf16[3,32,512]{2,1,0:T(8,128)(2,1)S(1)}, bf16[3,32,512]{2,1,0:T(8,128)(2,1)S(1)}, u32[]{:S(2)}, u32[]{:S(2)}) collective-permute-start(bf16[3,32,512]{2,1,0:T(8,128)(2,1)S(1)} %add_convert_fusion.1), channel_id=1, source_target_pairs={{0,2},{1,3},{2,0},{3,1},{4,5},{5,4},{6,7},{7,6},{8,10},{9,11},{10,... | collective-permute-start | bytes 294920 | tf_op jit(solution)/shard_map/grad_down1_group_1/ppermute | solution.py:50
  60.3 6.5 %collective-permute-start.33 = (bf16[3,32,512]{2,1,0:T(8,128)(2,1)S(1)}, bf16[3,32,512]{2,1,0:T(8,128)(2,1)S(1)}, u32[]{:S(2)}, u32[]{:S(2)}) collective-permute-start(bf16[3,32,512]{2,1,0:T(8,128)(2,1)S(1)} %add_convert_fusion.2), channel_id=1, source_target_pairs={{0,2},{1,3},{2,0},{3,1},{4,5},{5,4},{6,7},{7,6},{8,10},{9,11},{10,... | collective-permute-start | bytes 294920 | tf_op jit(solution)/shard_map/grad_down0_group_1/ppermute | solution.py:50
  (7 other events, 37.4 us)

commit v7 on v6

--- a/solution.py
+++ b/solution.py
@@ -302,14 +302,15 @@
         down = down + [exchange(part, step, "down") for part in down]
         time = time + [exchange(part, step, "time") for part in time]
     down_own = exchange(w_down, last, "down_own")
-    cot_next = shifted(cot[:2], "tm", -1)
+    rims = lax.optimization_barrier(jnp.concatenate([cot[:2], x[frames - 2:]]))
+    cot_next = shifted(rims[:2], "tm", -1)
     down_late = [exchange(part, last, "down") for part in down[1:]]
     time_late = after(jnp.pad(w_time[None], ((0, early - 1), (0, 0), (0, 0), (0, 0))), down_own)
     for i in range(1, early):
         time_late = lax.dynamic_update_slice(time_late, time[i][None], (i, 0, 0, 0))
     first = [cot_next, down_own] + down[1:] + time[1:]
     time_late = after(time_late, cot_next, *down)
-    x_before = shifted(after(x[frames - 2:], time_late), "tm", 1)
+    x_before = shifted(after(rims[2:], time_late), "tm", 1)
     time_late = exchange(time_late, last, "time")
     down = down + [down_own]
     down_other = [core_swap(part, "down") for part in down]

time: 68 us -> 67.8 us (level)
  waiting for transfers between devices: 9.84 us -> 12.3 us
  local copies, waits for them, and re-layouts: 3.14 us -> 1.25 us
    ppermute x11, waiting for transfers between devices: 5.41 us -> 7.85 us  [exchange(): return lax.ppermute(value, 'tm', route)]
    pad x1, local copies, waits for them, and re-layouts: 0.96 us -> 0.03 us  [shards(): jnp.pad(w_time[None], ((0, early - 1), (0, 0), (0, 0), (0, 0)))]
    slice x2, local copies, waits for them, and re-layouts: 1.94 us -> 1.1 us  [the longest x1 1.07 us: shards(): rims = lax.optimization_barrier(jnp.concatenate([cot[:2], x[frames - 2:]]))]
  transfers between devices with their start and end apart: 35 -> 35, of which waited for: 10 -> 11; matrix products, arithmetic and copies ran while one was open for 9% -> 6% of each run, Pallas kernels for 22% -> 22%
where the time goes in v7:
time: 67.8 us; the launch traced here: 67.6 us
  starting transfers between devices  34.9 us (51%)
  Pallas kernels  14.8 us (22%)
  waiting for transfers between devices  12.3 us (18%)
  other arithmetic  3.37 us (5%)
  local copies, waits for them, and re-layouts  1.25 us (2%)
  between operations  0.96 us (1%)
    pallas_call x5, Pallas kernels, call(): pl.pallas_call(kernel, in_specs=[SMEM] + [VMEM] * (len(inputs) - 1), out_...  14.8 us
    ppermute x11, starting transfers between devices, exchange(): return lax.ppermute(value, 'tm', route)  14.2 us
    ppermute x6, starting transfers between devices, group_exchange(): return lax.ppermute(value, ('tm', 'group'), route)  9.46 us
    ppermute x11, waiting for transfers between devices, exchange(): return lax.ppermute(value, 'tm', route)  7.85 us
    ppermute x15, starting transfers between devices, core_swap(): lax.ppermute(value, 'tm', [(i, i ^ 1) for i in range(lax.axis_size('tm'))])  5.67 us
    ppermute x3, starting transfers between devices, shifted(): return lax.ppermute(block, axis, route)  5.58 us
    ppermute x6, waiting for transfers between devices, group_exchange(): return lax.ppermute(value, ('tm', 'group'), route)  3.29 us
  transfers between devices with their start and end apart: 35, of which 11 were waited for; matrix products, arithmetic and copies ran while one was open for 6% of the time, Pallas kernels for 22%

profile of v7, /device:TPU:0, one launch (start us, length us, event | category | flops | bytes accessed | tf_op | source)
XLA Modules:
  0.0 67.6 jit_solution(5456278105109392743)
XLA Ops:
  1.2 2.6 %collective-permute-start.3 = (bf16[3,64,512]{2,1,0:T(8,128)(2,1)}, bf16[3,64,512]{2,1,0:T(8,128)(2,1)S(1)}, u32[]{:S(2)}, u32[]{:S(2)}) collective-permute-start(bf16[3,64,512]{2,1,0:T(8,128)(2,1)} %refs_0_.6), channel_id=1, source_target_pairs={{0,8},{4,20},{8,0},{12,28},{16,24},{20,4},{24,16},{28,12},{1,9},{5... | collective-permute-start | bytes 589832 | tf_op jit(solution)/shard_map/time_tm_0/ppermute | solution.py:32
  3.8 2.0 %collective-permute-start.1 = (bf16[3,64,512]{2,1,0:T(8,128)(2,1)}, bf16[3,64,512]{2,1,0:T(8,128)(2,1)S(1)}, u32[]{:S(2)}, u32[]{:S(2)}) collective-permute-start(bf16[3,64,512]{2,1,0:T(8,128)(2,1)} %refs_0_.7), channel_id=1, source_target_pairs={{0,16},{4,12},{8,24},{12,4},{16,0},{20,28},{24,8},{28,20},{1,17},{... | collective-permute-start | bytes 589832 | tf_op jit(solution)/shard_map/down_own_tm_1/ppermute | solution.py:32
  5.8 1.1 %slice_bitcast_fusion = (bf16[2,128,512]{2,1,0:T(8,128)(2,1)S(1)}, bf16[2,128,512]{2,1,0:T(8,128)(2,1)S(1)}) fusion(bf16[1,8,128,512]{3,2,1,0:T(8,128)(2,1)} %param.5, bf16[1,4,128,512]{3,2,1,0:T(8,128)(2,1)} %param.9), kind=kLoop, calls=%fused_computation.18 | loop fusion | bytes 1048576 | tf_op jit(solution)/shard_map/slice | solution.py:305
  7.0 1.4 %collective-permute-start = (bf16[2,128,512]{2,1,0:T(8,128)(2,1)S(1)}, bf16[2,128,512]{2,1,0:T(8,128)(2,1)S(1)}, u32[]{:S(2)}, u32[]{:S(2)}) collective-permute-start(bf16[2,128,512]{2,1,0:T(8,128)(2,1)S(1)} %get-tuple-element.103), channel_id=1, source_target_pairs={{4,0},{8,4},{12,8},{16,12},{20,16},{24,20},{28,24},{5,1},{9,5},{13... | collective-permute-start | bytes 786440 | tf_op jit(solution)/shard_map/halo_tm-1_2/ppermute | solution.py:57
  8.8 2.7 %collective-permute-done.1.refs_2_ = bf16[3,64,512]{2,1,0:T(8,128)(2,1)S(1)} collective-permute-done((bf16[3,64,512]{2,1,0:T(8,128)(2,1)}, bf16[3,64,512]{2,1,0:T(8,128)(2,1)S(1)}, u32[]{:S(2)}, u32[]{:S(2)}) %collective-permute-start.1) | collective-permute-done | bytes 196640 | tf_op jit(solution)/shard_map/down_own_tm_1/ppermute | solution.py:32
  12.1 1.8 %collective-permute-start.4 = (bf16[3,64,512]{2,1,0:T(8,128)(2,1)S(1)}, bf16[3,64,512]{2,1,0:T(8,128)(2,1)S(1)}, u32[]{:S(2)}, u32[]{:S(2)}) collective-permute-start(bf16[3,64,512]{2,1,0:T(8,128)(2,1)S(1)} %collective-permute-done.2.refs_1_), channel_id=1, source_target_pairs={{0,16},{4,12},{8,24},{12,4},{16,0},{20,28},{24,8},{28,20},{1,17},{... | collective-permute-start | bytes 589832 | tf_op jit(solution)/shard_map/down_tm_1/ppermute | solution.py:32
  14.1 0.6 collective-permute-start.9
  14.7 1.9 %collective-permute-start.16 = (bf16[2,3,64,512]{3,2,1,0:T(8,128)(2,1)S(1)}, bf16[2,3,64,512]{3,2,1,0:T(8,128)(2,1)S(1)}, u32[]{:S(2)}, u32[]{:S(2)}) collective-permute-start(bf16[2,3,64,512]{3,2,1,0:T(8,128)(2,1)S(1)} %bitcast_dynamic-update-slice_fusion), channel_id=1, source_target_pairs={{0,16},{4,12},{8,24},{12,4},{16,0},{20,28},{24,8},{28,20},{1,17},{... | collective-permute-start | bytes 1179656 | tf_op jit(solution)/shard_map/time_tm_1/ppermute | solution.py:32
  16.6 2.6 %collective-permute-start.12 = (bf16[2,128,512]{2,1,0:T(8,128)(2,1)S(1)}, bf16[2,128,512]{2,1,0:T(8,128)(2,1)S(1)}, u32[]{:S(2)}, u32[]{:S(2)}) collective-permute-start(bf16[2,128,512]{2,1,0:T(8,128)(2,1)S(1)} %get-tuple-element.60), channel_id=1, source_target_pairs={{0,4},{4,8},{8,12},{12,16},{16,20},{20,24},{24,28},{1,5},{5,9},{9,... | collective-permute-start | bytes 786440 | tf_op jit(solution)/shard_map/halo_tm1_2/ppermute | solution.py:57
  19.2 1.4 %collective-permute-start.10 = (bf16[3,64,512]{2,1,0:T(8,128)(2,1)S(1)}, bf16[3,64,512]{2,1,0:T(8,128)(2,1)S(1)}, u32[]{:S(2)}, u32[]{:S(2)}) collective-permute-start(bf16[3,64,512]{2,1,0:T(8,128)(2,1)S(1)} %collective-permute-done.4.refs_3_), channel_id=1, source_target_pairs={{0,4},{4,0},{8,12},{12,8},{16,20},{20,16},{24,28},{28,24},{1,5},{5... | collective-permute-start | bytes 589832 | tf_op jit(solution)/shard_map/down_tm_core/ppermute | solution.py:37
  20.6 0.9 %features.1 = (bf16[8,128,512]{2,1,0:T(8,128)(2,1)S(1)}, bf16[512,1024]{1,0:T(8,128)(2,1)S(1)}) custom-call(s32[1]{0:T(128)} %bitcast.meta, bf16[8,128,512]{2,1,0:T(8,128)(2,1)S(1)} %bitcast.27), custom_call_target="tpu_custom_call" | custom-call | flops 20000000000 | bytes 1000 | tf_op jit(solution)/shard_map/features/pallas_call | solution.py:280
  21.7 3.5 %backward.1 = (f32[8,128,512]{2,1,0:T(8,128)S(1)}, bf16[10,128,512]{2,1,0:T(8,128)(2,1)S(1)}, f32[2,3,64,512]{3,2,1,0:T(8,128)S(1)}, f32[2,3,64,512]{3,2,1,0:T(8...) custom-call(s32[23]{0:T(128)S(1)} %pad_add_fusion.meta, ...), custom_call_target="tpu_custom_call" | custom-call | flops 1000000 | bytes 1000 | tf_op jit(solution)/shard_map/backward/pallas_call | solution.py:280
  28.0 0.6 collective-permute-start.19
  28.6 3.6 %forward.1 = (bf16[8,128,512]{2,1,0:T(8,128)(2,1)S(1)}, bf16[2,128,512]{2,1,0:T(8,128)(2,1)S(1)}, f32[2,3,64,512]{3,2,1,0:T(8,128)S(1)}, f32[2,3,64,512]{3,2,1,0...) custom-call(s32[23]{0:T(128)S(1)} %pad_add_fusion.meta, ...), custom_call_target="tpu_custom_call" | custom-call | flops 1000000 | bytes 1000 | tf_op jit(solution)/shard_map/forward/pallas_call | solution.py:280
  33.4 2.4 %collective-permute-done.19 = bf16[2,3,64,512]{3,2,1,0:T(8,128)(2,1)S(1)} collective-permute-done((bf16[2,3,64,512]{3,2,1,0:T(8,128)(2,1)S(1)}, bf16[2,3,64,512]{3,2,1,0:T(8,128)(2,1)S(1)}, u32[]{:S(2)}, u32[]{:S(2)}) %collective-permute-start.19) | collective-permute-done | bytes 393248 | tf_op jit(solution)/shard_map/grad_time_tm_0/ppermute | solution.py:32
  36.1 1.1 %collective-permute-start.24 = (bf16[1,3,64,512]{3,2,1,0:T(8,128)(2,1)S(1)}, bf16[1,3,64,512]{3,2,1,0:T(8,128)(2,1)S(1)}, u32[]{:S(2)}, u32[]{:S(2)}) collective-permute-start(bf16[1,3,64,512]{3,2,1,0:T(8,128)(2,1)S(1)} %slice.148), channel_id=1, source_target_pairs={{0,16},{4,12},{8,24},{12,4},{16,0},{20,28},{24,8},{28,20},{1,17},{... | collective-permute-start | bytes 589832 | tf_op jit(solution)/shard_map/grad_time_tm_1/ppermute | solution.py:32
  38.0 1.9 %collective-permute-start.23 = (bf16[2,3,32,512]{3,2,1,0:T(8,128)(2,1)S(1)}, bf16[2,3,32,512]{3,2,1,0:T(8,128)(2,1)S(1)}, u32[]{:S(2)}, u32[]{:S(2)}) collective-permute-start(bf16[2,3,32,512]{3,2,1,0:T(8,128)(2,1)S(1)} %get-tuple-element.105), channel_id=1, source_target_pairs={{0,8},{4,20},{8,0},{12,28},{16,24},{20,4},{24,16},{28,12},{1,9},{5... | collective-permute-start | bytes 589832 | tf_op jit(solution)/shard_map/grad_down0_tm_0/ppermute | solution.py:32
  39.9 4.4 %clips.1 = bf16[8,128,512]{2,1,0:T(8,128)(2,1)} custom-call(s32[23]{0:T(128)S(1)} %pad_add_fusion.meta, bf16[8,128,512]{2,1,0:T(8,128)(2,1)S(1)} %bitcast.29, f32[8,128,512]{2,1,0:T(8,128)S(1)} %get-tuple-element.85.gh, bf16[10,128,512]{2,1,0:T(8,128)(2,1)S(1)} %get-tuple-element.69.gm, bf16[3,64,512]{2,1,0:T(8,128)(2,1)S(1)} %copy-done.2, ...), custom_call_target="tpu_custom_call" | custom-call | flops 1000000 | bytes 1000 | tf_op jit(solution)/shard_map/clips/pallas_call | solution.py:280
  44.3 1.6 %collective-permute-start.28 = (bf16[3,64,512]{2,1,0:T(8,128)(2,1)S(1)}, bf16[3,64,512]{2,1,0:T(8,128)(2,1)S(1)}, u32[]{:S(2)}, u32[]{:S(2)}) collective-permute-start(bf16[3,64,512]{2,1,0:T(8,128)(2,1)S(1)} %fusion.4), channel_id=1, source_target_pairs={{0,1},{1,0},{2,3},{3,2},{4,6},{5,7},{6,4},{7,5},{8,9},{9,8},{10,11... | collective-permute-start | bytes 589832 | tf_op jit(solution)/shard_map/grad_time_group_0/ppermute | solution.py:50
  46.0 1.0 %collective-permute-start.25 = (bf16[1,3,32,512]{3,2,1,0:T(8,128)(2,1)S(1)}, bf16[1,3,32,512]{3,2,1,0:T(8,128)(2,1)S(1)}, u32[]{:S(2)}, u32[]{:S(2)}) collective-permute-start(bf16[1,3,32,512]{3,2,1,0:T(8,128)(2,1)S(1)} %slice.150), channel_id=1, source_target_pairs={{0,16},{4,12},{8,24},{12,4},{16,0},{20,28},{24,8},{28,20},{1,17},{... | collective-permute-start | bytes 294920 | tf_op jit(solution)/shard_map/grad_down0_tm_1/ppermute | solution.py:32
  47.1 1.1 %collective-permute-start.29 = (bf16[1,3,32,512]{3,2,1,0:T(8,128)(2,1)S(1)}, bf16[1,3,32,512]{3,2,1,0:T(8,128)(2,1)S(1)}, u32[]{:S(2)}, u32[]{:S(2)}) collective-permute-start(bf16[1,3,32,512]{3,2,1,0:T(8,128)(2,1)S(1)} %slice.149), channel_id=1, source_target_pairs={{0,16},{4,12},{8,24},{12,4},{16,0},{20,28},{24,8},{28,20},{1,17},{... | collective-permute-start | bytes 294920 | tf_op jit(solution)/shard_map/grad_down1_tm_1/ppermute | solution.py:32
  48.2 2.4 %collective-permute-done.25 = bf16[1,3,32,512]{3,2,1,0:T(8,128)(2,1)S(1)} collective-permute-done((bf16[1,3,32,512]{3,2,1,0:T(8,128)(2,1)S(1)}, bf16[1,3,32,512]{3,2,1,0:T(8,128)(2,1)S(1)}, u32[]{:S(2)}, u32[]{:S(2)}) %collective-permute-start.25) | collective-permute-done | bytes 98336 | tf_op jit(solution)/shard_map/grad_down0_tm_1/ppermute | solution.py:32
  50.7 1.3 %collective-permute-start.27 = (bf16[3,32,512]{2,1,0:T(8,128)(2,1)S(1)}, bf16[3,32,512]{2,1,0:T(8,128)(2,1)S(1)}, u32[]{:S(2)}, u32[]{:S(2)}) collective-permute-start(bf16[3,32,512]{2,1,0:T(8,128)(2,1)S(1)} %fusion.7), channel_id=1, source_target_pairs={{0,1},{1,0},{2,3},{3,2},{4,6},{5,7},{6,4},{7,5},{8,9},{9,8},{10,11... | collective-permute-start | bytes 294920 | tf_op jit(solution)/shard_map/grad_down0_group_0/ppermute | solution.py:50
  52.1 1.1 %collective-permute-start.30 = (bf16[3,32,512]{2,1,0:T(8,128)(2,1)S(1)}, bf16[3,32,512]{2,1,0:T(8,128)(2,1)S(1)}, u32[]{:S(2)}, u32[]{:S(2)}) collective-permute-start(bf16[3,32,512]{2,1,0:T(8,128)(2,1)S(1)} %fusion.8), channel_id=1, source_target_pairs={{0,1},{1,0},{2,3},{3,2},{4,6},{5,7},{6,4},{7,5},{8,9},{9,8},{10,11... | collective-permute-start | bytes 294920 | tf_op jit(solution)/shard_map/grad_down1_group_0/ppermute | solution.py:50
  53.2 1.6 %collective-permute-start.31 = (bf16[2,128,512]{2,1,0:T(8,128)(2,1)S(1)}, bf16[2,128,512]{2,1,0:T(8,128)(2,1)S(1)}, u32[]{:S(2)}, u32[]{:S(2)}) collective-permute-start(bf16[2,128,512]{2,1,0:T(8,128)(2,1)S(1)} %get-tuple-element.96), channel_id=1, source_target_pairs={{0,4},{4,8},{8,12},{12,16},{16,20},{20,24},{24,28},{1,5},{5,9},{9,... | collective-permute-start | bytes 786440 | tf_op jit(solution)/shard_map/halo_tm1_2/ppermute | solution.py:57
  54.8 2.4 %collective-permute-start.32 = (bf16[3,64,512]{2,1,0:T(8,128)(2,1)S(1)}, bf16[3,64,512]{2,1,0:T(8,128)(2,1)S(1)}, u32[]{:S(2)}, u32[]{:S(2)}) collective-permute-start(bf16[3,64,512]{2,1,0:T(8,128)(2,1)S(1)} %add_convert_fusion), channel_id=1, source_target_pairs={{0,2},{1,3},{2,0},{3,1},{4,5},{5,4},{6,7},{7,6},{8,10},{9,11},{10,... | collective-permute-start | bytes 589832 | tf_op jit(solution)/shard_map/grad_time_group_1/ppermute | solution.py:50
  57.5 2.9 %collective-permute-start.34 = (bf16[3,32,512]{2,1,0:T(8,128)(2,1)S(1)}, bf16[3,32,512]{2,1,0:T(8,128)(2,1)S(1)}, u32[]{:S(2)}, u32[]{:S(2)}) collective-permute-start(bf16[3,32,512]{2,1,0:T(8,128)(2,1)S(1)} %add_convert_fusion.1), channel_id=1, source_target_pairs={{0,2},{1,3},{2,0},{3,1},{4,5},{5,4},{6,7},{7,6},{8,10},{9,11},{10,... | collective-permute-start | bytes 294920 | tf_op jit(solution)/shard_map/grad_down1_group_1/ppermute | solution.py:50
  60.6 2.4 %reduced.1 = bf16[4,128,512]{2,1,0:T(8,128)(2,1)} custom-call(s32[23]{0:T(128)S(1)} %pad_add_fusion.meta, bf16[2,128,512]{2,1,0:T(8,128)(2,1)S(1)} %collective-permute-done.31.before, bf16[8,128,512]{2,1,0:T(8,128)(2,1)S(1)} %get-tuple-element.74.hidden, bf16[3,64,512]{2,1,0:T(8,128)(2,1)S(1)} %copy-done.3, ...), custom_call_target="tpu_custom_call" | custom-call | flops 1000000 | bytes 1000 | tf_op jit(solution)/shard_map/reduced/pallas_call | solution.py:280
  63.0 0.8 %convert_add_fusion = f32[3,64,512]{2,1,0:T(8,128)} fusion(bf16[3,64,512]{2,1,0:T(8,128)(2,1)S(1)} %collective-permute-done.32, bf16[3,64,512]{2,1,0:T(8,128)(2,1)S(1)} %add_convert_fusion), kind=kLoop, calls=%fused_computation.16 | loop fusion | flops 294912 | bytes 786432 | tf_op jit(solution)/shard_map/add | solution.py:409
  63.8 1.1 %collective-permute-done.34 = bf16[3,32,512]{2,1,0:T(8,128)(2,1)S(1)} collective-permute-done((bf16[3,32,512]{2,1,0:T(8,128)(2,1)S(1)}, bf16[3,32,512]{2,1,0:T(8,128)(2,1)S(1)}, u32[]{:S(2)}, u32[]{:S(2)}) %collective-permute-start.34) | collective-permute-done | bytes 98336 | tf_op jit(solution)/shard_map/grad_down1_group_1/ppermute | solution.py:50
  64.9 1.9 %collective-permute-done.33 = bf16[3,32,512]{2,1,0:T(8,128)(2,1)S(1)} collective-permute-done((bf16[3,32,512]{2,1,0:T(8,128)(2,1)S(1)}, bf16[3,32,512]{2,1,0:T(8,128)(2,1)S(1)}, u32[]{:S(2)}, u32[]{:S(2)}) %collective-permute-start.33) | collective-permute-done | bytes 98336 | tf_op jit(solution)/shard_map/grad_down0_group_1/ppermute | solution.py:50
  66.9 0.8 %pad_maximum_fusion.1 = f32[3,64,512]{2,1,0:T(8,128)} fusion(f32[3,32,512]{2,1,0:T(8,128)S(1)} %convert_add_fusion.1, f32[3,32,512]{2,1,0:T(8,128)S(1)} %convert_add_fusion.2), kind=kLoop, calls=%fused_computation.15 | loop fusion | flops 98304 | bytes 786432 | tf_op jit(solution)/shard_map/concatenate | solution.py:422
  (85 shorter events, 7.7 us)
Async XLA Ops:
  0.7 11.4 %collective-permute-start.8 = (bf16[3,64,512]{2,1,0:T(8,128)(2,1)}, bf16[3,64,512]{2,1,0:T(8,128)(2,1)S(1)}, u32[]{:S(2)}, u32[]{:S(2)}) collective-permute-start(bf16[3,64,512]{2,1,0:T(8,128)(2,1)} %refs_0_.6), channel_id=1, source_target_pairs={{0,4},{4,0},{8,12},{12,8},{16,20},{20,16},{24,28},{28,24},{1,5},{5... | collective-permute-start | bytes 589832 | tf_op jit(solution)/shard_map/time_tm_core/ppermute | solution.py:37
  1.2 12.7 %collective-permute-start.3 = (bf16[3,64,512]{2,1,0:T(8,128)(2,1)}, bf16[3,64,512]{2,1,0:T(8,128)(2,1)S(1)}, u32[]{:S(2)}, u32[]{:S(2)}) collective-permute-start(bf16[3,64,512]{2,1,0:T(8,128)(2,1)} %refs_0_.6), channel_id=1, source_target_pairs={{0,8},{4,20},{8,0},{12,28},{16,24},{20,4},{24,16},{28,12},{1,9},{5... | collective-permute-start | bytes 589832 | tf_op jit(solution)/shard_map/time_tm_0/ppermute | solution.py:32
  3.7 8.1 %collective-permute-start.2 = (bf16[3,64,512]{2,1,0:T(8,128)(2,1)}, bf16[3,64,512]{2,1,0:T(8,128)(2,1)S(1)}, u32[]{:S(2)}, u32[]{:S(2)}) collective-permute-start(bf16[3,64,512]{2,1,0:T(8,128)(2,1)} %refs_0_.7), channel_id=1, source_target_pairs={{0,8},{4,20},{8,0},{12,28},{16,24},{20,4},{24,16},{28,12},{1,9},{5... | collective-permute-start | bytes 589832 | tf_op jit(solution)/shard_map/down_tm_0/ppermute | solution.py:32
  3.8 7.8 %collective-permute-start.1 = (bf16[3,64,512]{2,1,0:T(8,128)(2,1)}, bf16[3,64,512]{2,1,0:T(8,128)(2,1)S(1)}, u32[]{:S(2)}, u32[]{:S(2)}) collective-permute-start(bf16[3,64,512]{2,1,0:T(8,128)(2,1)} %refs_0_.7), channel_id=1, source_target_pairs={{0,16},{4,12},{8,24},{12,4},{16,0},{20,28},{24,8},{28,20},{1,17},{... | collective-permute-start | bytes 589832 | tf_op jit(solution)/shard_map/down_own_tm_1/ppermute | solution.py:32
  7.0 7.1 %collective-permute-start = (bf16[2,128,512]{2,1,0:T(8,128)(2,1)S(1)}, bf16[2,128,512]{2,1,0:T(8,128)(2,1)S(1)}, u32[]{:S(2)}, u32[]{:S(2)}) collective-permute-start(bf16[2,128,512]{2,1,0:T(8,128)(2,1)S(1)} %get-tuple-element.103), channel_id=1, source_target_pairs={{4,0},{8,4},{12,8},{16,12},{20,16},{24,20},{28,24},{5,1},{9,5},{13... | collective-permute-start | bytes 786440 | tf_op jit(solution)/shard_map/halo_tm-1_2/ppermute | solution.py:57
  11.6 3.1 %collective-permute-start.5 = (bf16[3,64,512]{2,1,0:T(8,128)(2,1)S(1)}, bf16[3,64,512]{2,1,0:T(8,128)(2,1)S(1)}, u32[]{:S(2)}, u32[]{:S(2)}) collective-permute-start(bf16[3,64,512]{2,1,0:T(8,128)(2,1)S(1)} %copy-done.3), channel_id=1, source_target_pairs={{0,4},{4,0},{8,12},{12,8},{16,20},{20,16},{24,28},{28,24},{1,5},{5... | collective-permute-start | bytes 589832 | tf_op jit(solution)/shard_map/down_tm_core/ppermute | solution.py:37
  11.8 7.4 %collective-permute-start.6 = (bf16[3,64,512]{2,1,0:T(8,128)(2,1)S(1)}, bf16[3,64,512]{2,1,0:T(8,128)(2,1)S(1)}, u32[]{:S(2)}, u32[]{:S(2)}) collective-permute-start(bf16[3,64,512]{2,1,0:T(8,128)(2,1)S(1)} %collective-permute-done.2.refs_1_), channel_id=1, source_target_pairs={{0,4},{4,0},{8,12},{12,8},{16,20},{20,16},{24,28},{28,24},{1,5},{5... | collective-permute-start | bytes 589832 | tf_op jit(solution)/shard_map/down_tm_core/ppermute | solution.py:37
  12.1 7.1 %collective-permute-start.4 = (bf16[3,64,512]{2,1,0:T(8,128)(2,1)S(1)}, bf16[3,64,512]{2,1,0:T(8,128)(2,1)S(1)}, u32[]{:S(2)}, u32[]{:S(2)}) collective-permute-start(bf16[3,64,512]{2,1,0:T(8,128)(2,1)S(1)} %collective-permute-done.2.refs_1_), channel_id=1, source_target_pairs={{0,16},{4,12},{8,24},{12,4},{16,0},{20,28},{24,8},{28,20},{1,17},{... | collective-permute-start | bytes 589832 | tf_op jit(solution)/shard_map/down_tm_1/ppermute | solution.py:32
  13.9 5.3 %collective-permute-start.7 = (bf16[3,64,512]{2,1,0:T(8,128)(2,1)S(1)}, bf16[3,64,512]{2,1,0:T(8,128)(2,1)S(1)}, u32[]{:S(2)}, u32[]{:S(2)}) collective-permute-start(bf16[3,64,512]{2,1,0:T(8,128)(2,1)S(1)} %collective-permute-done.1.refs_2_), channel_id=1, source_target_pairs={{0,4},{4,0},{8,12},{12,8},{16,20},{20,16},{24,28},{28,24},{1,5},{5... | collective-permute-start | bytes 589832 | tf_op jit(solution)/shard_map/down_tm_core/ppermute | solution.py:37
  14.1 2.5 %collective-permute-start.9 = (bf16[3,64,512]{2,1,0:T(8,128)(2,1)S(1)}, bf16[3,64,512]{2,1,0:T(8,128)(2,1)S(1)}, u32[]{:S(2)}, u32[]{:S(2)}) collective-permute-start(bf16[3,64,512]{2,1,0:T(8,128)(2,1)S(1)} %collective-permute-done.3.refs_1_), channel_id=1, source_target_pairs={{0,4},{4,0},{8,12},{12,8},{16,20},{20,16},{24,28},{28,24},{1,5},{5... | collective-permute-start | bytes 589832 | tf_op jit(solution)/shard_map/time_tm_core/ppermute | solution.py:37
  14.7 11.4 %collective-permute-start.16 = (bf16[2,3,64,512]{3,2,1,0:T(8,128)(2,1)S(1)}, bf16[2,3,64,512]{3,2,1,0:T(8,128)(2,1)S(1)}, u32[]{:S(2)}, u32[]{:S(2)}) collective-permute-start(bf16[2,3,64,512]{3,2,1,0:T(8,128)(2,1)S(1)} %bitcast_dynamic-update-slice_fusion), channel_id=1, source_target_pairs={{0,16},{4,12},{8,24},{12,4},{16,0},{20,28},{24,8},{28,20},{1,17},{... | collective-permute-start | bytes 1179656 | tf_op jit(solution)/shard_map/time_tm_1/ppermute | solution.py:32
  16.6 9.7 %collective-permute-start.12 = (bf16[2,128,512]{2,1,0:T(8,128)(2,1)S(1)}, bf16[2,128,512]{2,1,0:T(8,128)(2,1)S(1)}, u32[]{:S(2)}, u32[]{:S(2)}) collective-permute-start(bf16[2,128,512]{2,1,0:T(8,128)(2,1)S(1)} %get-tuple-element.60), channel_id=1, source_target_pairs={{0,4},{4,8},{8,12},{12,16},{16,20},{20,24},{24,28},{1,5},{5,9},{9,... | collective-permute-start | bytes 786440 | tf_op jit(solution)/shard_map/halo_tm1_2/ppermute | solution.py:57
  19.2 2.5 %collective-permute-start.10 = (bf16[3,64,512]{2,1,0:T(8,128)(2,1)S(1)}, bf16[3,64,512]{2,1,0:T(8,128)(2,1)S(1)}, u32[]{:S(2)}, u32[]{:S(2)}) collective-permute-start(bf16[3,64,512]{2,1,0:T(8,128)(2,1)S(1)} %collective-permute-done.4.refs_3_), channel_id=1, source_target_pairs={{0,4},{4,0},{8,12},{12,8},{16,20},{20,16},{24,28},{28,24},{1,5},{5... | collective-permute-start | bytes 589832 | tf_op jit(solution)/shard_map/down_tm_core/ppermute | solution.py:37
  25.8 1.6 %collective-permute-start.14 = (bf16[3,64,512]{2,1,0:T(8,128)(2,1)S(1)}, bf16[3,64,512]{2,1,0:T(8,128)(2,1)S(1)}, u32[]{:S(2)}, u32[]{:S(2)}) collective-permute-start(bf16[3,64,512]{2,1,0:T(8,128)(2,1)S(1)} %get-tuple-element.64), channel_id=1, source_target_pairs={{0,4},{4,0},{8,12},{12,8},{16,20},{20,16},{24,28},{28,24},{1,5},{5... | collective-permute-start | bytes 589832 | tf_op jit(solution)/shard_map/grad_time_tm_core/ppermute | solution.py:37
  26.3 2.3 %collective-permute-start.17 = (bf16[2,3,64,512]{3,2,1,0:T(8,128)(2,1)S(1)}, bf16[2,3,64,512]{3,2,1,0:T(8,128)(2,1)S(1)}, u32[]{:S(2)}, u32[]{:S(2)}) collective-permute-start(bf16[2,3,64,512]{3,2,1,0:T(8,128)(2,1)S(1)} %collective-permute-done.16.refs_2_), channel_id=1, source_target_pairs={{0,4},{4,0},{8,12},{12,8},{16,20},{20,16},{24,28},{28,24},{1,5},{5... | collective-permute-start | bytes 1179656 | tf_op jit(solution)/shard_map/time_tm_core/ppermute | solution.py:37
  28.0 7.8 %collective-permute-start.19 = (bf16[2,3,64,512]{3,2,1,0:T(8,128)(2,1)S(1)}, bf16[2,3,64,512]{3,2,1,0:T(8,128)(2,1)S(1)}, u32[]{:S(2)}, u32[]{:S(2)}) collective-permute-start(bf16[2,3,64,512]{3,2,1,0:T(8,128)(2,1)S(1)} %fusion.2), channel_id=1, source_target_pairs={{0,8},{4,20},{8,0},{12,28},{16,24},{20,4},{24,16},{28,12},{1,9},{5... | collective-permute-start | bytes 1179656 | tf_op jit(solution)/shard_map/grad_time_tm_0/ppermute | solution.py:32
  32.2 5.0 %collective-permute-start.18 = (bf16[3,64,512]{2,1,0:T(8,128)(2,1)S(1)}, bf16[3,64,512]{2,1,0:T(8,128)(2,1)S(1)}, u32[]{:S(2)}, u32[]{:S(2)}) collective-permute-start(bf16[3,64,512]{2,1,0:T(8,128)(2,1)S(1)} %get-tuple-element.72), channel_id=1, source_target_pairs={{0,4},{4,0},{8,12},{12,8},{16,20},{20,16},{24,28},{28,24},{1,5},{5... | collective-permute-start | bytes 589832 | tf_op jit(solution)/shard_map/grad_down_tm_core/ppermute | solution.py:37
  32.8 4.4 %collective-permute-start.20 = (bf16[3,64,512]{2,1,0:T(8,128)(2,1)S(1)}, bf16[3,64,512]{2,1,0:T(8,128)(2,1)S(1)}, u32[]{:S(2)}, u32[]{:S(2)}) collective-permute-start(bf16[3,64,512]{2,1,0:T(8,128)(2,1)S(1)} %get-tuple-element.77), channel_id=1, source_target_pairs={{0,4},{4,0},{8,12},{12,8},{16,20},{20,16},{24,28},{28,24},{1,5},{5... | collective-permute-start | bytes 589832 | tf_op jit(solution)/shard_map/grad_down_tm_core/ppermute | solution.py:37
  32.9 4.3 %collective-permute-start.21 = (bf16[3,64,512]{2,1,0:T(8,128)(2,1)S(1)}, bf16[3,64,512]{2,1,0:T(8,128)(2,1)S(1)}, u32[]{:S(2)}, u32[]{:S(2)}) collective-permute-start(bf16[3,64,512]{2,1,0:T(8,128)(2,1)S(1)} %get-tuple-element.79), channel_id=1, source_target_pairs={{0,4},{4,0},{8,12},{12,8},{16,20},{20,16},{24,28},{28,24},{1,5},{5... | collective-permute-start | bytes 589832 | tf_op jit(solution)/shard_map/grad_down_tm_core/ppermute | solution.py:37
  33.3 3.9 %collective-permute-start.22 = (bf16[3,64,512]{2,1,0:T(8,128)(2,1)S(1)}, bf16[3,64,512]{2,1,0:T(8,128)(2,1)S(1)}, u32[]{:S(2)}, u32[]{:S(2)}) collective-permute-start(bf16[3,64,512]{2,1,0:T(8,128)(2,1)S(1)} %get-tuple-element.81), channel_id=1, source_target_pairs={{0,4},{4,0},{8,12},{12,8},{16,20},{20,16},{24,28},{28,24},{1,5},{5... | collective-permute-start | bytes 589832 | tf_op jit(solution)/shard_map/grad_down_tm_core/ppermute | solution.py:37
  36.1 8.2 %collective-permute-start.24 = (bf16[1,3,64,512]{3,2,1,0:T(8,128)(2,1)S(1)}, bf16[1,3,64,512]{3,2,1,0:T(8,128)(2,1)S(1)}, u32[]{:S(2)}, u32[]{:S(2)}) collective-permute-start(bf16[1,3,64,512]{3,2,1,0:T(8,128)(2,1)S(1)} %slice.148), channel_id=1, source_target_pairs={{0,16},{4,12},{8,24},{12,4},{16,0},{20,28},{24,8},{28,20},{1,17},{... | collective-permute-start | bytes 589832 | tf_op jit(solution)/shard_map/grad_time_tm_1/ppermute | solution.py:32
  37.8 9.3 %collective-permute-start.26 = (bf16[2,3,32,512]{3,2,1,0:T(8,128)(2,1)S(1)}, bf16[2,3,32,512]{3,2,1,0:T(8,128)(2,1)S(1)}, u32[]{:S(2)}, u32[]{:S(2)}) collective-permute-start(bf16[2,3,32,512]{3,2,1,0:T(8,128)(2,1)S(1)} %get-tuple-element.104), channel_id=1, source_target_pairs={{0,8},{4,20},{8,0},{12,28},{16,24},{20,4},{24,16},{28,12},{1,9},{5... | collective-permute-start | bytes 589832 | tf_op jit(solution)/shard_map/grad_down1_tm_0/ppermute | solution.py:32
  38.0 7.9 %collective-permute-start.23 = (bf16[2,3,32,512]{3,2,1,0:T(8,128)(2,1)S(1)}, bf16[2,3,32,512]{3,2,1,0:T(8,128)(2,1)S(1)}, u32[]{:S(2)}, u32[]{:S(2)}) collective-permute-start(bf16[2,3,32,512]{3,2,1,0:T(8,128)(2,1)S(1)} %get-tuple-element.105), channel_id=1, source_target_pairs={{0,8},{4,20},{8,0},{12,28},{16,24},{20,4},{24,16},{28,12},{1,9},{5... | collective-permute-start | bytes 589832 | tf_op jit(solution)/shard_map/grad_down0_tm_0/ppermute | solution.py:32
  44.3 10.5 %collective-permute-start.28 = (bf16[3,64,512]{2,1,0:T(8,128)(2,1)S(1)}, bf16[3,64,512]{2,1,0:T(8,128)(2,1)S(1)}, u32[]{:S(2)}, u32[]{:S(2)}) collective-permute-start(bf16[3,64,512]{2,1,0:T(8,128)(2,1)S(1)} %fusion.4), channel_id=1, source_target_pairs={{0,1},{1,0},{2,3},{3,2},{4,6},{5,7},{6,4},{7,5},{8,9},{9,8},{10,11... | collective-permute-start | bytes 589832 | tf_op jit(solution)/shard_map/grad_time_group_0/ppermute | solution.py:50
  46.0 4.7 %collective-permute-start.25 = (bf16[1,3,32,512]{3,2,1,0:T(8,128)(2,1)S(1)}, bf16[1,3,32,512]{3,2,1,0:T(8,128)(2,1)S(1)}, u32[]{:S(2)}, u32[]{:S(2)}) collective-permute-start(bf16[1,3,32,512]{3,2,1,0:T(8,128)(2,1)S(1)} %slice.150), channel_id=1, source_target_pairs={{0,16},{4,12},{8,24},{12,4},{16,0},{20,28},{24,8},{28,20},{1,17},{... | collective-permute-start | bytes 294920 | tf_op jit(solution)/shard_map/grad_down0_tm_1/ppermute | solution.py:32
  47.1 4.9 %collective-permute-start.29 = (bf16[1,3,32,512]{3,2,1,0:T(8,128)(2,1)S(1)}, bf16[1,3,32,512]{3,2,1,0:T(8,128)(2,1)S(1)}, u32[]{:S(2)}, u32[]{:S(2)}) collective-permute-start(bf16[1,3,32,512]{3,2,1,0:T(8,128)(2,1)S(1)} %slice.149), channel_id=1, source_target_pairs={{0,16},{4,12},{8,24},{12,4},{16,0},{20,28},{24,8},{28,20},{1,17},{... | collective-permute-start | bytes 294920 | tf_op jit(solution)/shard_map/grad_down1_tm_1/ppermute | solution.py:32
  50.7 6.5 %collective-permute-start.27 = (bf16[3,32,512]{2,1,0:T(8,128)(2,1)S(1)}, bf16[3,32,512]{2,1,0:T(8,128)(2,1)S(1)}, u32[]{:S(2)}, u32[]{:S(2)}) collective-permute-start(bf16[3,32,512]{2,1,0:T(8,128)(2,1)S(1)} %fusion.7), channel_id=1, source_target_pairs={{0,1},{1,0},{2,3},{3,2},{4,6},{5,7},{6,4},{7,5},{8,9},{9,8},{10,11... | collective-permute-start | bytes 294920 | tf_op jit(solution)/shard_map/grad_down0_group_0/ppermute | solution.py:50
  52.1 5.4 %collective-permute-start.30 = (bf16[3,32,512]{2,1,0:T(8,128)(2,1)S(1)}, bf16[3,32,512]{2,1,0:T(8,128)(2,1)S(1)}, u32[]{:S(2)}, u32[]{:S(2)}) collective-permute-start(bf16[3,32,512]{2,1,0:T(8,128)(2,1)S(1)} %fusion.8), channel_id=1, source_target_pairs={{0,1},{1,0},{2,3},{3,2},{4,6},{5,7},{6,4},{7,5},{8,9},{9,8},{10,11... | collective-permute-start | bytes 294920 | tf_op jit(solution)/shard_map/grad_down1_group_0/ppermute | solution.py:50
  53.2 7.4 %collective-permute-start.31 = (bf16[2,128,512]{2,1,0:T(8,128)(2,1)S(1)}, bf16[2,128,512]{2,1,0:T(8,128)(2,1)S(1)}, u32[]{:S(2)}, u32[]{:S(2)}) collective-permute-start(bf16[2,128,512]{2,1,0:T(8,128)(2,1)S(1)} %get-tuple-element.96), channel_id=1, source_target_pairs={{0,4},{4,8},{8,12},{12,16},{16,20},{20,24},{24,28},{1,5},{5,9},{9,... | collective-permute-start | bytes 786440 | tf_op jit(solution)/shard_map/halo_tm1_2/ppermute | solution.py:57
  54.8 8.2 %collective-permute-start.32 = (bf16[3,64,512]{2,1,0:T(8,128)(2,1)S(1)}, bf16[3,64,512]{2,1,0:T(8,128)(2,1)S(1)}, u32[]{:S(2)}, u32[]{:S(2)}) collective-permute-start(bf16[3,64,512]{2,1,0:T(8,128)(2,1)S(1)} %add_convert_fusion), channel_id=1, source_target_pairs={{0,2},{1,3},{2,0},{3,1},{4,5},{5,4},{6,7},{7,6},{8,10},{9,11},{10,... | collective-permute-start | bytes 589832 | tf_op jit(solution)/shard_map/grad_time_group_1/ppermute | solution.py:50
  57.5 7.3 %collective-permute-start.34 = (bf16[3,32,512]{2,1,0:T(8,128)(2,1)S(1)}, bf16[3,32,512]{2,1,0:T(8,128)(2,1)S(1)}, u32[]{:S(2)}, u32[]{:S(2)}) collective-permute-start(bf16[3,32,512]{2,1,0:T(8,128)(2,1)S(1)} %add_convert_fusion.1), channel_id=1, source_target_pairs={{0,2},{1,3},{2,0},{3,1},{4,5},{5,4},{6,7},{7,6},{8,10},{9,11},{10,... | collective-permute-start | bytes 294920 | tf_op jit(solution)/shard_map/grad_down1_group_1/ppermute | solution.py:50
  60.5 6.4 %collective-permute-start.33 = (bf16[3,32,512]{2,1,0:T(8,128)(2,1)S(1)}, bf16[3,32,512]{2,1,0:T(8,128)(2,1)S(1)}, u32[]{:S(2)}, u32[]{:S(2)}) collective-permute-start(bf16[3,32,512]{2,1,0:T(8,128)(2,1)S(1)} %add_convert_fusion.2), channel_id=1, source_target_pairs={{0,2},{1,3},{2,0},{3,1},{4,5},{5,4},{6,7},{7,6},{8,10},{9,11},{10,... | collective-permute-start | bytes 294920 | tf_op jit(solution)/shard_map/grad_down0_group_1/ppermute | solution.py:50
  (8 other events, 39.9 us)
